TPU v7x, 512 devices: a whole 4x4x16 slice. The times are simulated.
512 devices in a mesh: row: 64 (over z, x_lo, core), col: 8 (over x_hi, y).
Axes of the slice: x: 4 (x_hi: 2, x_lo: 2; x = x_hi * 2 + x_lo), y: 4, z: 16, core: 2. Of those that a mesh axis runs over, the one named last changes fastest.
Arguments:
- tokens: bfloat16 [1024, 4096], P('row', 'col'), may hold values from -6 to 6
- probe_draw: int32 [1024, 4096], P(None, 'col'), may hold values from 0 to 1
- w_in: bfloat16 [4096, 16384], P('col', 'row'), may hold values from -0.09375 to 0.09375
- w_out: bfloat16 [16384, 4096], P('row', 'col'), may hold values from -0.09375 to 0.09375
Outputs:
- grad_in: float32 [4096, 16384], P('col', 'row')
- grad_out: float32 [16384, 4096], P('row', 'col')
All inputs are finite; a program needn't handle non-finite values.
Results may differ from a plain program's by a relative error of at most 0.013.
Values may be sent and summed in bfloat16 or wider, within the bound.
No kernel may reach another device: no remote copies, remote signals or barrier semaphores. Data moves between devices by JAX's collectives and lax.ppermute only.
A program may use at most 64 MiB of HBM per device.

v0:
```python
import jax
import jax.numpy as jnp
from jax import lax
from jax.sharding import PartitionSpec as P


def local_terms(hidden, signal):
    cdf_part = 0.5 * (1.0 + lax.erf(hidden * 0.7071067811865476))
    pdf_part = jnp.exp(-0.5 * hidden * hidden) * 0.3989422804014327
    slope_full = cdf_part + hidden * pdf_part
    slopes = slope_full.astype(jnp.bfloat16)
    bending = (signal * pdf_part * (2.0 - hidden * hidden)).astype(jnp.bfloat16)
    gated = (signal * slope_full).astype(jnp.bfloat16)
    return (slopes, bending, gated)


def contract_rows(left, right):
    return lax.dot_general(
        left, right, (((0,), (0,)), ((), ())), preferred_element_type=jnp.float32
    )


def contract_cols(left, right):
    return lax.dot_general(
        left, right, (((1,), (1,)), ((), ())), preferred_element_type=jnp.float32
    )


def on_device(tokens, probe_draw, w_in, w_out):
    sign_values = (2 * probe_draw - 1).astype(jnp.bfloat16)
    total_rows = probe_draw.shape[0]
    token_full = lax.all_gather(tokens, "row", axis=0, tiled=True)
    hidden_part = jnp.dot(token_full, w_in, preferred_element_type=jnp.float32)
    signal_part = contract_cols(sign_values, w_out)
    hidden, signal = lax.psum((hidden_part, signal_part), "col")
    slopes, bending, gated = local_terms(hidden, signal)
    jac_own = lax.psum_scatter(
        contract_cols(gated, w_in), "row", scatter_dimension=0, tiled=True
    ).astype(jnp.bfloat16)
    jac_rows = lax.all_gather(jac_own, "row", axis=0, tiled=True)
    back_part = jnp.dot(jac_rows, w_in, preferred_element_type=jnp.float32)
    back_proj = lax.psum(back_part, "col")
    curv_term = (back_proj * bending).astype(jnp.bfloat16)
    slope_term = (back_proj * slopes).astype(jnp.bfloat16)
    factor = 1.0 / jnp.sqrt(jnp.float32(total_rows))
    grad_in = factor * (contract_rows(token_full, curv_term) + contract_rows(jac_rows, gated))
    grad_out = factor * contract_rows(slope_term, sign_values)
    return (grad_in, grad_out)


def solution(mesh):
    return jax.shard_map(
        on_device,
        mesh=mesh,
        in_specs=(P("row", "col"), P(None, "col"), P("col", "row"), P("row", "col")),
        out_specs=(P("col", "row"), P("row", "col")),
        check_vma=False,
    )
```

profile of v0, /device:TPU:1, one launch (start us, length us, event | category | flops | bytes accessed | tf_op | source)
XLA Modules:
  0.0 709.3 jit_solution(12134224397101569801)
XLA Ops:
  7.2 0.0 copy-start
  7.2 0.0 all-gather.3.cloned.1.call-start
  7.2 0.7 all-gather.3.cloned.1.call-update
  7.9 0.0 all-reduce.6.cloned.1.call-start
  8.0 3.0 fusion.13
  11.0 125.4 %all-gather.3.cloned.1.call-done = bf16[1024,512]{1,0:T(8,128)(2,1)} async-done(((bf16[16,512]{1,0:T(8,128)(2,1)}), bf16[1024,512]{1,0:T(8,128)(2,1)}) %all-gather.3.cloned.1.call-update) | async-done | bytes 1048592 | tf_op jit(solution)/shard_map/all_gather | solution.py:32
  136.4 0.0 copy-done
  136.4 2.6 fusion.22
  139.1 0.0 all-reduce.6.cloned.1.call-update
  139.1 0.0 reduce-scatter.2.cloned.1.call-start
  139.2 99.9 %all-reduce.6.cloned.1.call-done = (f32[1024,256]{1,0:T(8,128)}, f32[1024,256]{1,0:T(8,128)}) async-done(((f32[1024,256]{1,0:T(8,128)}, f32[1024,256]{1,0:T(8,128)}), (f32[1024,256]{1,0:T(8,128)}, f32[1024,256]{1,0:T(8,128)})) %all-reduce.6.cloned.1.call-update) | async-done | bytes 2097168 | tf_op jit(solution)/shard_map/psum | solution.py:35
  239.0 2.0 multiply_convert_fusion.2
  241.0 0.0 copy-start.3
  241.0 0.8 copy-done.3
  241.8 1.8 fusion.23
  243.6 0.0 reduce-scatter.2.cloned.1.call-update
  243.6 0.0 copy-start.1
  243.6 0.0 copy-start.6
  243.6 0.0 copy-start.7
  243.6 0.0 all-gather.5.cloned.1.call-start
  243.7 228.2 %reduce-scatter.2.cloned.1.call-done = f32[16,512]{1,0:T(8,128)} async-done(((f32[1024,512]{1,0:T(8,128)}), f32[16,512]{1,0:T(8,128)}) %reduce-scatter.2.cloned.1.call-update) | async-done | bytes 32784 | tf_op jit(solution)/shard_map/reduce_scatter | solution.py:37
  471.9 1.4 convert_element_type.29
  473.3 0.0 all-gather.5.cloned.1.call-update
  473.3 0.0 all-reduce.4.cloned.1.call-start
  473.4 123.5 %all-gather.5.cloned.1.call-done = bf16[1024,512]{1,0:T(8,128)(2,1)} async-done(((bf16[16,512]{1,0:T(8,128)(2,1)}), bf16[1024,512]{1,0:T(8,128)(2,1)}) %all-gather.5.cloned.1.call-update) | async-done | bytes 1048592 | tf_op jit(solution)/shard_map/all_gather | solution.py:40
  596.9 2.7 fusion.24
  599.6 0.0 all-reduce.4.cloned.1.call-update
  599.6 94.9 %all-reduce.4.cloned.1.call-done = f32[1024,256]{1,0:T(8,128)} async-done(((f32[1024,256]{1,0:T(8,128)}), f32[1024,256]{1,0:T(8,128)}) %all-reduce.4.cloned.1.call-update) | async-done | bytes 1048592 | tf_op jit(solution)/shard_map/psum | solution.py:42
  694.5 0.0 copy-done.1
  694.5 0.0 copy-done.6
  694.5 0.0 copy-done.7
  694.5 0.0 copy-start.4
  694.5 0.0 copy-start.5
  694.5 2.0 convolution_bitcast_fusion
  696.5 0.0 copy-done.4
  696.5 0.0 copy-done.5
  696.5 0.0 copy-start.2
  696.5 1.3 fusion
  697.8 2.0 copy.7
  699.9 0.0 copy-done.2
  699.9 3.0 convolution_multiply_fusion
Async XLA Ops:
  7.2 129.3 %copy-start = (bf16[512,256]{1,0:T(8,128)(2,1)S(1)}, bf16[512,256]{1,0:T(8,128)(2,1)}, u32[]{:S(2)}) copy-start(bf16[512,256]{1,0:T(8,128)(2,1)} %param.6) | copy-start | bytes 786436
  7.2 129.3 %all-gather.3.cloned.1.call-start = ((), (), s32[]{:S(2)}) async-start(), calls=%async_computation.1 | async-start | bytes 1064960 | tf_op jit(solution)/shard_map/all_gather | solution.py:32
  7.9 231.1 %all-reduce.6.cloned.1.call-start = ((), (), s32[]{:S(2)}) async-start(), calls=%async_computation.5 | async-start | bytes 4194304 | tf_op jit(solution)/shard_map/psum | solution.py:35
  139.1 332.8 %reduce-scatter.2.cloned.1.call-start = ((), (), s32[]{:S(2)}) async-start(), calls=%async_computation.2 | async-start | bytes 2129920 | tf_op jit(solution)/shard_map/reduce_scatter | solution.py:37
  241.0 0.8 copy-start.3
  243.6 450.9 %copy-start.1 = (f32[1024,256]{1,0:T(8,128)S(1)}, f32[1024,256]{1,0:T(8,128)}, u32[]{:S(2)}) copy-start(f32[1024,256]{1,0:T(8,128)} %get-tuple-element.5) | copy-start | bytes 3145732
  243.6 450.9 %copy-start.6 = (bf16[1024,512]{1,0:T(8,128)(2,1)S(1)}, bf16[1024,512]{1,0:T(8,128)(2,1)}, u32[]{:S(2)}) copy-start(bf16[1024,512]{1,0:T(8,128)(2,1)} %all-gather.3.cloned.1.call-done) | copy-start | bytes 3145732
  243.6 450.9 %copy-start.7 = (f32[1024,256]{1,0:T(8,128)S(1)}, f32[1024,256]{1,0:T(8,128)}, u32[]{:S(2)}) copy-start(f32[1024,256]{1,0:T(8,128)} %get-tuple-element.4) | copy-start | bytes 3145732
  243.6 353.3 %all-gather.5.cloned.1.call-start = ((), (), s32[]{:S(2)}) async-start(), calls=%async_computation.3 | async-start | bytes 1064960 | tf_op jit(solution)/shard_map/all_gather | solution.py:40
  473.3 221.2 %all-reduce.4.cloned.1.call-start = ((), (), s32[]{:S(2)}) async-start(), calls=%async_computation.4 | async-start | bytes 2097152 | tf_op jit(solution)/shard_map/psum | solution.py:42
  694.5 2.0 copy-start.4
  694.5 2.0 copy-start.5
  696.5 3.3 copy-start.2
Sparse Core Ops, SparseCore 0:
  10.2 126.2 all-gather.2
  139.4 99.5 all-reduce.5
  243.7 228.1 reduce-scatter.1
  474.7 122.1 all-gather.4
  599.9 94.4 all-reduce.3
where the time goes:
time: 713 us; the launch traced here: 709 us
  waiting for transfers between devices  673 us (94%)
  matrix products  16.4 us (2%)
  between operations  13.9 us (2%)
    reduce_scatter x1, waiting for transfers between devices, on_device(): lax.psum_scatter(contract_cols(gated, w_in), 'row', scatter_dimension=0,...  228 us
    all_gather x1, waiting for transfers between devices, on_device(): token_full = lax.all_gather(tokens, 'row', axis=0, tiled=True)  125 us
    all_gather x1, waiting for transfers between devices, on_device(): jac_rows = lax.all_gather(jac_own, 'row', axis=0, tiled=True)  124 us
    psum x1, waiting for transfers between devices, on_device(): hidden, signal = lax.psum((hidden_part, signal_part), 'col')  99.9 us
    psum x1, waiting for transfers between devices, on_device(): back_proj = lax.psum(back_part, 'col')  94.9 us
  transfers between devices with their start and end apart: 5, of which 5 were waited for; matrix products, arithmetic and copies ran while one was open for 0% of the time, Pallas kernels for 0%

commit v1 on v0

v1 whole, which is shorter than its diff:
```python
import jax
import jax.numpy as jnp
from jax import lax
from jax.sharding import Mesh, PartitionSpec as P

Z, NEAR, COL = ("z",), ("xl", "core"), ("xh", "y")
BF, F32 = jnp.bfloat16, jnp.float32


def local_terms(hidden, signal):
    cdf_part = 0.5 * (1.0 + lax.erf(hidden * 0.7071067811865476))
    pdf_part = jnp.exp(-0.5 * hidden * hidden) * 0.3989422804014327
    slope_full = cdf_part + hidden * pdf_part
    slopes = slope_full.astype(BF)
    bending = (signal * pdf_part * (2.0 - hidden * hidden)).astype(BF)
    gated = (signal * slope_full).astype(BF)
    return (slopes, bending, gated)


def contract_rows(left, right):
    return lax.dot_general(
        left, right, (((0,), (0,)), ((), ())), preferred_element_type=F32
    )


def contract_cols(left, right):
    return lax.dot_general(
        left, right, (((1,), (1,)), ((), ())), preferred_element_type=F32
    )


def exchange(blocks, axes):
    return lax.all_to_all(blocks, axes, 0, 0, tiled=True)


def gather(block, axes, count):
    rows, cols = block.shape
    return exchange(
        jnp.broadcast_to(block[None], (count, rows, cols)), axes
    ).reshape(count * rows, cols)


def scatter_sum(array, axes, count):
    rows, cols = array.shape
    blocks = array.astype(BF).reshape(count, rows // count, cols)
    return exchange(blocks, axes).astype(F32).sum(axis=0)


def on_device(tokens, probe_draw, w_in, w_out):
    total_rows = probe_draw.shape[0]
    own_rows, feats = tokens.shape
    nz, nn, nc = (lax.axis_size(a) for a in (Z, NEAR, COL))
    hid = w_in.shape[1]
    sign_values = (2 * probe_draw - 1).astype(BF)
    sign_values = (
        sign_values.reshape(nz, nn, own_rows, feats)
        .transpose(1, 0, 2, 3)
        .reshape(total_rows, feats)
    )
    signal_part = contract_cols(sign_values, w_out)
    token_full = gather(gather(tokens, Z, nz), NEAR, nn)
    hidden_part = jnp.dot(token_full, w_in, preferred_element_type=F32)
    both = scatter_sum(
        jnp.concatenate([hidden_part, signal_part], axis=1), COL, nc
    )
    slopes, bending, gated_own = local_terms(both[:, :hid], both[:, hid:])
    gated = gather(gated_own, COL, nc)
    jac_part = contract_cols(gated, w_in)
    jac_own = scatter_sum(scatter_sum(jac_part, NEAR, nn), Z, nz).astype(BF)
    jac_rows = gather(gather(jac_own, Z, nz), NEAR, nn)
    back_part = jnp.dot(jac_rows, w_in, preferred_element_type=F32)
    back_proj = scatter_sum(back_part, COL, nc)
    curv_own = (back_proj * bending).astype(BF)
    slope_own = (back_proj * slopes).astype(BF)
    terms = gather(jnp.concatenate([curv_own, slope_own], axis=1), COL, nc)
    curv_term, slope_term = terms[:, :hid], terms[:, hid:]
    factor = 1.0 / jnp.sqrt(jnp.float32(total_rows))
    grad_in = factor * (
        contract_rows(token_full, curv_term) + contract_rows(jac_rows, gated)
    )
    grad_out = factor * contract_rows(slope_term, sign_values)
    return (grad_in, grad_out)


def solution(mesh):
    fine = Mesh(
        mesh.devices.reshape(16, 2, 2, 2, 4), ("z", "xl", "core", "xh", "y")
    )
    row, col = Z + NEAR, COL
    return jax.shard_map(
        on_device,
        mesh=fine,
        in_specs=(P(row, col), P(None, col), P(col, row), P(row, col)),
        out_specs=(P(col, row), P(row, col)),
        check_vma=False,
    )
```

time: 713 us -> 213 us (0.30)
  waiting for transfers between devices: 673 us -> 11.1 us
  blocking collectives: 0 us -> 177 us
  between operations: 13.9 us -> 0.77 us
  matrix products: 16.4 us -> 4 us
  starting transfers between devices: 0.2 us -> 9.66 us
    all_gather x2 -> x0, waiting for transfers between devices: 249 us -> none  [the longest x1 125 us: on_device(): token_full = lax.all_gather(tokens, 'row', axis=0, tiled=True)]
    reduce_scatter x1 -> x0, waiting for transfers between devices: 228 us -> none  [on_device(): lax.psum_scatter(contract_cols(gated, w_in), 'row', scatter_dimension=0,...]
    psum x2 -> x0, waiting for transfers between devices: 195 us -> none  [the longest x1 99.9 us: on_device(): hidden, signal = lax.psum((hidden_part, signal_part), 'col')]
    all_to_all x0 -> x9, blocking collectives: none -> 177 us  [exchange(): return lax.all_to_all(blocks, axes, 0, 0, tiled=True)]
    all_to_all x0 -> x1, waiting for transfers between devices: none -> 11.1 us  [exchange(): return lax.all_to_all(blocks, axes, 0, 0, tiled=True)]
    all_to_all x0 -> x1, starting transfers between devices: none -> 9.66 us  [exchange(): return lax.all_to_all(blocks, axes, 0, 0, tiled=True)]
  transfers between devices with their start and end apart: 5 -> 1, of which waited for: 5 -> 1; matrix products, arithmetic and copies ran while one was open for 0% -> 1% of each run, Pallas kernels for 0% -> 0%
where the time goes in v1:
time: 213 us; the launch traced here: 210 us
  blocking collectives  177 us (83%)
  waiting for transfers between devices  11.1 us (5%)
  starting transfers between devices  9.66 us (5%)
  other arithmetic  4.81 us (2%)
  matrix products  4 us (2%)
  local copies, waits for them, and re-layouts  3.14 us (1%)
    all_to_all x9, blocking collectives, exchange(): return lax.all_to_all(blocks, axes, 0, 0, tiled=True)  177 us
    all_to_all x1, waiting for transfers between devices, exchange(): return lax.all_to_all(blocks, axes, 0, 0, tiled=True)  11.1 us
    all_to_all x1, starting transfers between devices, exchange(): return lax.all_to_all(blocks, axes, 0, 0, tiled=True)  9.66 us
  transfers between devices with their start and end apart: 1, of which 1 were waited for; matrix products, arithmetic and copies ran while one was open for 1% of the time, Pallas kernels for 0%

profile of v1, /device:TPU:1, one launch (start us, length us, event | category | flops | bytes accessed | tf_op | source)
XLA Modules:
  0.0 210.2 jit_solution(12903196745070848483)
XLA Ops:
  0.6 0.0 copy-start
  0.6 0.8 broadcast_in_dim.16
  1.4 28.7 %all_to_all.50 = bf16[16,16,512]{2,1,0:T(8,128)(2,1)S(1)} all-to-all(bf16[16,16,512]{2,1,0:T(8,128)(2,1)S(1)} %broadcast_in_dim.16), channel_id=1, replica_groups=mesh['z'=16,'xl'=2,'core'=2,'xh'=2,'y'=4] {'z'}, dimensions={0} | all-to-all | bytes 524288 | tf_op jit(solution)/shard_map/all_to_all | solution.py:33
  30.1 1.1 broadcast_in_dim.18
  31.2 9.7 %all-to-all-start.1 = ((bf16[4,256,512]{2,1,0:T(8,128)(2,1)}), bf16[4,256,512]{2,1,0:T(8,128)(2,1)S(1)}, u32[]{:S(2)}, u32[]{:S(2)}) async-start(bf16[4,256,512]{2,1,0:T(8,128)(2,1)} %broadcast_in_dim.18), calls=%async_computation.1 | async-start | bytes 2097152 | tf_op jit(solution)/shard_map/all_to_all | solution.py:33
  40.8 0.0 copy-start.1
  40.8 1.9 add_convert_fusion
  42.8 0.1 copy.18
  42.8 0.0 copy-done.1
  42.9 0.5 convolution_convert_fusion.2
  43.3 11.1 %all-to-all-done.1 = bf16[4,256,512]{2,1,0:T(8,128)(2,1)S(1)} async-done(((bf16[4,256,512]{2,1,0:T(8,128)(2,1)}), bf16[4,256,512]{2,1,0:T(8,128)(2,1)S(1)}, u32[]{:S(2)}, u32[]{:S(2)}) %all-to-all-start.1) | async-done | bytes 1048608 | tf_op jit(solution)/shard_map/all_to_all | solution.py:33
  54.4 0.0 copy-done
  54.4 0.4 convolution_convert_fusion.3
  54.9 0.1 pad_maximum_fusion
  55.0 21.8 %all_to_all.51 = bf16[8,128,512]{2,1,0:T(8,128)(2,1)S(1)} all-to-all(bf16[8,128,512]{2,1,0:T(8,128)(2,1)S(1)} %pad_maximum_fusion), channel_id=1, replica_groups=mesh['z'=16,'xl'=2,'core'=2,'xh'=2,'y'=4] {'xh','y'}, dimensions={0} | all-to-all | bytes 2097152 | tf_op jit(solution)/shard_map/all_to_all | solution.py:33
  76.8 0.1 convert_reduce_fusion
  77.0 0.1 multiply_convert_fusion.2
  77.1 12.2 %all_to_all.52 = bf16[8,128,256]{2,1,0:T(8,128)(2,1)S(1)} all-to-all(bf16[8,128,256]{2,1,0:T(8,128)(2,1)S(1)} %broadcast_in_dim.19), channel_id=1, replica_groups=mesh['z'=16,'xl'=2,'core'=2,'xh'=2,'y'=4] {'xh','y'}, dimensions={0} | all-to-all | bytes 1048576 | tf_op jit(solution)/shard_map/all_to_all | solution.py:33
  89.2 0.5 convolution_convert_fusion
  89.7 19.9 %all_to_all.53 = bf16[4,256,512]{2,1,0:T(8,128)(2,1)} all-to-all(bf16[4,256,512]{2,1,0:T(8,128)(2,1)S(1)} %bitcast.42), channel_id=1, replica_groups=mesh['z'=16,'xl'=2,'core'=2,'xh'=2,'y'=4] {'xl','core'}, dimensions={0} | all-to-all | bytes 2097152 | tf_op jit(solution)/shard_map/all_to_all | solution.py:33
  109.6 1.5 reduce_sum.43
  111.1 18.4 %all_to_all.54 = bf16[16,16,512]{2,1,0:T(8,128)(2,1)} all-to-all(bf16[16,16,512]{2,1,0:T(8,128)(2,1)S(1)} %bitcast.45), channel_id=1, replica_groups=mesh['z'=16,'xl'=2,'core'=2,'xh'=2,'y'=4] {'z'}, dimensions={0} | all-to-all | bytes 524288 | tf_op jit(solution)/shard_map/all_to_all | solution.py:33
  129.5 1.0 reduce_sum.44
  130.5 24.0 %all_to_all.55 = bf16[16,16,512]{2,1,0:T(8,128)(2,1)S(1)} all-to-all(bf16[16,16,512]{2,1,0:T(8,128)(2,1)S(1)} %broadcast_in_dim.20), channel_id=1, replica_groups=mesh['z'=16,'xl'=2,'core'=2,'xh'=2,'y'=4] {'z'}, dimensions={0} | all-to-all | bytes 524288 | tf_op jit(solution)/shard_map/all_to_all | solution.py:33
  154.5 0.1 broadcast_in_dim.44
  154.6 22.2 %all_to_all.56 = bf16[4,256,512]{2,1,0:T(8,128)(2,1)S(1)} all-to-all(bf16[4,256,512]{2,1,0:T(8,128)(2,1)S(1)} %broadcast_in_dim.44), channel_id=1, replica_groups=mesh['z'=16,'xl'=2,'core'=2,'xh'=2,'y'=4] {'xl','core'}, dimensions={0} | all-to-all | bytes 2097152 | tf_op jit(solution)/shard_map/all_to_all | solution.py:33
  176.8 0.4 convolution_convert_fusion.1
  177.2 12.1 %all_to_all.57 = bf16[8,128,256]{2,1,0:T(8,128)(2,1)S(1)} all-to-all(bf16[8,128,256]{2,1,0:T(8,128)(2,1)S(1)} %bitcast.43), channel_id=1, replica_groups=mesh['z'=16,'xl'=2,'core'=2,'xh'=2,'y'=4] {'xh','y'}, dimensions={0} | all-to-all | bytes 1048576 | tf_op jit(solution)/shard_map/all_to_all | solution.py:33
  189.3 0.1 convert_reduce_fusion.1
  189.4 0.1 multiply_convert_fusion.1
  189.5 0.1 broadcast_in_dim.45
  189.6 17.4 %all_to_all.58 = bf16[8,128,512]{2,1,0:T(8,128)(2,1)S(1)} all-to-all(bf16[8,128,512]{2,1,0:T(8,128)(2,1)S(1)} %broadcast_in_dim.45), channel_id=1, replica_groups=mesh['z'=16,'xl'=2,'core'=2,'xh'=2,'y'=4] {'xh','y'}, dimensions={0} | all-to-all | bytes 2097152 | tf_op jit(solution)/shard_map/all_to_all | solution.py:33
  206.9 1.3 convolution_multiply_fusion
  208.2 0.5 convolution_bitcast_fusion
  208.7 0.5 fusion
  209.2 1.0 copy.21
  (3 shorter events, 0.1 us)
Async XLA Ops:
  0.6 53.8 %copy-start = (bf16[512,256]{1,0:T(8,128)(2,1)S(1)}, bf16[512,256]{1,0:T(8,128)(2,1)}, u32[]{:S(2)}) copy-start(bf16[512,256]{1,0:T(8,128)(2,1)} %param.6) | copy-start | bytes 786436
  31.2 23.3 %all-to-all-start.1 = ((bf16[4,256,512]{2,1,0:T(8,128)(2,1)}), bf16[4,256,512]{2,1,0:T(8,128)(2,1)S(1)}, u32[]{:S(2)}, u32[]{:S(2)}) async-start(bf16[4,256,512]{2,1,0:T(8,128)(2,1)} %broadcast_in_dim.18), calls=%async_computation.1 | async-start | bytes 2097152 | tf_op jit(solution)/shard_map/all_to_all | solution.py:33
  40.8 2.0 copy-start.1

commit v2 on v1

--- a/solution.py
+++ b/solution.py
@@ -3,7 +3,7 @@
 from jax import lax
 from jax.sharding import Mesh, PartitionSpec as P
 
-Z, NEAR, COL = ("z",), ("xl", "core"), ("xh", "y")
+LINE, COL = ("z", "xl"), ("xh", "y")
 BF, F32 = jnp.bfloat16, jnp.float32
 
 
@@ -46,47 +46,64 @@
     return exchange(blocks, axes).astype(F32).sum(axis=0)
 
 
+def other_core(array):
+    return lax.ppermute(array, "core", [(0, 1), (1, 0)])
+
+
 def on_device(tokens, probe_draw, w_in, w_out):
     total_rows = probe_draw.shape[0]
     own_rows, feats = tokens.shape
-    nz, nn, nc = (lax.axis_size(a) for a in (Z, NEAR, COL))
+    nl, nc = lax.axis_size(LINE), lax.axis_size(COL)
     hid = w_in.shape[1]
-    sign_values = (2 * probe_draw - 1).astype(BF)
-    sign_values = (
-        sign_values.reshape(nz, nn, own_rows, feats)
-        .transpose(1, 0, 2, 3)
-        .reshape(total_rows, feats)
-    )
-    signal_part = contract_cols(sign_values, w_out)
-    token_full = gather(gather(tokens, Z, nz), NEAR, nn)
-    hidden_part = jnp.dot(token_full, w_in, preferred_element_type=F32)
+    w_in_pair = jnp.concatenate([w_in, other_core(w_in)], axis=1)
+    w_out_pair = jnp.concatenate([w_out, other_core(w_out)], axis=0)
+    draw = lax.dynamic_index_in_dim(
+        probe_draw.reshape(nl, 2, own_rows, feats),
+        lax.axis_index("core"),
+        axis=1,
+        keepdims=False,
+    ).reshape(nl * own_rows, feats)
+    sign_values = (2 * draw - 1).astype(BF)
+    signal_part = contract_cols(sign_values, w_out_pair)
+    token_part = gather(tokens, LINE, nl)
+    hidden_part = jnp.dot(token_part, w_in_pair, preferred_element_type=F32)
     both = scatter_sum(
         jnp.concatenate([hidden_part, signal_part], axis=1), COL, nc
     )
-    slopes, bending, gated_own = local_terms(both[:, :hid], both[:, hid:])
+    slopes, bending, gated_own = local_terms(
+        both[:, : 2 * hid], both[:, 2 * hid :]
+    )
     gated = gather(gated_own, COL, nc)
-    jac_part = contract_cols(gated, w_in)
-    jac_own = scatter_sum(scatter_sum(jac_part, NEAR, nn), Z, nz).astype(BF)
-    jac_rows = gather(gather(jac_own, Z, nz), NEAR, nn)
-    back_part = jnp.dot(jac_rows, w_in, preferred_element_type=F32)
+    jac_own = scatter_sum(contract_cols(gated, w_in_pair), LINE, nl).astype(BF)
+    jac_rows = gather(jac_own, LINE, nl)
+    back_part = jnp.dot(jac_rows, w_in_pair, preferred_element_type=F32)
     back_proj = scatter_sum(back_part, COL, nc)
     curv_own = (back_proj * bending).astype(BF)
     slope_own = (back_proj * slopes).astype(BF)
     terms = gather(jnp.concatenate([curv_own, slope_own], axis=1), COL, nc)
-    curv_term, slope_term = terms[:, :hid], terms[:, hid:]
+    curv_term, slope_term = terms[:, : 2 * hid], terms[:, 2 * hid :]
     factor = 1.0 / jnp.sqrt(jnp.float32(total_rows))
-    grad_in = factor * (
-        contract_rows(token_full, curv_term) + contract_rows(jac_rows, gated)
+
+    def grads(part):
+        return (
+            contract_rows(token_part, curv_term[:, part])
+            + contract_rows(jac_rows, gated[:, part]),
+            contract_rows(slope_term[:, part], sign_values),
+        )
+
+    in_far, out_far = grads(slice(hid, 2 * hid))
+    in_near, out_near = grads(slice(0, hid))
+    return (
+        factor * (in_near + other_core(in_far)),
+        factor * (out_near + other_core(out_far)),
     )
-    grad_out = factor * contract_rows(slope_term, sign_values)
-    return (grad_in, grad_out)
 
 
 def solution(mesh):
     fine = Mesh(
         mesh.devices.reshape(16, 2, 2, 2, 4), ("z", "xl", "core", "xh", "y")
     )
-    row, col = Z + NEAR, COL
+    row, col = LINE + ("core",), COL
     return jax.shard_map(
         on_device,
         mesh=fine,

time: 213 us -> 204 us (0.958)
  blocking collectives: 177 us -> 117 us
  starting transfers between devices: 9.66 us -> 36 us
  waiting for transfers between devices: 11.1 us -> 33.9 us
  matrix products: 4 us -> 8.36 us
  other arithmetic: 4.81 us -> 1.97 us
    all_to_all x9 -> x5, blocking collectives: 177 us -> 117 us  [exchange(): return lax.all_to_all(blocks, axes, 0, 0, tiled=True)]
    all_to_all x1 -> x2, waiting for transfers between devices: 11.1 us -> 33.9 us  [exchange(): return lax.all_to_all(blocks, axes, 0, 0, tiled=True)]
    ppermute x0 -> x4, starting transfers between devices: none -> 14.8 us  [other_core(): return lax.ppermute(array, 'core', [(0, 1), (1, 0)])]
    all_to_all x1 -> x2, starting transfers between devices: 9.66 us -> 21.2 us  [exchange(): return lax.all_to_all(blocks, axes, 0, 0, tiled=True)]
    dot_general x3 -> x6, matrix products: 2.21 us -> 6.55 us  [contract_rows(): lax.dot_general(left, right, (((0,), (0,)), ((), ())), preferred_element_...]
    reduce_sum x4 -> x3, other arithmetic: 2.66 us -> 0.33 us  [scatter_sum(): return exchange(blocks, axes).astype(F32).sum(axis=0)]
  transfers between devices with their start and end apart: 1 -> 6, of which waited for: 1 -> 2; matrix products, arithmetic and copies ran while one was open for 1% -> 3% of each run, Pallas kernels for 0% -> 0%
where the time goes in v2:
time: 204 us; the launch traced here: 203 us
  blocking collectives  117 us (57%)
  starting transfers between devices  36 us (18%)
  waiting for transfers between devices  33.9 us (17%)
  matrix products  8.36 us (4%)
  local copies, waits for them, and re-layouts  4.84 us (2%)
    all_to_all x5, blocking collectives, exchange(): return lax.all_to_all(blocks, axes, 0, 0, tiled=True)  117 us
    all_to_all x2, waiting for transfers between devices, exchange(): return lax.all_to_all(blocks, axes, 0, 0, tiled=True)  33.9 us
    all_to_all x2, starting transfers between devices, exchange(): return lax.all_to_all(blocks, axes, 0, 0, tiled=True)  21.2 us
    ppermute x4, starting transfers between devices, other_core(): return lax.ppermute(array, 'core', [(0, 1), (1, 0)])  14.8 us
    dot_general x6, matrix products, contract_rows(): lax.dot_general(left, right, (((0,), (0,)), ((), ())), preferred_element_...  6.55 us
  transfers between devices with their start and end apart: 6, of which 2 were waited for; matrix products, arithmetic and copies ran while one was open for 3% of the time, Pallas kernels for 0%

profile of v2, /device:TPU:1, one launch (start us, length us, event | category | flops | bytes accessed | tf_op | source)
XLA Modules:
  0.0 203.0 jit_solution(2265463814198481250)
XLA Ops:
  0.6 0.0 copy-start
  0.6 1.6 broadcast_in_dim.8
  2.3 17.0 %all-to-all-start = ((bf16[32,16,512]{2,1,0:T(8,128)(2,1)}), bf16[32,16,512]{2,1,0:T(8,128)(2,1)S(1)}, u32[]{:S(2)}, u32[]{:S(2)}) async-start(bf16[32,16,512]{2,1,0:T(8,128)(2,1)} %broadcast_in_dim.8), calls=%async_computation | async-start | bytes 1048576 | tf_op jit(solution)/shard_map/all_to_all | solution.py:33
  19.2 2.9 %collective-permute-start = (bf16[512,256]{1,0:T(8,128)(2,1)}, bf16[512,256]{1,0:T(8,128)(2,1)S(1)}, u32[]{:S(2)}, u32[]{:S(2)}) collective-permute-start(bf16[512,256]{1,0:T(8,128)(2,1)} %param.6), channel_id=1, source_target_pairs={{0,8},{8,0},{1,9},{9,1},{2,10},{10,2},{3,11},{11,3},{4,12},{12,4},... | collective-permute-start | bytes 786440 | tf_op jit(solution)/shard_map/ppermute | solution.py:50
  22.1 1.9 collective-permute-start.1
  24.0 1.0 constant_dynamic-update-slice_fusion.1
  25.0 1.4 fusion.6
  26.4 0.0 collective-permute-done
  26.4 0.0 collective-permute-done.1
  26.4 0.0 copy-done
  26.4 0.5 convolution_convert_fusion.3
  26.9 23.3 %all-to-all-done = bf16[32,16,512]{2,1,0:T(8,128)(2,1)S(1)} async-done(((bf16[32,16,512]{2,1,0:T(8,128)(2,1)}), bf16[32,16,512]{2,1,0:T(8,128)(2,1)S(1)}, u32[]{:S(2)}, u32[]{:S(2)}) %all-to-all-start) | async-done | bytes 524320 | tf_op jit(solution)/shard_map/all_to_all | solution.py:33
  50.2 0.4 convolution_convert_fusion
  50.6 0.1 pad_maximum_fusion
  50.8 19.2 %all_to_all.35 = bf16[8,64,1024]{2,1,0:T(8,128)(2,1)S(1)} all-to-all(bf16[8,64,1024]{2,1,0:T(8,128)(2,1)S(1)} %pad_maximum_fusion), channel_id=1, replica_groups=mesh['z'=16,'xl'=2,'core'=2,'xh'=2,'y'=4] {'xh','y'}, dimensions={0} | all-to-all | bytes 2097152 | tf_op jit(solution)/shard_map/all_to_all | solution.py:33
  69.9 0.2 convert_reduce_fusion
  70.1 0.1 multiply_convert_fusion.2
  70.2 13.0 %all_to_all.36 = bf16[8,64,512]{2,1,0:T(8,128)(2,1)S(1)} all-to-all(bf16[8,64,512]{2,1,0:T(8,128)(2,1)S(1)} %broadcast_in_dim.9), channel_id=1, replica_groups=mesh['z'=16,'xl'=2,'core'=2,'xh'=2,'y'=4] {'xh','y'}, dimensions={0} | all-to-all | bytes 1048576 | tf_op jit(solution)/shard_map/all_to_all | solution.py:33
  83.2 0.5 convolution_convert_fusion.2
  83.7 34.5 %all_to_all.37 = bf16[32,16,512]{2,1,0:T(8,128)(2,1)S(1)} all-to-all(bf16[32,16,512]{2,1,0:T(8,128)(2,1)S(1)} %bitcast.59), channel_id=1, replica_groups=mesh['z'=16,'xl'=2,'core'=2,'xh'=2,'y'=4] {'z','xl'}, dimensions={0} | all-to-all | bytes 1048576 | tf_op jit(solution)/shard_map/all_to_all | solution.py:33
  118.2 0.1 reduce_sum.31
  118.2 0.1 broadcast_in_dim.10
  118.3 35.6 %all_to_all.38 = bf16[32,16,512]{2,1,0:T(8,128)(2,1)S(1)} all-to-all(bf16[32,16,512]{2,1,0:T(8,128)(2,1)S(1)} %broadcast_in_dim.10), channel_id=1, replica_groups=mesh['z'=16,'xl'=2,'core'=2,'xh'=2,'y'=4] {'z','xl'}, dimensions={0} | all-to-all | bytes 1048576 | tf_op jit(solution)/shard_map/all_to_all | solution.py:33
  153.9 0.4 convolution_convert_fusion.1
  154.4 14.9 %all_to_all.39 = bf16[8,64,512]{2,1,0:T(8,128)(2,1)S(1)} all-to-all(bf16[8,64,512]{2,1,0:T(8,128)(2,1)S(1)} %bitcast.58), channel_id=1, replica_groups=mesh['z'=16,'xl'=2,'core'=2,'xh'=2,'y'=4] {'xh','y'}, dimensions={0} | all-to-all | bytes 1048576 | tf_op jit(solution)/shard_map/all_to_all | solution.py:33
  169.3 0.1 convert_reduce_fusion.1
  169.3 0.1 multiply_convert_fusion.1
  169.4 1.1 broadcast_in_dim.11
  170.6 4.2 %all-to-all-start.6 = ((bf16[8,64,1024]{2,1,0:T(8,128)(2,1)}), bf16[8,64,1024]{2,1,0:T(8,128)(2,1)}, u32[]{:S(2)}, u32[]{:S(2)}) async-start(bf16[8,64,1024]{2,1,0:T(8,128)(2,1)} %broadcast_in_dim.11), calls=%async_computation.6 | async-start | bytes 2097152 | tf_op jit(solution)/shard_map/all_to_all | solution.py:33
  174.8 0.3 fusion.12
  175.2 10.6 %all-to-all-done.6 = bf16[8,64,1024]{2,1,0:T(8,128)(2,1)} async-done(((bf16[8,64,1024]{2,1,0:T(8,128)(2,1)}), bf16[8,64,1024]{2,1,0:T(8,128)(2,1)}, u32[]{:S(2)}, u32[]{:S(2)}) %all-to-all-start.6) | async-done | bytes 1048608 | tf_op jit(solution)/shard_map/all_to_all | solution.py:33
  185.8 1.3 fusion.3
  187.0 8.1 %collective-permute-start.2 = (f32[512,256]{0,1:T(8,128)S(1)}, f32[512,256]{0,1:T(8,128)S(1)}, u32[]{:S(2)}, u32[]{:S(2)}) collective-permute-start(f32[512,256]{0,1:T(8,128)S(1)} %fusion.3), channel_id=1, source_target_pairs={{0,8},{8,0},{1,9},{9,1},{2,10},{10,2},{3,11},{11,3},{4,12},{12,4},... | collective-permute-start | bytes 1572872 | tf_op jit(solution)/shard_map/ppermute | solution.py:50
  195.1 1.3 fusion.9
  196.4 1.9 collective-permute-start.3
  198.3 0.3 fusion.15
  198.7 0.0 collective-permute-done.2
  198.7 1.3 fusion.2
  199.9 1.0 copy.9
  200.9 0.0 collective-permute-done.3
  200.9 2.1 %fusion.4 = f32[256,512]{1,0:T(8,128)} fusion(f32[256,512]{1,0:T(8,128)S(1)} %collective-permute-done.3, bf16[512,512]{1,0:T(8,128)(2,1)S(1)} %bitcast.57, bf16[512,1024]{1,0:T(8,128)(2,1)} %bitcast.10), kind=kOutput, calls=%fused_computation.12 | convolution fusion | flops 134479872 | bytes 1835008 | tf_op jit(solution)/shard_map/dot_general | solution.py:21
  (3 shorter events, 0.1 us)
Async XLA Ops:
  0.6 25.8 %copy-start = (bf16[256,512]{1,0:T(8,128)(2,1)S(1)}, bf16[256,512]{1,0:T(8,128)(2,1)}, u32[]{:S(2)}) copy-start(bf16[256,512]{1,0:T(8,128)(2,1)} %param.7) | copy-start | bytes 786436
  2.3 47.9 %all-to-all-start = ((bf16[32,16,512]{2,1,0:T(8,128)(2,1)}), bf16[32,16,512]{2,1,0:T(8,128)(2,1)S(1)}, u32[]{:S(2)}, u32[]{:S(2)}) async-start(bf16[32,16,512]{2,1,0:T(8,128)(2,1)} %broadcast_in_dim.8), calls=%async_computation | async-start | bytes 1048576 | tf_op jit(solution)/shard_map/all_to_all | solution.py:33
  19.2 7.2 %collective-permute-start = (bf16[512,256]{1,0:T(8,128)(2,1)}, bf16[512,256]{1,0:T(8,128)(2,1)S(1)}, u32[]{:S(2)}, u32[]{:S(2)}) collective-permute-start(bf16[512,256]{1,0:T(8,128)(2,1)} %param.6), channel_id=1, source_target_pairs={{0,8},{8,0},{1,9},{9,1},{2,10},{10,2},{3,11},{11,3},{4,12},{12,4},... | collective-permute-start | bytes 786440 | tf_op jit(solution)/shard_map/ppermute | solution.py:50
  22.1 4.3 %collective-permute-start.1 = (bf16[256,512]{1,0:T(8,128)(2,1)}, bf16[256,512]{1,0:T(8,128)(2,1)S(1)}, u32[]{:S(2)}, u32[]{:S(2)}) collective-permute-start(bf16[256,512]{1,0:T(8,128)(2,1)} %param.7), channel_id=1, source_target_pairs={{0,8},{8,0},{1,9},{9,1},{2,10},{10,2},{3,11},{11,3},{4,12},{12,4},... | collective-permute-start | bytes 786440 | tf_op jit(solution)/shard_map/ppermute | solution.py:50
  170.6 15.2 %all-to-all-start.6 = ((bf16[8,64,1024]{2,1,0:T(8,128)(2,1)}), bf16[8,64,1024]{2,1,0:T(8,128)(2,1)}, u32[]{:S(2)}, u32[]{:S(2)}) async-start(bf16[8,64,1024]{2,1,0:T(8,128)(2,1)} %broadcast_in_dim.11), calls=%async_computation.6 | async-start | bytes 2097152 | tf_op jit(solution)/shard_map/all_to_all | solution.py:33
  187.0 11.6 %collective-permute-start.2 = (f32[512,256]{0,1:T(8,128)S(1)}, f32[512,256]{0,1:T(8,128)S(1)}, u32[]{:S(2)}, u32[]{:S(2)}) collective-permute-start(f32[512,256]{0,1:T(8,128)S(1)} %fusion.3), channel_id=1, source_target_pairs={{0,8},{8,0},{1,9},{9,1},{2,10},{10,2},{3,11},{11,3},{4,12},{12,4},... | collective-permute-start | bytes 1572872 | tf_op jit(solution)/shard_map/ppermute | solution.py:50
  196.4 4.6 %collective-permute-start.3 = (f32[256,512]{1,0:T(8,128)S(1)}, f32[256,512]{1,0:T(8,128)S(1)}, u32[]{:S(2)}, u32[]{:S(2)}) collective-permute-start(f32[256,512]{1,0:T(8,128)S(1)} %fusion.9), channel_id=1, source_target_pairs={{0,8},{8,0},{1,9},{9,1},{2,10},{10,2},{3,11},{11,3},{4,12},{12,4},... | collective-permute-start | bytes 1572872 | tf_op jit(solution)/shard_map/ppermute | solution.py:50

commit v3 on v1

v3 whole, which is shorter than its diff:
```python
import jax
import jax.numpy as jnp
from jax import lax
from jax.sharding import Mesh, PartitionSpec as P

NEAR, COL = ("core", "xl"), ("xh", "y")
BF, F32 = jnp.bfloat16, jnp.float32


def local_terms(hidden, signal):
    cdf_part = 0.5 * (1.0 + lax.erf(hidden * 0.7071067811865476))
    pdf_part = jnp.exp(-0.5 * hidden * hidden) * 0.3989422804014327
    slope_full = cdf_part + hidden * pdf_part
    slopes = slope_full.astype(BF)
    bending = (signal * pdf_part * (2.0 - hidden * hidden)).astype(BF)
    gated = (signal * slope_full).astype(BF)
    return (slopes, bending, gated)


def contract_rows(left, right):
    return lax.dot_general(
        left, right, (((0,), (0,)), ((), ())), preferred_element_type=F32
    )


def contract_cols(left, right):
    return lax.dot_general(
        left, right, (((1,), (1,)), ((), ())), preferred_element_type=F32
    )


def exchange(blocks, axes):
    return lax.all_to_all(blocks, axes, 0, 0, tiled=True)


def gather(block, axes, count):
    rows, cols = block.shape
    return exchange(
        jnp.broadcast_to(block[None], (count, rows, cols)), axes
    ).reshape(count * rows, cols)


def scatter_sum(array, axes, count):
    rows, cols = array.shape
    blocks = array.astype(BF).reshape(count, rows // count, cols)
    return exchange(blocks, axes).astype(F32).sum(axis=0)


def pair_up(array, name, axis):
    far = lax.ppermute(array, name, [(0, 1), (1, 0)])
    return jnp.where(
        lax.axis_index(name) == 0,
        jnp.concatenate([array, far], axis=axis),
        jnp.concatenate([far, array], axis=axis),
    )


def on_device(tokens, probe_draw, w_in, w_out):
    total_rows = probe_draw.shape[0]
    own_rows, feats = tokens.shape
    nz, nn, nc = (lax.axis_size(a) for a in ("z", NEAR, COL))
    hid = w_in.shape[1]
    wide = nn * hid
    near = lax.axis_index(NEAR)
    w_in_all = pair_up(pair_up(w_in, "xl", 1), "core", 1)
    w_out_all = pair_up(pair_up(w_out, "xl", 0), "core", 0)
    draw = probe_draw.reshape(nz, nn, own_rows, feats)
    sign_all = (
        (2 * probe_draw - 1)
        .astype(BF)
        .reshape(nz, 2, 2, own_rows, feats)
        .transpose(2, 1, 0, 3, 4)
        .reshape(total_rows, feats)
    )
    mine = lax.axis_index(("xl", "core"))
    own_draw = lax.dynamic_index_in_dim(draw, mine, axis=1, keepdims=False)
    own_sign = (2 * own_draw - 1).astype(BF).reshape(nz * own_rows, feats)
    signal_part = contract_cols(own_sign, w_out_all)
    own_tokens = gather(tokens, "z", nz)
    all_tokens = lax.all_gather(own_tokens, NEAR, axis=0, tiled=True)
    hidden_part = jnp.dot(own_tokens, w_in_all, preferred_element_type=F32)
    both = scatter_sum(
        jnp.concatenate([hidden_part, signal_part], axis=1), COL, nc
    )
    slopes, bending, gated_own = local_terms(both[:, :wide], both[:, wide:])
    gated = gather(gated_own, COL, nc)
    gated_all = lax.all_gather(gated, NEAR, axis=0, tiled=True)
    gated_hid = lax.dynamic_slice_in_dim(gated_all, near * hid, hid, axis=1)
    jac_own = scatter_sum(contract_cols(gated, w_in_all), "z", nz).astype(BF)
    jac_rows = gather(jac_own, "z", nz)
    jac_all = lax.all_gather(jac_rows, NEAR, axis=0, tiled=True)
    back_part = jnp.dot(jac_rows, w_in_all, preferred_element_type=F32)
    back_proj = scatter_sum(back_part, COL, nc)
    rows = back_proj.shape[0]
    curv_own = (back_proj * bending).astype(BF).reshape(rows, nn, hid)
    slope_own = (back_proj * slopes).astype(BF).reshape(rows, nn, hid)
    terms = jnp.concatenate([curv_own, slope_own], axis=2).transpose(1, 0, 2)
    terms = jnp.broadcast_to(terms[:, None], (nn, nc, rows, 2 * hid))
    terms = exchange(
        terms.reshape(nn * nc, rows, 2 * hid), NEAR + COL
    ).reshape(total_rows, 2 * hid)
    curv_term, slope_term = terms[:, :hid], terms[:, hid:]
    factor = 1.0 / jnp.sqrt(jnp.float32(total_rows))
    grad_in = factor * (
        contract_rows(all_tokens, curv_term) + contract_rows(jac_all, gated_hid)
    )
    grad_out = factor * contract_rows(slope_term, sign_all)
    return (grad_in, grad_out)


def solution(mesh):
    fine = Mesh(
        mesh.devices.reshape(16, 2, 2, 2, 4), ("z", "xl", "core", "xh", "y")
    )
    row, col = ("z", "xl", "core"), COL
    return jax.shard_map(
        on_device,
        mesh=fine,
        in_specs=(P(row, col), P(None, col), P(col, row), P(row, col)),
        out_specs=(P(col, row), P(row, col)),
        check_vma=False,
    )
```

time: 213 us -> 213 us (level)
  blocking collectives: 177 us -> 63.7 us
  waiting for transfers between devices: 11.1 us -> 59.2 us
  starting transfers between devices: 9.66 us -> 53.1 us
  between operations: 0.77 us -> 14 us
  matrix products: 4 us -> 13.5 us
    all_to_all x9 -> x3, blocking collectives: 177 us -> 63.7 us  [exchange(): return lax.all_to_all(blocks, axes, 0, 0, tiled=True)]
    all_to_all x1 -> x4, starting transfers between devices: 9.66 us -> 39.2 us  [exchange(): return lax.all_to_all(blocks, axes, 0, 0, tiled=True)]
    all_to_all x1 -> x4, waiting for transfers between devices: 11.1 us -> 39.8 us  [exchange(): return lax.all_to_all(blocks, axes, 0, 0, tiled=True)]
    all_gather x0 -> x3, waiting for transfers between devices: none -> 16 us  [the longest x1 16 us: on_device(): jac_all = lax.all_gather(jac_rows, NEAR, axis=0, tiled=True)]
    ppermute x0 -> x4, starting transfers between devices: none -> 13.7 us  [pair_up(): far = lax.ppermute(array, name, [(0, 1), (1, 0)])]
    dot_general x2, matrix products: 0.86 us -> 4.34 us  [the longest x1 2.56 us: on_device(): back_part = jnp.dot(jac_rows, w_in_all, preferred_element_type=F32)]
    dot_general x2, matrix products: 0.93 us -> 4.36 us  [contract_cols(): lax.dot_general(left, right, (((1,), (1,)), ((), ())), preferred_element_...]
    dot_general x3, matrix products: 2.21 us -> 4.77 us  [contract_rows(): lax.dot_general(left, right, (((0,), (0,)), ((), ())), preferred_element_...]
  transfers between devices with their start and end apart: 1 -> 11, of which waited for: 1 -> 5; matrix products, arithmetic and copies ran while one was open for 1% -> 8% of each run, Pallas kernels for 0% -> 0%
where the time goes in v3:
time: 213 us; the launch traced here: 212 us
  blocking collectives  63.7 us (30%)
  waiting for transfers between devices  59.2 us (28%)
  starting transfers between devices  53.1 us (25%)
  between operations  14 us (7%)
  matrix products  13.5 us (6%)
  other arithmetic  4.39 us (2%)
  local copies, waits for them, and re-layouts  3.81 us (2%)
    all_to_all x3, blocking collectives, exchange(): return lax.all_to_all(blocks, axes, 0, 0, tiled=True)  63.7 us
    all_to_all x4, waiting for transfers between devices, exchange(): return lax.all_to_all(blocks, axes, 0, 0, tiled=True)  39.8 us
    all_to_all x4, starting transfers between devices, exchange(): return lax.all_to_all(blocks, axes, 0, 0, tiled=True)  39.2 us
    all_gather x1, waiting for transfers between devices, on_device(): jac_all = lax.all_gather(jac_rows, NEAR, axis=0, tiled=True)  16 us
    ppermute x4, starting transfers between devices, pair_up(): far = lax.ppermute(array, name, [(0, 1), (1, 0)])  13.7 us
    dot_general x3, matrix products, contract_rows(): lax.dot_general(left, right, (((0,), (0,)), ((), ())), preferred_element_...  4.77 us
    dot_general x2, matrix products, contract_cols(): lax.dot_general(left, right, (((1,), (1,)), ((), ())), preferred_element_...  4.36 us
  transfers between devices with their start and end apart: 11, of which 5 were waited for; matrix products, arithmetic and copies ran while one was open for 8% of the time, Pallas kernels for 0%

profile of v3, /device:TPU:1, one launch (start us, length us, event | category | flops | bytes accessed | tf_op | source)
XLA Modules:
  0.0 211.7 jit_solution(1319122325145488746)
XLA Ops:
  7.2 4.1 %collective-permute-start.2 = (bf16[256,512]{1,0:T(8,128)(2,1)}, bf16[256,512]{1,0:T(8,128)(2,1)S(1)}, u32[]{:S(2)}, u32[]{:S(2)}) collective-permute-start(bf16[256,512]{1,0:T(8,128)(2,1)} %param.7), channel_id=1, source_target_pairs={{0,16},{16,0},{1,17},{17,1},{2,18},{18,2},{3,19},{19,3},{4,20},{20... | collective-permute-start | bytes 786440 | tf_op jit(solution)/shard_map/ppermute | solution.py:50
  11.3 1.4 broadcast_in_dim.8
  12.7 14.9 %all-to-all-start = ((bf16[16,16,512]{2,1,0:T(8,128)(2,1)}), bf16[16,16,512]{2,1,0:T(8,128)(2,1)S(1)}, u32[]{:S(2)}, u32[]{:S(2)}) async-start(bf16[16,16,512]{2,1,0:T(8,128)(2,1)} %broadcast_in_dim.8), calls=%async_computation | async-start | bytes 524288 | tf_op jit(solution)/shard_map/all_to_all | solution.py:33
  27.6 2.2 %collective-permute-start = (bf16[512,256]{1,0:T(8,128)(2,1)}, bf16[512,256]{1,0:T(8,128)(2,1)}, u32[]{:S(2)}, u32[]{:S(2)}) collective-permute-start(bf16[512,256]{1,0:T(8,128)(2,1)} %param.6), channel_id=1, source_target_pairs={{0,16},{16,0},{1,17},{17,1},{2,18},{18,2},{3,19},{19,3},{4,20},{20... | collective-permute-start | bytes 786440 | tf_op jit(solution)/shard_map/ppermute | solution.py:50
  29.8 1.2 maximum_select_fusion.3
  31.0 3.4 %collective-permute-start.3 = (bf16[512,512]{1,0:T(8,128)(2,1)S(1)}, bf16[512,512]{1,0:T(8,128)(2,1)}, u32[]{:S(2)}, u32[]{:S(2)}) collective-permute-start(bf16[512,512]{1,0:T(8,128)(2,1)S(1)} %maximum_select_fusion.3), channel_id=1, source_target_pairs={{0,8},{8,0},{1,9},{9,1},{2,10},{10,2},{3,11},{11,3},{4,12},{12,4},... | collective-permute-start | bytes 1572872 | tf_op jit(solution)/shard_map/ppermute | solution.py:50
  34.4 2.0 collective-permute-done
  36.4 1.3 maximum_select_fusion.2
  37.7 0.0 copy-start.3
  37.7 4.1 %collective-permute-start.1 = (bf16[512,512]{1,0:T(8,128)(2,1)S(1)}, bf16[512,512]{1,0:T(8,128)(2,1)}, u32[]{:S(2)}, u32[]{:S(2)}) collective-permute-start(bf16[512,512]{1,0:T(8,128)(2,1)S(1)} %maximum_select_fusion.2), channel_id=1, source_target_pairs={{0,8},{8,0},{1,9},{9,1},{2,10},{10,2},{3,11},{11,3},{4,12},{12,4},... | collective-permute-start | bytes 1572872 | tf_op jit(solution)/shard_map/ppermute | solution.py:50
  41.8 0.1 fusion.12
  41.9 2.5 %convolution_convert_fusion.2 = bf16[8,32,1024]{2,1,0:T(8,128)(2,1)} fusion(bf16[8,32,512]{2,1,0:T(8,128)(2,1)S(1)} %bitcast.49, bf16[512,512]{1,0:T(8,128)(2,1)} %collective-permute-done.3, bf16[512,512]{1,0:T(8,128)(2,1)S(1)} %maximum_select_fusion.3, pred[]{:T(512)S(6)} %eq.8), kind=kOutput, calls=%fused_computation.4 | convolution fusion | flops 273416192 | bytes 1835009 | tf_op jit(solution)/shard_map/dot_general | solution.py:27
  44.5 0.0 copy-start.5
  44.5 1.8 convolution_convert_fusion
  46.3 1.1 pad_maximum_fusion
  47.4 6.4 %all-to-all-start.1 = ((bf16[8,32,2048]{2,1,0:T(8,128)(2,1)}), bf16[8,32,2048]{2,1,0:T(8,128)(2,1)S(1)}, u32[]{:S(2)}, u32[]{:S(2)}) async-start(bf16[8,32,2048]{2,1,0:T(8,128)(2,1)} %pad_maximum_fusion), calls=%async_computation.1 | async-start | bytes 2097152 | tf_op jit(solution)/shard_map/all_to_all | solution.py:33
  53.7 0.0 all-gather.4.cloned.1.call-start
  53.8 0.7 all-gather.4.cloned.1.call-update
  54.5 0.0 all-gather.8.cloned.1.call-start
  54.5 11.3 %all-to-all-done.1 = bf16[8,32,2048]{2,1,0:T(8,128)(2,1)S(1)} async-done(((bf16[8,32,2048]{2,1,0:T(8,128)(2,1)}), bf16[8,32,2048]{2,1,0:T(8,128)(2,1)S(1)}, u32[]{:S(2)}, u32[]{:S(2)}) %all-to-all-start.1) | async-done | bytes 1048608 | tf_op jit(solution)/shard_map/all_to_all | solution.py:33
  65.8 0.1 convert_reduce_fusion
  66.0 0.0 copy-start.4
  66.0 0.1 multiply_convert_fusion.2
  66.0 0.1 broadcast_in_dim.9
  66.1 19.6 %all_to_all.35 = bf16[8,32,1024]{2,1,0:T(8,128)(2,1)} all-to-all(bf16[8,32,1024]{2,1,0:T(8,128)(2,1)S(1)} %broadcast_in_dim.9), channel_id=1, replica_groups=mesh['z'=16,'xl'=2,'core'=2,'xh'=2,'y'=4] {'xh','y'}, dimensions={0} | all-to-all | bytes 1048576 | tf_op jit(solution)/shard_map/all_to_all | solution.py:33
  85.7 0.0 all-gather.8.cloned.1.call-update
  85.8 1.8 convolution_convert_fusion.3
  87.6 24.8 %all_to_all.36 = bf16[16,16,512]{2,1,0:T(8,128)(2,1)S(1)} all-to-all(bf16[16,16,512]{2,1,0:T(8,128)(2,1)S(1)} %bitcast.48), channel_id=1, replica_groups=mesh['z'=16,'xl'=2,'core'=2,'xh'=2,'y'=4] {'z'}, dimensions={0} | all-to-all | bytes 524288 | tf_op jit(solution)/shard_map/all_to_all | solution.py:33
  112.5 19.3 %all_to_all.37 = bf16[16,16,512]{2,1,0:T(8,128)(2,1)S(1)} all-to-all(bf16[16,16,512]{2,1,0:T(8,128)(2,1)S(1)} %broadcast_in_dim.10), channel_id=1, replica_groups=mesh['z'=16,'xl'=2,'core'=2,'xh'=2,'y'=4] {'z'}, dimensions={0} | all-to-all | bytes 524288 | tf_op jit(solution)/shard_map/all_to_all | solution.py:33
  131.7 2.6 %convolution_convert_fusion.1 = bf16[256,1024]{1,0:T(8,128)(2,1)} fusion(bf16[256,512]{1,0:T(8,128)(2,1)S(1)} %bitcast.45, bf16[512,512]{1,0:T(8,128)(2,1)} %collective-permute-done.1, bf16[512,512]{1,0:T(8,128)(2,1)S(1)} %copy-done.4, pred[]{:T(512)S(6)} %eq.8), kind=kOutput, calls=%fused_computation.3 | convolution fusion | flops 273416192 | bytes 1835009 | tf_op jit(solution)/shard_map/dot_general | solution.py:92
  134.3 6.0 %all-to-all-start.5 = ((bf16[8,32,1024]{2,1,0:T(8,128)(2,1)}), bf16[8,32,1024]{2,1,0:T(8,128)(2,1)S(1)}, u32[]{:S(2)}, u32[]{:S(2)}) async-start(bf16[8,32,1024]{2,1,0:T(8,128)(2,1)} %bitcast.9), calls=%async_computation.5 | async-start | bytes 1048576 | tf_op jit(solution)/shard_map/all_to_all | solution.py:33
  140.2 0.0 all-gather.6.cloned.1.call-start
  140.3 0.7 all-gather.6.cloned.1.call-update
  141.0 12.5 %all-to-all-done.5 = bf16[8,32,1024]{2,1,0:T(8,128)(2,1)S(1)} async-done(((bf16[8,32,1024]{2,1,0:T(8,128)(2,1)}), bf16[8,32,1024]{2,1,0:T(8,128)(2,1)S(1)}, u32[]{:S(2)}, u32[]{:S(2)}) %all-to-all-start.5) | async-done | bytes 524320 | tf_op jit(solution)/shard_map/all_to_all | solution.py:33
  153.5 0.1 convert_reduce_fusion.1
  153.5 0.1 multiply_convert_fusion.1
  153.7 0.1 maximum_bitcast_fusion
  153.8 1.1 broadcast_in_dim.11
  154.9 12.0 %all-to-all-start.6 = ((bf16[32,32,512]{2,1,0:T(8,128)(2,1)}), bf16[32,32,512]{2,1,0:T(8,128)(2,1)S(1)}, u32[]{:S(2)}, u32[]{:S(2)}) async-start(bf16[32,32,512]{2,1,0:T(8,128)(2,1)} %bitcast.11), calls=%async_computation.6 | async-start | bytes 2097152 | tf_op jit(solution)/shard_map/all_to_all | solution.py:33
  166.9 0.3 add_convert_fusion
  167.2 0.1 copy.17
  167.3 16.0 %all-to-all-done.6 = bf16[32,32,512]{2,1,0:T(8,128)(2,1)S(1)} async-done(((bf16[32,32,512]{2,1,0:T(8,128)(2,1)}), bf16[32,32,512]{2,1,0:T(8,128)(2,1)S(1)}, u32[]{:S(2)}, u32[]{:S(2)}) %all-to-all-start.6) | async-done | bytes 1048608 | tf_op jit(solution)/shard_map/all_to_all | solution.py:33
  183.3 1.3 convolution_multiply_fusion
  184.6 1.7 convolution_bitcast_fusion
  186.3 0.0 all-gather.8.cloned.1.call-done
  186.3 16.0 %all-gather.6.cloned.1.call-done = bf16[1024,512]{1,0:T(8,128)(2,1)} async-done(((bf16[256,512]{1,0:T(8,128)(2,1)}), bf16[1024,512]{1,0:T(8,128)(2,1)}) %all-gather.6.cloned.1.call-update) | async-done | bytes 1048592 | tf_op jit(solution)/shard_map/all_gather | solution.py:91
  202.3 1.8 fusion
  204.1 1.0 copy.18
  (19 shorter events, 0.2 us)
Async XLA Ops:
  7.2 34.7 %copy-start = (s32[1024,512]{1,0:T(8,128)S(1)}, s32[1024,512]{1,0:T(8,128)}, u32[]{:S(2)}) copy-start(s32[1024,512]{1,0:T(8,128)} %param.5) | copy-start | bytes 6291460
  7.2 22.6 %collective-permute-start.2 = (bf16[256,512]{1,0:T(8,128)(2,1)}, bf16[256,512]{1,0:T(8,128)(2,1)S(1)}, u32[]{:S(2)}, u32[]{:S(2)}) collective-permute-start(bf16[256,512]{1,0:T(8,128)(2,1)} %param.7), channel_id=1, source_target_pairs={{0,16},{16,0},{1,17},{17,1},{2,18},{18,2},{3,19},{19,3},{4,20},{20... | collective-permute-start | bytes 786440 | tf_op jit(solution)/shard_map/ppermute | solution.py:50
  12.7 31.7 %all-to-all-start = ((bf16[16,16,512]{2,1,0:T(8,128)(2,1)}), bf16[16,16,512]{2,1,0:T(8,128)(2,1)S(1)}, u32[]{:S(2)}, u32[]{:S(2)}) async-start(bf16[16,16,512]{2,1,0:T(8,128)(2,1)} %broadcast_in_dim.8), calls=%async_computation | async-start | bytes 524288 | tf_op jit(solution)/shard_map/all_to_all | solution.py:33
  27.6 8.8 %collective-permute-start = (bf16[512,256]{1,0:T(8,128)(2,1)}, bf16[512,256]{1,0:T(8,128)(2,1)}, u32[]{:S(2)}, u32[]{:S(2)}) collective-permute-start(bf16[512,256]{1,0:T(8,128)(2,1)} %param.6), channel_id=1, source_target_pairs={{0,16},{16,0},{1,17},{17,1},{2,18},{18,2},{3,19},{19,3},{4,20},{20... | collective-permute-start | bytes 786440 | tf_op jit(solution)/shard_map/ppermute | solution.py:50
  31.0 10.9 %collective-permute-start.3 = (bf16[512,512]{1,0:T(8,128)(2,1)S(1)}, bf16[512,512]{1,0:T(8,128)(2,1)}, u32[]{:S(2)}, u32[]{:S(2)}) collective-permute-start(bf16[512,512]{1,0:T(8,128)(2,1)S(1)} %maximum_select_fusion.3), channel_id=1, source_target_pairs={{0,8},{8,0},{1,9},{9,1},{2,10},{10,2},{3,11},{11,3},{4,12},{12,4},... | collective-permute-start | bytes 1572872 | tf_op jit(solution)/shard_map/ppermute | solution.py:50
  37.7 6.7 %copy-start.3 = (bf16[512,512]{1,0:T(8,128)(2,1)}, bf16[512,512]{1,0:T(8,128)(2,1)S(1)}, u32[]{:S(2)}) copy-start(bf16[512,512]{1,0:T(8,128)(2,1)S(1)} %maximum_select_fusion.2) | copy-start | bytes 1572868
  37.7 6.7 %collective-permute-start.1 = (bf16[512,512]{1,0:T(8,128)(2,1)S(1)}, bf16[512,512]{1,0:T(8,128)(2,1)}, u32[]{:S(2)}, u32[]{:S(2)}) collective-permute-start(bf16[512,512]{1,0:T(8,128)(2,1)S(1)} %maximum_select_fusion.2), channel_id=1, source_target_pairs={{0,8},{8,0},{1,9},{9,1},{2,10},{10,2},{3,11},{11,3},{4,12},{12,4},... | collective-permute-start | bytes 1572872 | tf_op jit(solution)/shard_map/ppermute | solution.py:50
  44.5 1.8 copy-start.1
  44.5 1.8 copy-start.5
  47.4 18.4 %all-to-all-start.1 = ((bf16[8,32,2048]{2,1,0:T(8,128)(2,1)}), bf16[8,32,2048]{2,1,0:T(8,128)(2,1)S(1)}, u32[]{:S(2)}, u32[]{:S(2)}) async-start(bf16[8,32,2048]{2,1,0:T(8,128)(2,1)} %pad_maximum_fusion), calls=%async_computation.1 | async-start | bytes 2097152 | tf_op jit(solution)/shard_map/all_to_all | solution.py:33
  53.7 130.9 %all-gather.4.cloned.1.call-start = ((), (), s32[]{:S(2)}) async-start(), calls=%async_computation.7 | async-start | bytes 1310720 | tf_op jit(solution)/shard_map/all_gather | solution.py:80
  54.5 131.8 %all-gather.8.cloned.1.call-start = ((), (), s32[]{:S(2)}) async-start(), calls=%async_computation.9 | async-start | bytes 2621440 | tf_op jit(solution)/shard_map/all_gather | solution.py:87
  66.0 19.8 %copy-start.4 = (bf16[512,512]{1,0:T(8,128)(2,1)S(1)}, bf16[512,512]{1,0:T(8,128)(2,1)}, u32[]{:S(2)}) copy-start(bf16[512,512]{1,0:T(8,128)(2,1)} %copy-done.3) | copy-start | bytes 1572868
  131.7 2.6 %copy-start.2 = (bf16[16,16,512]{2,1,0:T(8,128)(2,1)}, bf16[16,16,512]{2,1,0:T(8,128)(2,1)S(1)}, u32[]{:S(2)}) copy-start(bf16[16,16,512]{2,1,0:T(8,128)(2,1)S(1)} %all_to_all.37) | copy-start | bytes 786436
  134.3 19.2 %all-to-all-start.5 = ((bf16[8,32,1024]{2,1,0:T(8,128)(2,1)}), bf16[8,32,1024]{2,1,0:T(8,128)(2,1)S(1)}, u32[]{:S(2)}, u32[]{:S(2)}) async-start(bf16[8,32,1024]{2,1,0:T(8,128)(2,1)} %bitcast.9), calls=%async_computation.5 | async-start | bytes 1048576 | tf_op jit(solution)/shard_map/all_to_all | solution.py:33
  140.2 62.0 %all-gather.6.cloned.1.call-start = ((), (), s32[]{:S(2)}) async-start(), calls=%async_computation.8 | async-start | bytes 1310720 | tf_op jit(solution)/shard_map/all_gather | solution.py:91
  154.9 28.4 %all-to-all-start.6 = ((bf16[32,32,512]{2,1,0:T(8,128)(2,1)}), bf16[32,32,512]{2,1,0:T(8,128)(2,1)S(1)}, u32[]{:S(2)}, u32[]{:S(2)}) async-start(bf16[32,32,512]{2,1,0:T(8,128)(2,1)} %bitcast.11), calls=%async_computation.6 | async-start | bytes 2097152 | tf_op jit(solution)/shard_map/all_to_all | solution.py:33
Sparse Core Ops, SparseCore 0:
  56.7 40.9 all-gather.3
  99.7 61.6 all-gather.7
  164.1 38.1 all-gather.5

commit v4 on v3

--- a/solution.py
+++ b/solution.py
@@ -55,13 +55,27 @@
     )
 
 
+def hand_over(array, name, axis):
+    half = array.shape[-1] // 2
+    left, right = array[..., :half], array[..., half:]
+    first = lax.axis_index(name) == 0
+    kept = jnp.where(first, left, right)
+    far = lax.ppermute(
+        jnp.where(first, right, left), name, [(0, 1), (1, 0)]
+    )
+    return jnp.where(
+        first,
+        jnp.concatenate([kept, far], axis=axis),
+        jnp.concatenate([far, kept], axis=axis),
+    )
+
+
 def on_device(tokens, probe_draw, w_in, w_out):
     total_rows = probe_draw.shape[0]
     own_rows, feats = tokens.shape
     nz, nn, nc = (lax.axis_size(a) for a in ("z", NEAR, COL))
     hid = w_in.shape[1]
     wide = nn * hid
-    near = lax.axis_index(NEAR)
     w_in_all = pair_up(pair_up(w_in, "xl", 1), "core", 1)
     w_out_all = pair_up(pair_up(w_out, "xl", 0), "core", 0)
     draw = probe_draw.reshape(nz, nn, own_rows, feats)
@@ -77,18 +91,18 @@
     own_sign = (2 * own_draw - 1).astype(BF).reshape(nz * own_rows, feats)
     signal_part = contract_cols(own_sign, w_out_all)
     own_tokens = gather(tokens, "z", nz)
-    all_tokens = lax.all_gather(own_tokens, NEAR, axis=0, tiled=True)
+    all_tokens = pair_up(pair_up(own_tokens, "xl", 0), "core", 0)
     hidden_part = jnp.dot(own_tokens, w_in_all, preferred_element_type=F32)
     both = scatter_sum(
         jnp.concatenate([hidden_part, signal_part], axis=1), COL, nc
     )
     slopes, bending, gated_own = local_terms(both[:, :wide], both[:, wide:])
     gated = gather(gated_own, COL, nc)
-    gated_all = lax.all_gather(gated, NEAR, axis=0, tiled=True)
-    gated_hid = lax.dynamic_slice_in_dim(gated_all, near * hid, hid, axis=1)
+    gated_hid = hand_over(hand_over(gated[None], "core", 0), "xl", 1)
+    gated_hid = gated_hid.reshape(total_rows, hid)
     jac_own = scatter_sum(contract_cols(gated, w_in_all), "z", nz).astype(BF)
     jac_rows = gather(jac_own, "z", nz)
-    jac_all = lax.all_gather(jac_rows, NEAR, axis=0, tiled=True)
+    jac_all = pair_up(pair_up(jac_rows, "xl", 0), "core", 0)
     back_part = jnp.dot(jac_rows, w_in_all, preferred_element_type=F32)
     back_proj = scatter_sum(back_part, COL, nc)
     rows = back_proj.shape[0]

time: 213 us -> 182 us (0.85)
  waiting for transfers between devices: 59.2 us -> 10.1 us
  blocking collectives: 63.7 us -> 82.8 us
  between operations: 14 us -> 1.04 us
  starting transfers between devices: 53.1 us -> 63.9 us
    all_to_all x4 -> x3, waiting for transfers between devices: 39.8 us -> 0.01 us  [exchange(): return lax.all_to_all(blocks, axes, 0, 0, tiled=True)]
    all_to_all x3 -> x4, blocking collectives: 63.7 us -> 82.8 us  [exchange(): return lax.all_to_all(blocks, axes, 0, 0, tiled=True)]
    all_gather x3 -> x0, waiting for transfers between devices: 16 us -> none  [the longest x1 16 us: on_device(): jac_all = lax.all_gather(jac_rows, NEAR, axis=0, tiled=True)]
    ppermute x0 -> x2, starting transfers between devices: none -> 11.8 us  [hand_over(): far = lax.ppermute(jnp.where(first, right, left), name, [(0, 1), (1, 0)])]
    all_to_all x4 -> x3, starting transfers between devices: 39.2 us -> 28.4 us  [exchange(): return lax.all_to_all(blocks, axes, 0, 0, tiled=True)]
    ppermute x4 -> x8, starting transfers between devices: 13.7 us -> 23.6 us  [pair_up(): far = lax.ppermute(array, name, [(0, 1), (1, 0)])]
    ppermute x0 -> x2, waiting for transfers between devices: none -> 8.17 us  [hand_over(): far = lax.ppermute(jnp.where(first, right, left), name, [(0, 1), (1, 0)])]
    select_n x2 -> x4, other arithmetic: 2.5 us -> 5.02 us  [pair_up(): jnp.where(lax.axis_index(name) == 0, jnp.concatenate([array, far], axis=a...]
  transfers between devices with their start and end apart: 11 -> 13, of which waited for: 5 -> 2; matrix products, arithmetic and copies ran while one was open for 8% -> 8% of each run, Pallas kernels for 0% -> 0%
where the time goes in v4:
time: 182 us; the launch traced here: 181 us
  blocking collectives  82.8 us (45%)
  starting transfers between devices  63.9 us (35%)
  matrix products  14 us (8%)
  waiting for transfers between devices  10.1 us (6%)
  other arithmetic  6.28 us (3%)
  local copies, waits for them, and re-layouts  2.83 us (2%)
    all_to_all x4, blocking collectives, exchange(): return lax.all_to_all(blocks, axes, 0, 0, tiled=True)  82.8 us
    all_to_all x3, starting transfers between devices, exchange(): return lax.all_to_all(blocks, axes, 0, 0, tiled=True)  28.4 us
    ppermute x8, starting transfers between devices, pair_up(): far = lax.ppermute(array, name, [(0, 1), (1, 0)])  23.6 us
    ppermute x2, starting transfers between devices, hand_over(): far = lax.ppermute(jnp.where(first, right, left), name, [(0, 1), (1, 0)])  11.8 us
    ppermute x2, waiting for transfers between devices, hand_over(): far = lax.ppermute(jnp.where(first, right, left), name, [(0, 1), (1, 0)])  8.17 us
    dot_general x3, matrix products, contract_rows(): lax.dot_general(left, right, (((0,), (0,)), ((), ())), preferred_element_...  5.1 us
    select_n x4, other arithmetic, pair_up(): jnp.where(lax.axis_index(name) == 0, jnp.concatenate([array, far], axis=a...  5.02 us
    dot_general x2, matrix products, contract_cols(): lax.dot_general(left, right, (((1,), (1,)), ((), ())), preferred_element_...  4.24 us
  transfers between devices with their start and end apart: 13, of which 2 were waited for; matrix products, arithmetic and copies ran while one was open for 8% of the time, Pallas kernels for 0%

profile of v4, /device:TPU:1, one launch (start us, length us, event | category | flops | bytes accessed | tf_op | source)
XLA Modules:
  0.0 181.0 jit_solution(16266488653108076981)
XLA Ops:
  0.6 4.1 %collective-permute-start.4 = (bf16[256,512]{1,0:T(8,128)(2,1)}, bf16[256,512]{1,0:T(8,128)(2,1)S(1)}, u32[]{:S(2)}, u32[]{:S(2)}) collective-permute-start(bf16[256,512]{1,0:T(8,128)(2,1)} %param.7), channel_id=1, source_target_pairs={{0,16},{16,0},{1,17},{17,1},{2,18},{18,2},{3,19},{19,3},{4,20},{20... | collective-permute-start | bytes 786440 | tf_op jit(solution)/shard_map/ppermute | solution.py:50
  4.7 1.5 broadcast_in_dim.8
  6.2 14.9 %all-to-all-start = ((bf16[16,16,512]{2,1,0:T(8,128)(2,1)}), bf16[16,16,512]{2,1,0:T(8,128)(2,1)S(1)}, u32[]{:S(2)}, u32[]{:S(2)}) async-start(bf16[16,16,512]{2,1,0:T(8,128)(2,1)} %broadcast_in_dim.8), calls=%async_computation | async-start | bytes 524288 | tf_op jit(solution)/shard_map/all_to_all | solution.py:33
  21.1 2.2 %collective-permute-start.2 = (bf16[512,256]{1,0:T(8,128)(2,1)}, bf16[512,256]{1,0:T(8,128)(2,1)}, u32[]{:S(2)}, u32[]{:S(2)}) collective-permute-start(bf16[512,256]{1,0:T(8,128)(2,1)} %param.6), channel_id=1, source_target_pairs={{0,16},{16,0},{1,17},{17,1},{2,18},{18,2},{3,19},{19,3},{4,20},{20... | collective-permute-start | bytes 786440 | tf_op jit(solution)/shard_map/ppermute | solution.py:50
  23.3 0.0 collective-permute-done.4
  23.3 1.2 maximum_select_fusion.8
  24.5 3.4 %collective-permute-start.5 = (bf16[512,512]{1,0:T(8,128)(2,1)S(1)}, bf16[512,512]{1,0:T(8,128)(2,1)}, u32[]{:S(2)}, u32[]{:S(2)}) collective-permute-start(bf16[512,512]{1,0:T(8,128)(2,1)S(1)} %maximum_select_fusion.8), channel_id=1, source_target_pairs={{0,8},{8,0},{1,9},{9,1},{2,10},{10,2},{3,11},{11,3},{4,12},{12,4},... | collective-permute-start | bytes 1572872 | tf_op jit(solution)/shard_map/ppermute | solution.py:50
  28.0 1.9 %collective-permute-done.2 = bf16[512,256]{1,0:T(8,128)(2,1)} collective-permute-done((bf16[512,256]{1,0:T(8,128)(2,1)}, bf16[512,256]{1,0:T(8,128)(2,1)}, u32[]{:S(2)}, u32[]{:S(2)}) %collective-permute-start.2) | collective-permute-done | bytes 262176 | tf_op jit(solution)/shard_map/ppermute | solution.py:50
  29.9 1.3 maximum_select_fusion.7
  31.2 0.0 copy-start.3
  31.2 4.1 %collective-permute-start.3 = (bf16[512,512]{1,0:T(8,128)(2,1)S(1)}, bf16[512,512]{1,0:T(8,128)(2,1)}, u32[]{:S(2)}, u32[]{:S(2)}) collective-permute-start(bf16[512,512]{1,0:T(8,128)(2,1)S(1)} %maximum_select_fusion.7), channel_id=1, source_target_pairs={{0,8},{8,0},{1,9},{9,1},{2,10},{10,2},{3,11},{11,3},{4,12},{12,4},... | collective-permute-start | bytes 1572872 | tf_op jit(solution)/shard_map/ppermute | solution.py:50
  35.3 0.1 fusion.25
  35.4 0.0 collective-permute-done.5
  35.4 2.6 %convolution_convert_fusion.2 = bf16[8,32,1024]{2,1,0:T(8,128)(2,1)} fusion(bf16[8,32,512]{2,1,0:T(8,128)(2,1)S(1)} %bitcast.47, bf16[512,512]{1,0:T(8,128)(2,1)} %collective-permute-done.5, bf16[512,512]{1,0:T(8,128)(2,1)S(1)} %maximum_select_fusion.8, pred[]{:T(512)S(6)} %eq.4), kind=kOutput, calls=%fused_computation.4 | convolution fusion | flops 273416192 | bytes 1835009 | tf_op jit(solution)/shard_map/dot_general | solution.py:27
  38.0 0.0 copy-start.4
  38.0 1.8 convolution_convert_fusion
  39.8 0.1 pad_maximum_fusion
  39.9 19.5 %all_to_all.35 = bf16[8,32,2048]{2,1,0:T(8,128)(2,1)S(1)} all-to-all(bf16[8,32,2048]{2,1,0:T(8,128)(2,1)S(1)} %pad_maximum_fusion), channel_id=1, replica_groups=mesh['z'=16,'xl'=2,'core'=2,'xh'=2,'y'=4] {'xh','y'}, dimensions={0} | all-to-all | bytes 2097152 | tf_op jit(solution)/shard_map/all_to_all | solution.py:33
  59.4 0.1 convert_reduce_fusion
  59.5 0.1 multiply_convert_fusion.2
  59.6 0.1 broadcast_in_dim.9
  59.6 12.9 %all_to_all.36 = bf16[8,32,1024]{2,1,0:T(8,128)(2,1)S(1)} all-to-all(bf16[8,32,1024]{2,1,0:T(8,128)(2,1)S(1)} %broadcast_in_dim.9), channel_id=1, replica_groups=mesh['z'=16,'xl'=2,'core'=2,'xh'=2,'y'=4] {'xh','y'}, dimensions={0} | all-to-all | bytes 1048576 | tf_op jit(solution)/shard_map/all_to_all | solution.py:33
  72.6 1.7 convolution_convert_fusion.3
  74.2 27.8 %all_to_all.37 = bf16[16,16,512]{2,1,0:T(8,128)(2,1)S(1)} all-to-all(bf16[16,16,512]{2,1,0:T(8,128)(2,1)S(1)} %bitcast.46), channel_id=1, replica_groups=mesh['z'=16,'xl'=2,'core'=2,'xh'=2,'y'=4] {'z'}, dimensions={0} | all-to-all | bytes 524288 | tf_op jit(solution)/shard_map/all_to_all | solution.py:33
  102.1 22.7 %all_to_all.38 = bf16[16,16,512]{2,1,0:T(8,128)(2,1)} all-to-all(bf16[16,16,512]{2,1,0:T(8,128)(2,1)S(1)} %broadcast_in_dim.10), channel_id=1, replica_groups=mesh['z'=16,'xl'=2,'core'=2,'xh'=2,'y'=4] {'z'}, dimensions={0} | all-to-all | bytes 524288 | tf_op jit(solution)/shard_map/all_to_all | solution.py:33
  124.8 2.9 %convolution_convert_fusion.1 = bf16[256,1024]{1,0:T(8,128)(2,1)} fusion(bf16[256,512]{1,0:T(8,128)(2,1)} %bitcast.8, bf16[512,512]{1,0:T(8,128)(2,1)} %collective-permute-done.3, bf16[512,512]{1,0:T(8,128)(2,1)} %copy-done.3, pred[]{:T(512)S(6)} %eq.4), kind=kOutput, calls=%fused_computation.3 | convolution fusion | flops 273416192 | bytes 1835009 | tf_op jit(solution)/shard_map/dot_general | solution.py:106
  127.6 5.5 %all-to-all-start.5 = ((bf16[8,32,1024]{2,1,0:T(8,128)(2,1)}), bf16[8,32,1024]{2,1,0:T(8,128)(2,1)S(1)}, u32[]{:S(2)}, u32[]{:S(2)}) async-start(bf16[8,32,1024]{2,1,0:T(8,128)(2,1)} %bitcast.43), calls=%async_computation.5 | async-start | bytes 1048576 | tf_op jit(solution)/shard_map/all_to_all | solution.py:33
  133.1 8.5 %collective-permute-start.8 = (bf16[1,256,512]{2,1,0:T(8,128)(2,1)S(1)}, bf16[1,256,512]{2,1,0:T(8,128)(2,1)S(1)}, u32[]{:S(2)}, u32[]{:S(2)}) collective-permute-start(bf16[1,256,512]{2,1,0:T(8,128)(2,1)S(1)} %get-tuple-element.7), channel_id=1, source_target_pairs={{0,8},{8,0},{1,9},{9,1},{2,10},{10,2},{3,11},{11,3},{4,12},{12,4},... | collective-permute-start | bytes 786440 | tf_op jit(solution)/shard_map/ppermute | solution.py:63
  141.7 1.9 %collective-permute-start = (bf16[256,512]{1,0:T(8,128)(2,1)}, bf16[256,512]{1,0:T(8,128)(2,1)}, u32[]{:S(2)}, u32[]{:S(2)}) collective-permute-start(bf16[256,512]{1,0:T(8,128)(2,1)} %bitcast.41), channel_id=1, source_target_pairs={{0,16},{16,0},{1,17},{17,1},{2,18},{18,2},{3,19},{19,3},{4,20},{20... | collective-permute-start | bytes 786440 | tf_op jit(solution)/shard_map/ppermute | solution.py:50
  143.6 0.1 maximum_select_fusion.10
  143.7 3.4 %collective-permute-start.6 = (bf16[256,512]{1,0:T(8,128)(2,1)}, bf16[256,512]{1,0:T(8,128)(2,1)}, u32[]{:S(2)}, u32[]{:S(2)}) collective-permute-start(bf16[256,512]{1,0:T(8,128)(2,1)} %bitcast.8), channel_id=1, source_target_pairs={{0,16},{16,0},{1,17},{17,1},{2,18},{18,2},{3,19},{19,3},{4,20},{20... | collective-permute-start | bytes 786440 | tf_op jit(solution)/shard_map/ppermute | solution.py:50
  147.1 0.1 convert_reduce_fusion.1
  147.2 0.1 multiply_convert_fusion.1
  147.3 0.1 maximum_bitcast_fusion
  147.4 1.1 broadcast_in_dim.11
  148.5 8.0 %all-to-all-start.6 = ((bf16[32,32,512]{2,1,0:T(8,128)(2,1)}), bf16[32,32,512]{2,1,0:T(8,128)(2,1)}, u32[]{:S(2)}, u32[]{:S(2)}) async-start(bf16[32,32,512]{2,1,0:T(8,128)(2,1)} %bitcast.11), calls=%async_computation.6 | async-start | bytes 2097152 | tf_op jit(solution)/shard_map/all_to_all | solution.py:33
  156.6 3.3 %collective-permute-start.9 = (bf16[2,256,256]{2,1,0:T(8,128)(2,1)S(1)}, bf16[2,256,256]{2,1,0:T(8,128)(2,1)S(1)}, u32[]{:S(2)}, u32[]{:S(2)}) collective-permute-start(bf16[2,256,256]{2,1,0:T(8,128)(2,1)S(1)} %get-tuple-element.5), channel_id=1, source_target_pairs={{0,16},{16,0},{1,17},{17,1},{2,18},{18,2},{3,19},{19,3},{4,20},{20... | collective-permute-start | bytes 786440 | tf_op jit(solution)/shard_map/ppermute | solution.py:63
  159.9 1.3 maximum_select_fusion.9
  161.2 2.7 %collective-permute-start.7 = (bf16[512,512]{1,0:T(8,128)(2,1)S(1)}, bf16[512,512]{1,0:T(8,128)(2,1)S(1)}, u32[]{:S(2)}, u32[]{:S(2)}) collective-permute-start(bf16[512,512]{1,0:T(8,128)(2,1)S(1)} %maximum_select_fusion.9), channel_id=1, source_target_pairs={{0,8},{8,0},{1,9},{9,1},{2,10},{10,2},{3,11},{11,3},{4,12},{12,4},... | collective-permute-start | bytes 1572872 | tf_op jit(solution)/shard_map/ppermute | solution.py:50
  163.9 0.3 add_convert_fusion
  164.2 0.1 copy.12
  164.3 1.2 maximum_select_fusion.6
  165.5 1.9 %collective-permute-start.1 = (bf16[512,512]{1,0:T(8,128)(2,1)S(1)}, bf16[512,512]{1,0:T(8,128)(2,1)S(1)}, u32[]{:S(2)}, u32[]{:S(2)}) collective-permute-start(bf16[512,512]{1,0:T(8,128)(2,1)S(1)} %maximum_select_fusion.6), channel_id=1, source_target_pairs={{0,8},{8,0},{1,9},{9,1},{2,10},{10,2},{3,11},{11,3},{4,12},{12,4},... | collective-permute-start | bytes 1572872 | tf_op jit(solution)/shard_map/ppermute | solution.py:50
  167.4 8.2 %collective-permute-done.9 = bf16[2,256,256]{2,1,0:T(8,128)(2,1)S(1)} collective-permute-done((bf16[2,256,256]{2,1,0:T(8,128)(2,1)S(1)}, bf16[2,256,256]{2,1,0:T(8,128)(2,1)S(1)}, u32[]{:S(2)}, u32[]{:S(2)}) %collective-permute-start.9) | collective-permute-done | bytes 262176 | tf_op jit(solution)/shard_map/ppermute | solution.py:63
  175.6 0.2 maximum_select_fusion.11
  175.8 0.5 fusion.13
  176.3 2.3 %convolution_multiply_fusion = f32[256,512]{1,0:T(8,128)} fusion(bf16[1024,512]{1,0:T(8,128)(2,1)S(1)} %bitcast.39, bf16[1024,512]{1,0:T(8,128)(2,1)} %bitcast.12), kind=kOutput, calls=%fused_computation.5 | convolution fusion | flops 268566528 | bytes 2097152 | tf_op jit(solution)/shard_map/dot_general | solution.py:21
  178.6 2.3 %fusion = f32[512,256]{1,0:T(8,128)} fusion(f32[512,256]{1,0:T(8,128)S(1)} %fusion.13, bf16[512,512]{1,0:T(8,128)(2,1)S(1)} %collective-permute-done.1, bf16[512,512]{1,0:T(8,128)(2,1)S(1)} %maximum_select_fusion.6, pred[]{:T(512)S(6)} %eq.4, bf16[1024,512]{1,0:T(8,128)(2,1)} %bitcast.12), kind=kOutput, calls=%fused_computation.7 | convolution fusion | flops 273416192 | bytes 2621441 | tf_op jit(solution)/shard_map/dot_general | solution.py:21
  (24 shorter events, 0.3 us)
Async XLA Ops:
  0.6 34.7 %copy-start = (s32[1024,512]{1,0:T(8,128)S(1)}, s32[1024,512]{1,0:T(8,128)}, u32[]{:S(2)}) copy-start(s32[1024,512]{1,0:T(8,128)} %param.5) | copy-start | bytes 6291460
  0.6 22.7 %collective-permute-start.4 = (bf16[256,512]{1,0:T(8,128)(2,1)}, bf16[256,512]{1,0:T(8,128)(2,1)S(1)}, u32[]{:S(2)}, u32[]{:S(2)}) collective-permute-start(bf16[256,512]{1,0:T(8,128)(2,1)} %param.7), channel_id=1, source_target_pairs={{0,16},{16,0},{1,17},{17,1},{2,18},{18,2},{3,19},{19,3},{4,20},{20... | collective-permute-start | bytes 786440 | tf_op jit(solution)/shard_map/ppermute | solution.py:50
  6.2 31.8 %all-to-all-start = ((bf16[16,16,512]{2,1,0:T(8,128)(2,1)}), bf16[16,16,512]{2,1,0:T(8,128)(2,1)S(1)}, u32[]{:S(2)}, u32[]{:S(2)}) async-start(bf16[16,16,512]{2,1,0:T(8,128)(2,1)} %broadcast_in_dim.8), calls=%async_computation | async-start | bytes 524288 | tf_op jit(solution)/shard_map/all_to_all | solution.py:33
  21.1 8.8 %collective-permute-start.2 = (bf16[512,256]{1,0:T(8,128)(2,1)}, bf16[512,256]{1,0:T(8,128)(2,1)}, u32[]{:S(2)}, u32[]{:S(2)}) collective-permute-start(bf16[512,256]{1,0:T(8,128)(2,1)} %param.6), channel_id=1, source_target_pairs={{0,16},{16,0},{1,17},{17,1},{2,18},{18,2},{3,19},{19,3},{4,20},{20... | collective-permute-start | bytes 786440 | tf_op jit(solution)/shard_map/ppermute | solution.py:50
  24.5 10.9 %collective-permute-start.5 = (bf16[512,512]{1,0:T(8,128)(2,1)S(1)}, bf16[512,512]{1,0:T(8,128)(2,1)}, u32[]{:S(2)}, u32[]{:S(2)}) collective-permute-start(bf16[512,512]{1,0:T(8,128)(2,1)S(1)} %maximum_select_fusion.8), channel_id=1, source_target_pairs={{0,8},{8,0},{1,9},{9,1},{2,10},{10,2},{3,11},{11,3},{4,12},{12,4},... | collective-permute-start | bytes 1572872 | tf_op jit(solution)/shard_map/ppermute | solution.py:50
  31.2 41.3 %copy-start.3 = (bf16[512,512]{1,0:T(8,128)(2,1)}, bf16[512,512]{1,0:T(8,128)(2,1)S(1)}, u32[]{:S(2)}) copy-start(bf16[512,512]{1,0:T(8,128)(2,1)S(1)} %maximum_select_fusion.7) | copy-start | bytes 1572868
  31.2 6.8 %collective-permute-start.3 = (bf16[512,512]{1,0:T(8,128)(2,1)S(1)}, bf16[512,512]{1,0:T(8,128)(2,1)}, u32[]{:S(2)}, u32[]{:S(2)}) collective-permute-start(bf16[512,512]{1,0:T(8,128)(2,1)S(1)} %maximum_select_fusion.7), channel_id=1, source_target_pairs={{0,8},{8,0},{1,9},{9,1},{2,10},{10,2},{3,11},{11,3},{4,12},{12,4},... | collective-permute-start | bytes 1572872 | tf_op jit(solution)/shard_map/ppermute | solution.py:50
  38.0 1.8 copy-start.1
  38.0 1.8 copy-start.4
  127.6 19.5 %all-to-all-start.5 = ((bf16[8,32,1024]{2,1,0:T(8,128)(2,1)}), bf16[8,32,1024]{2,1,0:T(8,128)(2,1)S(1)}, u32[]{:S(2)}, u32[]{:S(2)}) async-start(bf16[8,32,1024]{2,1,0:T(8,128)(2,1)} %bitcast.43), calls=%async_computation.5 | async-start | bytes 1048576 | tf_op jit(solution)/shard_map/all_to_all | solution.py:33
  133.1 10.5 %collective-permute-start.8 = (bf16[1,256,512]{2,1,0:T(8,128)(2,1)S(1)}, bf16[1,256,512]{2,1,0:T(8,128)(2,1)S(1)}, u32[]{:S(2)}, u32[]{:S(2)}) collective-permute-start(bf16[1,256,512]{2,1,0:T(8,128)(2,1)S(1)} %get-tuple-element.7), channel_id=1, source_target_pairs={{0,8},{8,0},{1,9},{9,1},{2,10},{10,2},{3,11},{11,3},{4,12},{12,4},... | collective-permute-start | bytes 786440 | tf_op jit(solution)/shard_map/ppermute | solution.py:63
  141.7 22.6 %collective-permute-start = (bf16[256,512]{1,0:T(8,128)(2,1)}, bf16[256,512]{1,0:T(8,128)(2,1)}, u32[]{:S(2)}, u32[]{:S(2)}) collective-permute-start(bf16[256,512]{1,0:T(8,128)(2,1)} %bitcast.41), channel_id=1, source_target_pairs={{0,16},{16,0},{1,17},{17,1},{2,18},{18,2},{3,19},{19,3},{4,20},{20... | collective-permute-start | bytes 786440 | tf_op jit(solution)/shard_map/ppermute | solution.py:50
  143.7 16.2 %collective-permute-start.6 = (bf16[256,512]{1,0:T(8,128)(2,1)}, bf16[256,512]{1,0:T(8,128)(2,1)}, u32[]{:S(2)}, u32[]{:S(2)}) collective-permute-start(bf16[256,512]{1,0:T(8,128)(2,1)} %bitcast.8), channel_id=1, source_target_pairs={{0,16},{16,0},{1,17},{17,1},{2,18},{18,2},{3,19},{19,3},{4,20},{20... | collective-permute-start | bytes 786440 | tf_op jit(solution)/shard_map/ppermute | solution.py:50
  148.5 27.8 %all-to-all-start.6 = ((bf16[32,32,512]{2,1,0:T(8,128)(2,1)}), bf16[32,32,512]{2,1,0:T(8,128)(2,1)}, u32[]{:S(2)}, u32[]{:S(2)}) async-start(bf16[32,32,512]{2,1,0:T(8,128)(2,1)} %bitcast.11), calls=%async_computation.6 | async-start | bytes 2097152 | tf_op jit(solution)/shard_map/all_to_all | solution.py:33
  156.6 19.0 %collective-permute-start.9 = (bf16[2,256,256]{2,1,0:T(8,128)(2,1)S(1)}, bf16[2,256,256]{2,1,0:T(8,128)(2,1)S(1)}, u32[]{:S(2)}, u32[]{:S(2)}) collective-permute-start(bf16[2,256,256]{2,1,0:T(8,128)(2,1)S(1)} %get-tuple-element.5), channel_id=1, source_target_pairs={{0,16},{16,0},{1,17},{17,1},{2,18},{18,2},{3,19},{19,3},{4,20},{20... | collective-permute-start | bytes 786440 | tf_op jit(solution)/shard_map/ppermute | solution.py:63
  161.2 3.1 %copy-start.2 = (bf16[16,16,512]{2,1,0:T(8,128)(2,1)S(1)}, bf16[16,16,512]{2,1,0:T(8,128)(2,1)}, u32[]{:S(2)}) copy-start(bf16[16,16,512]{2,1,0:T(8,128)(2,1)} %copy-done.1) | copy-start | bytes 786436
  161.2 14.6 %collective-permute-start.7 = (bf16[512,512]{1,0:T(8,128)(2,1)S(1)}, bf16[512,512]{1,0:T(8,128)(2,1)S(1)}, u32[]{:S(2)}, u32[]{:S(2)}) collective-permute-start(bf16[512,512]{1,0:T(8,128)(2,1)S(1)} %maximum_select_fusion.9), channel_id=1, source_target_pairs={{0,8},{8,0},{1,9},{9,1},{2,10},{10,2},{3,11},{11,3},{4,12},{12,4},... | collective-permute-start | bytes 1572872 | tf_op jit(solution)/shard_map/ppermute | solution.py:50
  165.5 13.1 %collective-permute-start.1 = (bf16[512,512]{1,0:T(8,128)(2,1)S(1)}, bf16[512,512]{1,0:T(8,128)(2,1)S(1)}, u32[]{:S(2)}, u32[]{:S(2)}) collective-permute-start(bf16[512,512]{1,0:T(8,128)(2,1)S(1)} %maximum_select_fusion.6), channel_id=1, source_target_pairs={{0,8},{8,0},{1,9},{9,1},{2,10},{10,2},{3,11},{11,3},{4,12},{12,4},... | collective-permute-start | bytes 1572872 | tf_op jit(solution)/shard_map/ppermute | solution.py:50

commit v5 on v4

--- a/solution.py
+++ b/solution.py
@@ -70,6 +70,10 @@
     )
 
 
+def beside(chain, operand):
+    return lax.optimization_barrier((chain, operand))
+
+
 def on_device(tokens, probe_draw, w_in, w_out):
     total_rows = probe_draw.shape[0]
     own_rows, feats = tokens.shape
@@ -91,20 +95,27 @@
     own_sign = (2 * own_draw - 1).astype(BF).reshape(nz * own_rows, feats)
     signal_part = contract_cols(own_sign, w_out_all)
     own_tokens = gather(tokens, "z", nz)
-    all_tokens = pair_up(pair_up(own_tokens, "xl", 0), "core", 0)
+    token_pair = pair_up(own_tokens, "xl", 0)
     hidden_part = jnp.dot(own_tokens, w_in_all, preferred_element_type=F32)
     both = scatter_sum(
         jnp.concatenate([hidden_part, signal_part], axis=1), COL, nc
     )
+    both, token_pair = beside(both, token_pair)
     slopes, bending, gated_own = local_terms(both[:, :wide], both[:, wide:])
     gated = gather(gated_own, COL, nc)
-    gated_hid = hand_over(hand_over(gated[None], "core", 0), "xl", 1)
-    gated_hid = gated_hid.reshape(total_rows, hid)
+    all_tokens = pair_up(token_pair, "core", 0)
+    gated, all_tokens = beside(gated, all_tokens)
+    gated_pair = hand_over(gated[None], "core", 0)
     jac_own = scatter_sum(contract_cols(gated, w_in_all), "z", nz).astype(BF)
+    jac_own, gated_pair = beside(jac_own, gated_pair)
+    gated_hid = hand_over(gated_pair, "xl", 1).reshape(total_rows, hid)
     jac_rows = gather(jac_own, "z", nz)
-    jac_all = pair_up(pair_up(jac_rows, "xl", 0), "core", 0)
+    jac_rows, gated_hid = beside(jac_rows, gated_hid)
+    jac_pair = pair_up(jac_rows, "xl", 0)
     back_part = jnp.dot(jac_rows, w_in_all, preferred_element_type=F32)
     back_proj = scatter_sum(back_part, COL, nc)
+    back_proj, jac_pair = beside(back_proj, jac_pair)
+    jac_all = pair_up(jac_pair, "core", 0)
     rows = back_proj.shape[0]
     curv_own = (back_proj * bending).astype(BF).reshape(rows, nn, hid)
     slope_own = (back_proj * slopes).astype(BF).reshape(rows, nn, hid)

time: 182 us -> 199 us (1.093)
  the two profiles are of different devices: /device:TPU:1 before, /device:TPU:32 now
where the time goes in v5:
time: 199 us; the launch traced here: 197 us
  waiting for transfers between devices  84 us (42%)
  starting transfers between devices  81.7 us (41%)
  matrix products  16.1 us (8%)
  other arithmetic  10.2 us (5%)
  local copies, waits for them, and re-layouts  4.33 us (2%)
    all_to_all x7, starting transfers between devices, exchange(): return lax.all_to_all(blocks, axes, 0, 0, tiled=True)  59.2 us
    all_to_all x7, waiting for transfers between devices, exchange(): return lax.all_to_all(blocks, axes, 0, 0, tiled=True)  49 us
    ppermute x8, waiting for transfers between devices, pair_up(): far = lax.ppermute(array, name, [(0, 1), (1, 0)])  27.5 us
    ppermute x8, starting transfers between devices, pair_up(): far = lax.ppermute(array, name, [(0, 1), (1, 0)])  18.4 us
    ppermute x2, waiting for transfers between devices, hand_over(): far = lax.ppermute(jnp.where(first, right, left), name, [(0, 1), (1, 0)])  7.49 us
    select_n x5, other arithmetic, pair_up(): jnp.where(lax.axis_index(name) == 0, jnp.concatenate([array, far], axis=a...  7.13 us
    dot_general x3, matrix products, contract_rows(): lax.dot_general(left, right, (((0,), (0,)), ((), ())), preferred_element_...  6.35 us
    dot_general x2, matrix products, contract_cols(): lax.dot_general(left, right, (((1,), (1,)), ((), ())), preferred_element_...  5.25 us
  transfers between devices with their start and end apart: 17, of which 10 were waited for; matrix products, arithmetic and copies ran while one was open for 9% of the time, Pallas kernels for 0%

profile of v5, /device:TPU:32, one launch (start us, length us, event | category | flops | bytes accessed | tf_op | source)
XLA Modules:
  0.0 197.3 jit_solution(12390225590925267402)
XLA Ops:
  0.6 3.5 %collective-permute-start.2 = (bf16[256,512]{1,0:T(8,128)(2,1)}, bf16[256,512]{1,0:T(8,128)(2,1)S(1)}, u32[]{:S(2)}, u32[]{:S(2)}) collective-permute-start(bf16[256,512]{1,0:T(8,128)(2,1)} %param.7), channel_id=1, source_target_pairs={{0,16},{16,0},{1,17},{17,1},{2,18},{18,2},{3,19},{19,3},{4,20},{20... | collective-permute-start | bytes 786440 | tf_op jit(solution)/shard_map/ppermute | solution.py:50
  4.2 1.4 broadcast_in_dim.10
  5.6 15.2 %all-to-all-start = ((bf16[16,16,512]{2,1,0:T(8,128)(2,1)}), bf16[16,16,512]{2,1,0:T(8,128)(2,1)S(1)}, u32[]{:S(2)}, u32[]{:S(2)}) async-start(bf16[16,16,512]{2,1,0:T(8,128)(2,1)} %broadcast_in_dim.10), calls=%async_computation | async-start | bytes 524288 | tf_op jit(solution)/shard_map/all_to_all | solution.py:33
  20.8 2.4 %collective-permute-start = (bf16[512,256]{1,0:T(8,128)(2,1)}, bf16[512,256]{1,0:T(8,128)(2,1)}, u32[]{:S(2)}, u32[]{:S(2)}) collective-permute-start(bf16[512,256]{1,0:T(8,128)(2,1)} %param.6), channel_id=1, source_target_pairs={{0,16},{16,0},{1,17},{17,1},{2,18},{18,2},{3,19},{19,3},{4,20},{20... | collective-permute-start | bytes 786440 | tf_op jit(solution)/shard_map/ppermute | solution.py:50
  23.3 1.2 maximum_select_fusion.6
  24.5 1.9 collective-permute-start.3
  26.4 3.8 %collective-permute-done = bf16[512,256]{1,0:T(8,128)(2,1)} collective-permute-done((bf16[512,256]{1,0:T(8,128)(2,1)}, bf16[512,256]{1,0:T(8,128)(2,1)}, u32[]{:S(2)}, u32[]{:S(2)}) %collective-permute-start) | collective-permute-done | bytes 262176 | tf_op jit(solution)/shard_map/ppermute | solution.py:50
  30.2 1.3 maximum_select_fusion.5
  31.6 1.9 collective-permute-start.1
  33.6 2.6 %convolution_convert_fusion.2 = bf16[8,32,1024]{2,1,0:T(8,128)(2,1)} fusion(bf16[8,32,512]{2,1,0:T(8,128)(2,1)S(1)} %bitcast.50, bf16[512,512]{1,0:T(8,128)(2,1)} %collective-permute-done.3, bf16[512,512]{1,0:T(8,128)(2,1)S(1)} %maximum_select_fusion.6, pred[]{:T(512)S(6)} %eq.4), kind=kOutput, calls=%fused_computation.4 | convolution fusion | flops 273416192 | bytes 1835009 | tf_op jit(solution)/shard_map/dot_general | solution.py:27
  36.2 2.5 %all-to-all-done = bf16[16,16,512]{2,1,0:T(8,128)(2,1)S(1)} async-done(((bf16[16,16,512]{2,1,0:T(8,128)(2,1)}), bf16[16,16,512]{2,1,0:T(8,128)(2,1)S(1)}, u32[]{:S(2)}, u32[]{:S(2)}) %all-to-all-start) | async-done | bytes 262176 | tf_op jit(solution)/shard_map/all_to_all | solution.py:33
  38.7 1.7 convolution_convert_fusion
  40.4 1.1 pad_maximum_fusion
  41.5 6.6 %all-to-all-start.1 = ((bf16[8,32,2048]{2,1,0:T(8,128)(2,1)}), bf16[8,32,2048]{2,1,0:T(8,128)(2,1)S(1)}, u32[]{:S(2)}, u32[]{:S(2)}) async-start(bf16[8,32,2048]{2,1,0:T(8,128)(2,1)} %pad_maximum_fusion), calls=%async_computation.1 | async-start | bytes 2097152 | tf_op jit(solution)/shard_map/all_to_all | solution.py:33
  48.1 2.1 %collective-permute-start.4 = (bf16[256,512]{1,0:T(8,128)(2,1)S(1)}, bf16[256,512]{1,0:T(8,128)(2,1)S(1)}, u32[]{:S(2)}, u32[]{:S(2)}) collective-permute-start(bf16[256,512]{1,0:T(8,128)(2,1)S(1)} %bitcast.42), channel_id=1, source_target_pairs={{0,16},{16,0},{1,17},{17,1},{2,18},{18,2},{3,19},{19,3},{4,20},{20... | collective-permute-start | bytes 786440 | tf_op jit(solution)/shard_map/ppermute | solution.py:50
  50.3 14.4 %collective-permute-done.4 = bf16[256,512]{1,0:T(8,128)(2,1)S(1)} collective-permute-done((bf16[256,512]{1,0:T(8,128)(2,1)S(1)}, bf16[256,512]{1,0:T(8,128)(2,1)S(1)}, u32[]{:S(2)}, u32[]{:S(2)}) %collective-permute-start.4) | collective-permute-done | bytes 262176 | tf_op jit(solution)/shard_map/ppermute | solution.py:50
  64.7 1.0 maximum_select_fusion.7
  65.7 0.1 convert_reduce_fusion
  65.8 2.1 %collective-permute-start.5 = (bf16[512,512]{1,0:T(8,128)(2,1)}, bf16[512,512]{1,0:T(8,128)(2,1)}, u32[]{:S(2)}, u32[]{:S(2)}) collective-permute-start(bf16[512,512]{1,0:T(8,128)(2,1)} %maximum_select_fusion.7), channel_id=1, source_target_pairs={{0,8},{8,0},{1,9},{9,1},{2,10},{10,2},{3,11},{11,3},{4,12},{12,4},... | collective-permute-start | bytes 1572872 | tf_op jit(solution)/shard_map/ppermute | solution.py:50
  68.0 0.9 broadcast_in_dim.11
  68.8 8.0 %all-to-all-start.2 = ((bf16[8,32,1024]{2,1,0:T(8,128)(2,1)}), bf16[8,32,1024]{2,1,0:T(8,128)(2,1)S(1)}, u32[]{:S(2)}, u32[]{:S(2)}) async-start(bf16[8,32,1024]{2,1,0:T(8,128)(2,1)} %broadcast_in_dim.11), calls=%async_computation.2 | async-start | bytes 1048576 | tf_op jit(solution)/shard_map/all_to_all | solution.py:33
  76.8 2.6 %maximum_select_fusion.2 = bf16[1024,512]{1,0:T(8,128)(2,1)} fusion(bf16[512,512]{1,0:T(8,128)(2,1)} %collective-permute-done.5, bf16[512,512]{1,0:T(8,128)(2,1)S(1)} %copy-done.1, pred[]{:T(512)S(6)} %eq.4), kind=kLoop, calls=%fused_computation.18 | loop fusion | flops 4718592 | bytes 2097153 | tf_op jit(solution)/shard_map/jit(_where)/select_n | solution.py:51
  79.4 8.9 %all-to-all-done.2 = bf16[8,32,1024]{2,1,0:T(8,128)(2,1)S(1)} async-done(((bf16[8,32,1024]{2,1,0:T(8,128)(2,1)}), bf16[8,32,1024]{2,1,0:T(8,128)(2,1)S(1)}, u32[]{:S(2)}, u32[]{:S(2)}) %all-to-all-start.2) | async-done | bytes 524320 | tf_op jit(solution)/shard_map/all_to_all | solution.py:33
  88.3 2.7 %convolution_convert_fusion.3 = bf16[256,512]{1,0:T(8,128)(2,1)} fusion(bf16[256,1024]{1,0:T(8,128)(2,1)S(1)} %bitcast.38, bf16[512,512]{1,0:T(8,128)(2,1)} %collective-permute-done.1, bf16[512,512]{1,0:T(8,128)(2,1)} %copy-done.3, pred[]{:T(512)S(6)} %eq.4), kind=kOutput, calls=%fused_computation.8 | convolution fusion | flops 273285120 | bytes 1835009 | tf_op jit(solution)/shard_map/dot_general | solution.py:27
  91.0 11.2 %all-to-all-start.3 = ((bf16[16,16,512]{2,1,0:T(8,128)(2,1)}), bf16[16,16,512]{2,1,0:T(8,128)(2,1)S(1)}, u32[]{:S(2)}, u32[]{:S(2)}) async-start(bf16[16,16,512]{2,1,0:T(8,128)(2,1)} %bitcast.7), calls=%async_computation.3 | async-start | bytes 524288 | tf_op jit(solution)/shard_map/all_to_all | solution.py:33
  102.3 1.9 collective-permute-start.6
  104.2 1.5 collective-permute-done.6
  105.7 0.1 maximum_select_fusion.8
  105.8 14.0 %all-to-all-done.3 = bf16[16,16,512]{2,1,0:T(8,128)(2,1)S(1)} async-done(((bf16[16,16,512]{2,1,0:T(8,128)(2,1)}), bf16[16,16,512]{2,1,0:T(8,128)(2,1)S(1)}, u32[]{:S(2)}, u32[]{:S(2)}) %all-to-all-start.3) | async-done | bytes 262176 | tf_op jit(solution)/shard_map/all_to_all | solution.py:33
  119.8 0.7 broadcast_in_dim.13
  120.5 5.5 %all-to-all-start.4 = ((bf16[16,16,512]{2,1,0:T(8,128)(2,1)}), bf16[16,16,512]{2,1,0:T(8,128)(2,1)S(1)}, u32[]{:S(2)}, u32[]{:S(2)}) async-start(bf16[16,16,512]{2,1,0:T(8,128)(2,1)} %broadcast_in_dim.13), calls=%async_computation.4 | async-start | bytes 524288 | tf_op jit(solution)/shard_map/all_to_all | solution.py:33
  126.1 2.3 %collective-permute-start.7 = (bf16[2,256,256]{2,1,0:T(8,128)(2,1)S(1)}, bf16[2,256,256]{2,1,0:T(8,128)(2,1)S(1)}, u32[]{:S(2)}, u32[]{:S(2)}) collective-permute-start(bf16[2,256,256]{2,1,0:T(8,128)(2,1)S(1)} %get-tuple-element.25), channel_id=1, source_target_pairs={{0,16},{16,0},{1,17},{17,1},{2,18},{18,2},{3,19},{19,3},{4,20},{20... | collective-permute-start | bytes 786440 | tf_op jit(solution)/shard_map/ppermute | solution.py:63
  128.3 6.0 %collective-permute-done.7 = bf16[2,256,256]{2,1,0:T(8,128)(2,1)S(1)} collective-permute-done((bf16[2,256,256]{2,1,0:T(8,128)(2,1)S(1)}, bf16[2,256,256]{2,1,0:T(8,128)(2,1)S(1)}, u32[]{:S(2)}, u32[]{:S(2)}) %collective-permute-start.7) | collective-permute-done | bytes 262176 | tf_op jit(solution)/shard_map/ppermute | solution.py:63
  134.3 1.0 maximum_select_fusion.9
  135.3 8.4 %all-to-all-done.4 = bf16[16,16,512]{2,1,0:T(8,128)(2,1)S(1)} async-done(((bf16[16,16,512]{2,1,0:T(8,128)(2,1)}), bf16[16,16,512]{2,1,0:T(8,128)(2,1)S(1)}, u32[]{:S(2)}, u32[]{:S(2)}) %all-to-all-start.4) | async-done | bytes 262176 | tf_op jit(solution)/shard_map/all_to_all | solution.py:33
  143.8 2.8 %convolution_convert_fusion.1 = bf16[256,1024]{1,0:T(8,128)(2,1)} fusion(bf16[256,512]{1,0:T(8,128)(2,1)S(1)} %bitcast.44, bf16[512,512]{1,0:T(8,128)(2,1)} %collective-permute-done.1, bf16[512,512]{1,0:T(8,128)(2,1)} %copy-done.3, pred[]{:T(512)S(6)} %eq.4), kind=kOutput, calls=%fused_computation.3 | convolution fusion | flops 273416192 | bytes 1835009 | tf_op jit(solution)/shard_map/dot_general | solution.py:115
  146.6 4.6 %all-to-all-start.5 = ((bf16[8,32,1024]{2,1,0:T(8,128)(2,1)}), bf16[8,32,1024]{2,1,0:T(8,128)(2,1)S(1)}, u32[]{:S(2)}, u32[]{:S(2)}) async-start(bf16[8,32,1024]{2,1,0:T(8,128)(2,1)} %bitcast.47), calls=%async_computation.5 | async-start | bytes 1048576 | tf_op jit(solution)/shard_map/all_to_all | solution.py:33
  151.2 2.3 %collective-permute-start.8 = (bf16[256,512]{1,0:T(8,128)(2,1)S(1)}, bf16[256,512]{1,0:T(8,128)(2,1)S(1)}, u32[]{:S(2)}, u32[]{:S(2)}) collective-permute-start(bf16[256,512]{1,0:T(8,128)(2,1)S(1)} %bitcast.45), channel_id=1, source_target_pairs={{0,16},{16,0},{1,17},{17,1},{2,18},{18,2},{3,19},{19,3},{4,20},{20... | collective-permute-start | bytes 786440 | tf_op jit(solution)/shard_map/ppermute | solution.py:50
  153.4 9.3 %collective-permute-done.8 = bf16[256,512]{1,0:T(8,128)(2,1)S(1)} collective-permute-done((bf16[256,512]{1,0:T(8,128)(2,1)S(1)}, bf16[256,512]{1,0:T(8,128)(2,1)S(1)}, u32[]{:S(2)}, u32[]{:S(2)}) %collective-permute-start.8) | collective-permute-done | bytes 262176 | tf_op jit(solution)/shard_map/ppermute | solution.py:50
  162.8 1.0 maximum_select_fusion.10
  164.1 1.1 broadcast_in_dim.14
  165.2 8.1 %all-to-all-start.6 = ((bf16[32,32,512]{2,1,0:T(8,128)(2,1)}), bf16[32,32,512]{2,1,0:T(8,128)(2,1)}, u32[]{:S(2)}, u32[]{:S(2)}) async-start(bf16[32,32,512]{2,1,0:T(8,128)(2,1)} %bitcast.13), calls=%async_computation.6 | async-start | bytes 2097152 | tf_op jit(solution)/shard_map/all_to_all | solution.py:33
  173.3 0.3 add_convert_fusion
  173.7 2.1 %collective-permute-start.9 = (bf16[512,512]{1,0:T(8,128)(2,1)}, bf16[512,512]{1,0:T(8,128)(2,1)S(1)}, u32[]{:S(2)}, u32[]{:S(2)}) collective-permute-start(bf16[512,512]{1,0:T(8,128)(2,1)} %maximum_select_fusion.10), channel_id=1, source_target_pairs={{0,8},{8,0},{1,9},{9,1},{2,10},{10,2},{3,11},{11,3},{4,12},{12,4},... | collective-permute-start | bytes 1572872 | tf_op jit(solution)/shard_map/ppermute | solution.py:50
  175.8 15.2 %all-to-all-done.6 = bf16[32,32,512]{2,1,0:T(8,128)(2,1)} async-done(((bf16[32,32,512]{2,1,0:T(8,128)(2,1)}), bf16[32,32,512]{2,1,0:T(8,128)(2,1)}, u32[]{:S(2)}, u32[]{:S(2)}) %all-to-all-start.6) | async-done | bytes 1048608 | tf_op jit(solution)/shard_map/all_to_all | solution.py:33
  191.0 1.6 fusion.16
  192.6 2.3 %convolution_multiply_fusion = f32[256,512]{1,0:T(8,128)} fusion(bf16[1024,512]{1,0:T(8,128)(2,1)S(1)} %bitcast.40, bf16[1024,512]{1,0:T(8,128)(2,1)} %bitcast.14), kind=kOutput, calls=%fused_computation.5 | convolution fusion | flops 268566528 | bytes 2097152 | tf_op jit(solution)/shard_map/dot_general | solution.py:21
  194.9 2.5 %fusion = f32[512,256]{1,0:T(8,128)} fusion(f32[512,256]{1,0:T(8,128)S(1)} %fusion.16, bf16[1024,256]{1,0:T(8,128)(2,1)S(1)} %bitcast.48, bf16[512,512]{1,0:T(8,128)(2,1)S(1)} %collective-permute-done.9, bf16[512,512]{1,0:T(8,128)(2,1)} %maximum_select_fusion.10, pred[]{:T(512)S(6)} %eq.4), kind=kOutput, calls=%fused_computation.7 | convolution fusion | flops 273416192 | bytes 2621441 | tf_op jit(solution)/shard_map/dot_general | solution.py:21
  (31 shorter events, 0.7 us)
Async XLA Ops:
  0.6 32.9 %copy-start = (s32[1024,512]{1,0:T(8,128)S(1)}, s32[1024,512]{1,0:T(8,128)}, u32[]{:S(2)}) copy-start(s32[1024,512]{1,0:T(8,128)} %param.5) | copy-start | bytes 6291460
  0.6 22.7 %collective-permute-start.2 = (bf16[256,512]{1,0:T(8,128)(2,1)}, bf16[256,512]{1,0:T(8,128)(2,1)S(1)}, u32[]{:S(2)}, u32[]{:S(2)}) collective-permute-start(bf16[256,512]{1,0:T(8,128)(2,1)} %param.7), channel_id=1, source_target_pairs={{0,16},{16,0},{1,17},{17,1},{2,18},{18,2},{3,19},{19,3},{4,20},{20... | collective-permute-start | bytes 786440 | tf_op jit(solution)/shard_map/ppermute | solution.py:50
  5.6 33.0 %all-to-all-start = ((bf16[16,16,512]{2,1,0:T(8,128)(2,1)}), bf16[16,16,512]{2,1,0:T(8,128)(2,1)S(1)}, u32[]{:S(2)}, u32[]{:S(2)}) async-start(bf16[16,16,512]{2,1,0:T(8,128)(2,1)} %broadcast_in_dim.10), calls=%async_computation | async-start | bytes 524288 | tf_op jit(solution)/shard_map/all_to_all | solution.py:33
  20.8 9.4 %collective-permute-start = (bf16[512,256]{1,0:T(8,128)(2,1)}, bf16[512,256]{1,0:T(8,128)(2,1)}, u32[]{:S(2)}, u32[]{:S(2)}) collective-permute-start(bf16[512,256]{1,0:T(8,128)(2,1)} %param.6), channel_id=1, source_target_pairs={{0,16},{16,0},{1,17},{17,1},{2,18},{18,2},{3,19},{19,3},{4,20},{20... | collective-permute-start | bytes 786440 | tf_op jit(solution)/shard_map/ppermute | solution.py:50
  24.5 9.1 %collective-permute-start.3 = (bf16[512,512]{1,0:T(8,128)(2,1)S(1)}, bf16[512,512]{1,0:T(8,128)(2,1)}, u32[]{:S(2)}, u32[]{:S(2)}) collective-permute-start(bf16[512,512]{1,0:T(8,128)(2,1)S(1)} %maximum_select_fusion.6), channel_id=1, source_target_pairs={{0,8},{8,0},{1,9},{9,1},{2,10},{10,2},{3,11},{11,3},{4,12},{12,4},... | collective-permute-start | bytes 1572872 | tf_op jit(solution)/shard_map/ppermute | solution.py:50
  31.6 9.9 %copy-start.3 = (bf16[512,512]{1,0:T(8,128)(2,1)}, bf16[512,512]{1,0:T(8,128)(2,1)S(1)}, u32[]{:S(2)}) copy-start(bf16[512,512]{1,0:T(8,128)(2,1)S(1)} %maximum_select_fusion.5) | copy-start | bytes 1572868
  31.6 4.6 %collective-permute-start.1 = (bf16[512,512]{1,0:T(8,128)(2,1)S(1)}, bf16[512,512]{1,0:T(8,128)(2,1)}, u32[]{:S(2)}, u32[]{:S(2)}) collective-permute-start(bf16[512,512]{1,0:T(8,128)(2,1)S(1)} %maximum_select_fusion.5), channel_id=1, source_target_pairs={{0,8},{8,0},{1,9},{9,1},{2,10},{10,2},{3,11},{11,3},{4,12},{12,4},... | collective-permute-start | bytes 1572872 | tf_op jit(solution)/shard_map/ppermute | solution.py:50
  38.7 1.7 copy-start.5
  41.5 24.2 %all-to-all-start.1 = ((bf16[8,32,2048]{2,1,0:T(8,128)(2,1)}), bf16[8,32,2048]{2,1,0:T(8,128)(2,1)S(1)}, u32[]{:S(2)}, u32[]{:S(2)}) async-start(bf16[8,32,2048]{2,1,0:T(8,128)(2,1)} %pad_maximum_fusion), calls=%async_computation.1 | async-start | bytes 2097152 | tf_op jit(solution)/shard_map/all_to_all | solution.py:33
  48.1 16.5 %collective-permute-start.4 = (bf16[256,512]{1,0:T(8,128)(2,1)S(1)}, bf16[256,512]{1,0:T(8,128)(2,1)S(1)}, u32[]{:S(2)}, u32[]{:S(2)}) collective-permute-start(bf16[256,512]{1,0:T(8,128)(2,1)S(1)} %bitcast.42), channel_id=1, source_target_pairs={{0,16},{16,0},{1,17},{17,1},{2,18},{18,2},{3,19},{19,3},{4,20},{20... | collective-permute-start | bytes 786440 | tf_op jit(solution)/shard_map/ppermute | solution.py:50
  65.8 11.0 %copy-start.1 = (bf16[512,512]{1,0:T(8,128)(2,1)S(1)}, bf16[512,512]{1,0:T(8,128)(2,1)}, u32[]{:S(2)}) copy-start(bf16[512,512]{1,0:T(8,128)(2,1)} %maximum_select_fusion.7) | copy-start | bytes 1572868
  65.8 10.9 %collective-permute-start.5 = (bf16[512,512]{1,0:T(8,128)(2,1)}, bf16[512,512]{1,0:T(8,128)(2,1)}, u32[]{:S(2)}, u32[]{:S(2)}) collective-permute-start(bf16[512,512]{1,0:T(8,128)(2,1)} %maximum_select_fusion.7), channel_id=1, source_target_pairs={{0,8},{8,0},{1,9},{9,1},{2,10},{10,2},{3,11},{11,3},{4,12},{12,4},... | collective-permute-start | bytes 1572872 | tf_op jit(solution)/shard_map/ppermute | solution.py:50
  68.8 19.5 %all-to-all-start.2 = ((bf16[8,32,1024]{2,1,0:T(8,128)(2,1)}), bf16[8,32,1024]{2,1,0:T(8,128)(2,1)S(1)}, u32[]{:S(2)}, u32[]{:S(2)}) async-start(bf16[8,32,1024]{2,1,0:T(8,128)(2,1)} %broadcast_in_dim.11), calls=%async_computation.2 | async-start | bytes 1048576 | tf_op jit(solution)/shard_map/all_to_all | solution.py:33
  91.0 28.7 %all-to-all-start.3 = ((bf16[16,16,512]{2,1,0:T(8,128)(2,1)}), bf16[16,16,512]{2,1,0:T(8,128)(2,1)S(1)}, u32[]{:S(2)}, u32[]{:S(2)}) async-start(bf16[16,16,512]{2,1,0:T(8,128)(2,1)} %bitcast.7), calls=%async_computation.3 | async-start | bytes 524288 | tf_op jit(solution)/shard_map/all_to_all | solution.py:33
  102.3 3.4 %collective-permute-start.6 = (bf16[1,256,512]{2,1,0:T(8,128)(2,1)S(1)}, bf16[1,256,512]{2,1,0:T(8,128)(2,1)S(1)}, u32[]{:S(2)}, u32[]{:S(2)}) collective-permute-start(bf16[1,256,512]{2,1,0:T(8,128)(2,1)S(1)} %get-tuple-element.27), channel_id=1, source_target_pairs={{0,8},{8,0},{1,9},{9,1},{2,10},{10,2},{3,11},{11,3},{4,12},{12,4},... | collective-permute-start | bytes 786440 | tf_op jit(solution)/shard_map/ppermute | solution.py:63
  120.5 23.2 %all-to-all-start.4 = ((bf16[16,16,512]{2,1,0:T(8,128)(2,1)}), bf16[16,16,512]{2,1,0:T(8,128)(2,1)S(1)}, u32[]{:S(2)}, u32[]{:S(2)}) async-start(bf16[16,16,512]{2,1,0:T(8,128)(2,1)} %broadcast_in_dim.13), calls=%async_computation.4 | async-start | bytes 524288 | tf_op jit(solution)/shard_map/all_to_all | solution.py:33
  126.1 8.3 %collective-permute-start.7 = (bf16[2,256,256]{2,1,0:T(8,128)(2,1)S(1)}, bf16[2,256,256]{2,1,0:T(8,128)(2,1)S(1)}, u32[]{:S(2)}, u32[]{:S(2)}) collective-permute-start(bf16[2,256,256]{2,1,0:T(8,128)(2,1)S(1)} %get-tuple-element.25), channel_id=1, source_target_pairs={{0,16},{16,0},{1,17},{17,1},{2,18},{18,2},{3,19},{19,3},{4,20},{20... | collective-permute-start | bytes 786440 | tf_op jit(solution)/shard_map/ppermute | solution.py:63
  146.6 17.2 %all-to-all-start.5 = ((bf16[8,32,1024]{2,1,0:T(8,128)(2,1)}), bf16[8,32,1024]{2,1,0:T(8,128)(2,1)S(1)}, u32[]{:S(2)}, u32[]{:S(2)}) async-start(bf16[8,32,1024]{2,1,0:T(8,128)(2,1)} %bitcast.47), calls=%async_computation.5 | async-start | bytes 1048576 | tf_op jit(solution)/shard_map/all_to_all | solution.py:33
  151.2 11.6 %collective-permute-start.8 = (bf16[256,512]{1,0:T(8,128)(2,1)S(1)}, bf16[256,512]{1,0:T(8,128)(2,1)S(1)}, u32[]{:S(2)}, u32[]{:S(2)}) collective-permute-start(bf16[256,512]{1,0:T(8,128)(2,1)S(1)} %bitcast.45), channel_id=1, source_target_pairs={{0,16},{16,0},{1,17},{17,1},{2,18},{18,2},{3,19},{19,3},{4,20},{20... | collective-permute-start | bytes 786440 | tf_op jit(solution)/shard_map/ppermute | solution.py:50
  165.2 25.7 %all-to-all-start.6 = ((bf16[32,32,512]{2,1,0:T(8,128)(2,1)}), bf16[32,32,512]{2,1,0:T(8,128)(2,1)}, u32[]{:S(2)}, u32[]{:S(2)}) async-start(bf16[32,32,512]{2,1,0:T(8,128)(2,1)} %bitcast.13), calls=%async_computation.6 | async-start | bytes 2097152 | tf_op jit(solution)/shard_map/all_to_all | solution.py:33
  173.3 17.7 %copy-start.2 = (bf16[1024,512]{1,0:T(8,128)(2,1)S(1)}, bf16[1024,512]{1,0:T(8,128)(2,1)}, u32[]{:S(2)}) copy-start(bf16[1024,512]{1,0:T(8,128)(2,1)} %maximum_select_fusion.2) | copy-start | bytes 3145732
  173.7 21.2 %collective-permute-start.9 = (bf16[512,512]{1,0:T(8,128)(2,1)}, bf16[512,512]{1,0:T(8,128)(2,1)S(1)}, u32[]{:S(2)}, u32[]{:S(2)}) collective-permute-start(bf16[512,512]{1,0:T(8,128)(2,1)} %maximum_select_fusion.10), channel_id=1, source_target_pairs={{0,8},{8,0},{1,9},{9,1},{2,10},{10,2},{3,11},{11,3},{4,12},{12,4},... | collective-permute-start | bytes 1572872 | tf_op jit(solution)/shard_map/ppermute | solution.py:50
  191.0 3.9 %copy-start.4 = (bf16[2,512,256]{2,1,0:T(8,128)(2,1)S(1)}, bf16[2,512,256]{2,1,0:T(8,128)(2,1)}, u32[]{:S(2)}) copy-start(bf16[2,512,256]{2,1,0:T(8,128)(2,1)} %maximum_select_fusion.9) | copy-start | bytes 1572868

commit v6 on v4

--- a/solution.py
+++ b/solution.py
@@ -40,10 +40,13 @@
     ).reshape(count * rows, cols)
 
 
-def scatter_sum(array, axes, count):
+def split(array, count):
     rows, cols = array.shape
-    blocks = array.astype(BF).reshape(count, rows // count, cols)
-    return exchange(blocks, axes).astype(F32).sum(axis=0)
+    return array.astype(BF).reshape(count, rows // count, cols)
+
+
+def add_up(blocks):
+    return blocks.astype(F32).sum(axis=0)
 
 
 def pair_up(array, name, axis):
@@ -70,6 +73,10 @@
     )
 
 
+def tie(*arrays):
+    return lax.optimization_barrier(arrays)
+
+
 def on_device(tokens, probe_draw, w_in, w_out):
     total_rows = probe_draw.shape[0]
     own_rows, feats = tokens.shape
@@ -79,40 +86,51 @@
     w_in_all = pair_up(pair_up(w_in, "xl", 1), "core", 1)
     w_out_all = pair_up(pair_up(w_out, "xl", 0), "core", 0)
     draw = probe_draw.reshape(nz, nn, own_rows, feats)
+    mine = lax.axis_index(("xl", "core"))
+    own_draw = lax.dynamic_index_in_dim(draw, mine, axis=1, keepdims=False)
+    own_sign = (2 * own_draw - 1).astype(BF).reshape(nz * own_rows, feats)
+    signal_part = contract_cols(own_sign, w_out_all)
+    own_tokens = gather(tokens, "z", nz)
+    hidden_part = jnp.dot(own_tokens, w_in_all, preferred_element_type=F32)
+    blocks = split(jnp.concatenate([hidden_part, signal_part], axis=1), nc)
+    blocks, draw = tie(blocks, probe_draw)
     sign_all = (
-        (2 * probe_draw - 1)
+        (2 * draw - 1)
         .astype(BF)
         .reshape(nz, 2, 2, own_rows, feats)
         .transpose(2, 1, 0, 3, 4)
         .reshape(total_rows, feats)
     )
-    mine = lax.axis_index(("xl", "core"))
-    own_draw = lax.dynamic_index_in_dim(draw, mine, axis=1, keepdims=False)
-    own_sign = (2 * own_draw - 1).astype(BF).reshape(nz * own_rows, feats)
-    signal_part = contract_cols(own_sign, w_out_all)
-    own_tokens = gather(tokens, "z", nz)
-    all_tokens = pair_up(pair_up(own_tokens, "xl", 0), "core", 0)
-    hidden_part = jnp.dot(own_tokens, w_in_all, preferred_element_type=F32)
-    both = scatter_sum(
-        jnp.concatenate([hidden_part, signal_part], axis=1), COL, nc
-    )
+    both, sign_all, w_in_all = tie(exchange(blocks, COL), sign_all, w_in_all)
+    both = add_up(both)
     slopes, bending, gated_own = local_terms(both[:, :wide], both[:, wide:])
     gated = gather(gated_own, COL, nc)
-    gated_hid = hand_over(hand_over(gated[None], "core", 0), "xl", 1)
-    gated_hid = gated_hid.reshape(total_rows, hid)
-    jac_own = scatter_sum(contract_cols(gated, w_in_all), "z", nz).astype(BF)
-    jac_rows = gather(jac_own, "z", nz)
-    jac_all = pair_up(pair_up(jac_rows, "xl", 0), "core", 0)
+    blocks = split(contract_cols(gated, w_in_all), nz)
+    blocks, late_tokens, late_gated = tie(blocks, own_tokens, gated)
+    token_pair = pair_up(late_tokens, "xl", 0)
+    gated_pair = hand_over(late_gated[None], "core", 0)
+    jac_sum, token_pair, gated_pair = tie(
+        exchange(blocks, "z"), token_pair, gated_pair
+    )
+    jac_own = add_up(jac_sum).astype(BF)
+    all_tokens = pair_up(token_pair, "core", 0)
+    gated_hid = hand_over(gated_pair, "xl", 1).reshape(total_rows, hid)
+    jac_rows, all_tokens, gated_hid = tie(
+        gather(jac_own, "z", nz), all_tokens, gated_hid
+    )
     back_part = jnp.dot(jac_rows, w_in_all, preferred_element_type=F32)
-    back_proj = scatter_sum(back_part, COL, nc)
+    jac_pair = pair_up(jac_rows, "xl", 0)
+    back_proj = add_up(exchange(split(back_part, nc), COL))
     rows = back_proj.shape[0]
     curv_own = (back_proj * bending).astype(BF).reshape(rows, nn, hid)
     slope_own = (back_proj * slopes).astype(BF).reshape(rows, nn, hid)
     terms = jnp.concatenate([curv_own, slope_own], axis=2).transpose(1, 0, 2)
     terms = jnp.broadcast_to(terms[:, None], (nn, nc, rows, 2 * hid))
-    terms = exchange(
-        terms.reshape(nn * nc, rows, 2 * hid), NEAR + COL
-    ).reshape(total_rows, 2 * hid)
+    jac_all = pair_up(jac_pair, "core", 0)
+    terms, jac_all = tie(
+        exchange(terms.reshape(nn * nc, rows, 2 * hid), NEAR + COL), jac_all
+    )
+    terms = terms.reshape(total_rows, 2 * hid)
     curv_term, slope_term = terms[:, :hid], terms[:, hid:]
     factor = 1.0 / jnp.sqrt(jnp.float32(total_rows))
     grad_in = factor * (

time: 182 us -> 175 us (0.962)
  blocking collectives: 82.8 us -> 12.3 us
  waiting for transfers between devices: 10.1 us -> 42.1 us
  starting transfers between devices: 63.9 us -> 94 us
  matrix products: 14 us -> 9.72 us
  other arithmetic: 6.28 us -> 9.86 us
    all_to_all x4 -> x1, blocking collectives: 82.8 us -> 12.3 us  [exchange(): return lax.all_to_all(blocks, axes, 0, 0, tiled=True)]
    all_to_all x3 -> x6, starting transfers between devices: 28.4 us -> 64.2 us  [exchange(): return lax.all_to_all(blocks, axes, 0, 0, tiled=True)]
    all_to_all x3 -> x6, waiting for transfers between devices: 0.01 us -> 31.4 us  [exchange(): return lax.all_to_all(blocks, axes, 0, 0, tiled=True)]
    ppermute x2, starting transfers between devices: 11.8 us -> 7.14 us  [hand_over(): far = lax.ppermute(jnp.where(first, right, left), name, [(0, 1), (1, 0)])]
    select_n x4 -> x7, other arithmetic: 5.02 us -> 4.96 us  [pair_up(): jnp.where(lax.axis_index(name) == 0, jnp.concatenate([array, far], axis=a...]
  transfers between devices with their start and end apart: 13 -> 16, of which waited for: 2 -> 9; matrix products, arithmetic and copies ran while one was open for 8% -> 8% of each run, Pallas kernels for 0% -> 0%
where the time goes in v6:
time: 175 us; the launch traced here: 173 us
  starting transfers between devices  94 us (54%)
  waiting for transfers between devices  42.1 us (24%)
  blocking collectives  12.3 us (7%)
  other arithmetic  9.86 us (6%)
  matrix products  9.72 us (6%)
  local copies, waits for them, and re-layouts  4.49 us (3%)
    all_to_all x6, starting transfers between devices, exchange(): return lax.all_to_all(blocks, axes, 0, 0, tiled=True)  64.2 us
    all_to_all x6, waiting for transfers between devices, exchange(): return lax.all_to_all(blocks, axes, 0, 0, tiled=True)  31.4 us
    ppermute x8, starting transfers between devices, pair_up(): far = lax.ppermute(array, name, [(0, 1), (1, 0)])  22.6 us
    all_to_all x1, blocking collectives, exchange(): return lax.all_to_all(blocks, axes, 0, 0, tiled=True)  12.3 us
    ppermute x2, waiting for transfers between devices, hand_over(): far = lax.ppermute(jnp.where(first, right, left), name, [(0, 1), (1, 0)])  8.5 us
    ppermute x2, starting transfers between devices, hand_over(): far = lax.ppermute(jnp.where(first, right, left), name, [(0, 1), (1, 0)])  7.14 us
    dot_general x3, matrix products, contract_rows(): lax.dot_general(left, right, (((0,), (0,)), ((), ())), preferred_element_...  5.17 us
    select_n x7, other arithmetic, pair_up(): jnp.where(lax.axis_index(name) == 0, jnp.concatenate([array, far], axis=a...  4.96 us
  transfers between devices with their start and end apart: 16, of which 9 were waited for; matrix products, arithmetic and copies ran while one was open for 8% of the time, Pallas kernels for 0%

profile of v6, /device:TPU:1, one launch (start us, length us, event | category | flops | bytes accessed | tf_op | source)
XLA Modules:
  0.0 173.5 jit_solution(11067110791510949433)
XLA Ops:
  0.6 4.0 %collective-permute-start = (bf16[512,256]{1,0:T(8,128)(2,1)}, bf16[512,256]{1,0:T(8,128)(2,1)S(1)}, u32[]{:S(2)}, u32[]{:S(2)}) collective-permute-start(bf16[512,256]{1,0:T(8,128)(2,1)} %param.6), channel_id=1, source_target_pairs={{0,16},{16,0},{1,17},{17,1},{2,18},{18,2},{3,19},{19,3},{4,20},{20... | collective-permute-start | bytes 786440 | tf_op jit(solution)/shard_map/ppermute | solution.py:53
  4.6 1.9 %collective-permute-start.2 = (bf16[256,512]{1,0:T(8,128)(2,1)}, bf16[256,512]{1,0:T(8,128)(2,1)S(1)}, u32[]{:S(2)}, u32[]{:S(2)}) collective-permute-start(bf16[256,512]{1,0:T(8,128)(2,1)} %param.7), channel_id=1, source_target_pairs={{0,16},{16,0},{1,17},{17,1},{2,18},{18,2},{3,19},{19,3},{4,20},{20... | collective-permute-start | bytes 786440 | tf_op jit(solution)/shard_map/ppermute | solution.py:53
  6.5 1.4 broadcast_in_dim.10
  8.0 15.2 %all-to-all-start = ((bf16[16,16,512]{2,1,0:T(8,128)(2,1)}), bf16[16,16,512]{2,1,0:T(8,128)(2,1)S(1)}, u32[]{:S(2)}, u32[]{:S(2)}) async-start(bf16[16,16,512]{2,1,0:T(8,128)(2,1)} %broadcast_in_dim.10), calls=%async_computation | async-start | bytes 524288 | tf_op jit(solution)/shard_map/all_to_all | solution.py:33
  23.1 1.2 maximum_select_fusion.4
  24.3 3.4 %collective-permute-start.1 = (bf16[512,512]{1,0:T(8,128)(2,1)S(1)}, bf16[512,512]{1,0:T(8,128)(2,1)S(1)}, u32[]{:S(2)}, u32[]{:S(2)}) collective-permute-start(bf16[512,512]{1,0:T(8,128)(2,1)S(1)} %maximum_select_fusion.4), channel_id=1, source_target_pairs={{0,8},{8,0},{1,9},{9,1},{2,10},{10,2},{3,11},{11,3},{4,12},{12,4},... | collective-permute-start | bytes 1572872 | tf_op jit(solution)/shard_map/ppermute | solution.py:53
  27.7 1.2 maximum_select_fusion.5
  29.0 1.9 %collective-permute-start.3 = (bf16[512,512]{1,0:T(8,128)(2,1)S(1)}, bf16[512,512]{1,0:T(8,128)(2,1)}, u32[]{:S(2)}, u32[]{:S(2)}) collective-permute-start(bf16[512,512]{1,0:T(8,128)(2,1)S(1)} %maximum_select_fusion.5), channel_id=1, source_target_pairs={{0,8},{8,0},{1,9},{9,1},{2,10},{10,2},{3,11},{11,3},{4,12},{12,4},... | collective-permute-start | bytes 1572872 | tf_op jit(solution)/shard_map/ppermute | solution.py:53
  30.9 1.1 fusion.13
  32.0 0.3 maximum_select_fusion
  32.3 0.6 collective-permute-done.3
  32.9 1.7 convolution_convert_fusion.2
  34.6 1.3 all-to-all-done
  35.9 0.4 convolution_convert_fusion
  36.4 1.1 pad_maximum_fusion
  37.4 6.7 %all-to-all-start.1 = ((bf16[8,32,2048]{2,1,0:T(8,128)(2,1)}), bf16[8,32,2048]{2,1,0:T(8,128)(2,1)S(1)}, u32[]{:S(2)}, u32[]{:S(2)}) async-start(bf16[8,32,2048]{2,1,0:T(8,128)(2,1)} %pad_maximum_fusion), calls=%async_computation.1 | async-start | bytes 2097152 | tf_op jit(solution)/shard_map/all_to_all | solution.py:33
  44.1 1.9 %add_convert_fusion = bf16[1024,512]{1,0:T(8,128)(2,1)S(1)} fusion(s32[1024,512]{1,0:T(8,128)} %param.5), kind=kLoop, calls=%fused_computation.1 | loop fusion | flops 1572864 | bytes 3145728 | tf_op jit(solution)/shard_map/convert_element_type | solution.py:99
  46.0 1.0 copy.11
  47.0 7.8 %all-to-all-done.1 = bf16[8,32,2048]{2,1,0:T(8,128)(2,1)S(1)} async-done(((bf16[8,32,2048]{2,1,0:T(8,128)(2,1)}), bf16[8,32,2048]{2,1,0:T(8,128)(2,1)S(1)}, u32[]{:S(2)}, u32[]{:S(2)}) %all-to-all-start.1) | async-done | bytes 1048608 | tf_op jit(solution)/shard_map/all_to_all | solution.py:33
  55.1 12.3 %all_to_all.35 = bf16[8,32,1024]{2,1,0:T(8,128)(2,1)S(1)} all-to-all(bf16[8,32,1024]{2,1,0:T(8,128)(2,1)S(1)} %broadcast_in_dim.11), channel_id=1, replica_groups=mesh['z'=16,'xl'=2,'core'=2,'xh'=2,'y'=4] {'xh','y'}, dimensions={0} | all-to-all | bytes 1048576 | tf_op jit(solution)/shard_map/all_to_all | solution.py:33
  67.4 1.2 convolution_convert_fusion.3
  68.6 18.1 %all-to-all-start.3 = ((bf16[16,16,512]{2,1,0:T(8,128)(2,1)}), bf16[16,16,512]{2,1,0:T(8,128)(2,1)S(1)}, u32[]{:S(2)}, u32[]{:S(2)}) async-start(bf16[16,16,512]{2,1,0:T(8,128)(2,1)} %bitcast.10), calls=%async_computation.3 | async-start | bytes 524288 | tf_op jit(solution)/shard_map/all_to_all | solution.py:33
  86.7 2.2 %collective-permute-start.4 = (bf16[256,512]{1,0:T(8,128)(2,1)S(1)}, bf16[256,512]{1,0:T(8,128)(2,1)S(1)}, u32[]{:S(2)}, u32[]{:S(2)}) collective-permute-start(bf16[256,512]{1,0:T(8,128)(2,1)S(1)} %bitcast.45), channel_id=1, source_target_pairs={{0,16},{16,0},{1,17},{17,1},{2,18},{18,2},{3,19},{19,3},{4,20},{20... | collective-permute-start | bytes 786440 | tf_op jit(solution)/shard_map/ppermute | solution.py:53
  89.0 4.9 %collective-permute-start.5 = (bf16[1,256,512]{2,1,0:T(8,128)(2,1)S(1)}, bf16[1,256,512]{2,1,0:T(8,128)(2,1)S(1)}, u32[]{:S(2)}, u32[]{:S(2)}) collective-permute-start(bf16[1,256,512]{2,1,0:T(8,128)(2,1)S(1)} %get-tuple-element.39), channel_id=1, source_target_pairs={{0,8},{8,0},{1,9},{9,1},{2,10},{10,2},{3,11},{11,3},{4,12},{12,4},... | collective-permute-start | bytes 786440 | tf_op jit(solution)/shard_map/ppermute | solution.py:66
  93.9 0.2 maximum_select_fusion.6
  94.2 0.9 collective-permute-done.5
  95.2 4.4 %all-to-all-done.3 = bf16[16,16,512]{2,1,0:T(8,128)(2,1)S(1)} async-done(((bf16[16,16,512]{2,1,0:T(8,128)(2,1)}), bf16[16,16,512]{2,1,0:T(8,128)(2,1)S(1)}, u32[]{:S(2)}, u32[]{:S(2)}) %all-to-all-start.3) | async-done | bytes 262176 | tf_op jit(solution)/shard_map/all_to_all | solution.py:33
  99.6 0.7 broadcast_in_dim.13
  100.3 10.0 %all-to-all-start.4 = ((bf16[16,16,512]{2,1,0:T(8,128)(2,1)}), bf16[16,16,512]{2,1,0:T(8,128)(2,1)S(1)}, u32[]{:S(2)}, u32[]{:S(2)}) async-start(bf16[16,16,512]{2,1,0:T(8,128)(2,1)} %broadcast_in_dim.13), calls=%async_computation.4 | async-start | bytes 524288 | tf_op jit(solution)/shard_map/all_to_all | solution.py:33
  110.3 4.3 %collective-permute-start.6 = (bf16[512,512]{1,0:T(8,128)(2,1)S(1)}, bf16[512,512]{1,0:T(8,128)(2,1)S(1)}, u32[]{:S(2)}, u32[]{:S(2)}) collective-permute-start(bf16[512,512]{1,0:T(8,128)(2,1)S(1)} %maximum_select_fusion.6), channel_id=1, source_target_pairs={{0,8},{8,0},{1,9},{9,1},{2,10},{10,2},{3,11},{11,3},{4,12},{12,4},... | collective-permute-start | bytes 1572872 | tf_op jit(solution)/shard_map/ppermute | solution.py:53
  114.6 2.2 %collective-permute-start.7 = (bf16[2,256,256]{2,1,0:T(8,128)(2,1)S(1)}, bf16[2,256,256]{2,1,0:T(8,128)(2,1)S(1)}, u32[]{:S(2)}, u32[]{:S(2)}) collective-permute-start(bf16[2,256,256]{2,1,0:T(8,128)(2,1)S(1)} %get-tuple-element.37), channel_id=1, source_target_pairs={{0,16},{16,0},{1,17},{17,1},{2,18},{18,2},{3,19},{19,3},{4,20},{20... | collective-permute-start | bytes 786440 | tf_op jit(solution)/shard_map/ppermute | solution.py:66
  116.8 7.6 %collective-permute-done.7 = bf16[2,256,256]{2,1,0:T(8,128)(2,1)S(1)} collective-permute-done((bf16[2,256,256]{2,1,0:T(8,128)(2,1)S(1)}, bf16[2,256,256]{2,1,0:T(8,128)(2,1)S(1)}, u32[]{:S(2)}, u32[]{:S(2)}) %collective-permute-start.7) | collective-permute-done | bytes 262176 | tf_op jit(solution)/shard_map/ppermute | solution.py:66
  124.4 0.2 maximum_select_fusion.8
  124.6 1.4 maximum_select_fusion.2
  126.1 1.2 convolution_convert_fusion.1
  127.3 3.5 %all-to-all-start.5 = ((bf16[8,32,1024]{2,1,0:T(8,128)(2,1)}), bf16[8,32,1024]{2,1,0:T(8,128)(2,1)S(1)}, u32[]{:S(2)}, u32[]{:S(2)}) async-start(bf16[8,32,1024]{2,1,0:T(8,128)(2,1)} %bitcast.14), calls=%async_computation.5 | async-start | bytes 1048576 | tf_op jit(solution)/shard_map/all_to_all | solution.py:33
  130.8 2.6 %collective-permute-start.8 = (bf16[256,512]{1,0:T(8,128)(2,1)S(1)}, bf16[256,512]{1,0:T(8,128)(2,1)S(1)}, u32[]{:S(2)}, u32[]{:S(2)}) collective-permute-start(bf16[256,512]{1,0:T(8,128)(2,1)S(1)} %bitcast.48), channel_id=1, source_target_pairs={{0,16},{16,0},{1,17},{17,1},{2,18},{18,2},{3,19},{19,3},{4,20},{20... | collective-permute-start | bytes 786440 | tf_op jit(solution)/shard_map/ppermute | solution.py:53
  133.4 6.0 %all-to-all-done.5 = bf16[8,32,1024]{2,1,0:T(8,128)(2,1)S(1)} async-done(((bf16[8,32,1024]{2,1,0:T(8,128)(2,1)}), bf16[8,32,1024]{2,1,0:T(8,128)(2,1)S(1)}, u32[]{:S(2)}, u32[]{:S(2)}) %all-to-all-start.5) | async-done | bytes 524320 | tf_op jit(solution)/shard_map/all_to_all | solution.py:33
  139.7 1.1 broadcast_in_dim.14
  140.8 10.8 %all-to-all-start.6 = ((bf16[32,32,512]{2,1,0:T(8,128)(2,1)}), bf16[32,32,512]{2,1,0:T(8,128)(2,1)}, u32[]{:S(2)}, u32[]{:S(2)}) async-start(bf16[32,32,512]{2,1,0:T(8,128)(2,1)} %bitcast.16), calls=%async_computation.6 | async-start | bytes 2097152 | tf_op jit(solution)/shard_map/all_to_all | solution.py:33
  151.7 0.2 maximum_select_fusion.9
  151.9 2.4 %collective-permute-start.9 = (bf16[512,512]{1,0:T(8,128)(2,1)S(1)}, bf16[512,512]{1,0:T(8,128)(2,1)S(1)}, u32[]{:S(2)}, u32[]{:S(2)}) collective-permute-start(bf16[512,512]{1,0:T(8,128)(2,1)S(1)} %maximum_select_fusion.9), channel_id=1, source_target_pairs={{0,8},{8,0},{1,9},{9,1},{2,10},{10,2},{3,11},{11,3},{4,12},{12,4},... | collective-permute-start | bytes 1572872 | tf_op jit(solution)/shard_map/ppermute | solution.py:53
  154.3 1.6 collective-permute-done.9
  155.9 0.5 maximum_select_fusion.3
  156.3 12.0 %all-to-all-done.6 = bf16[32,32,512]{2,1,0:T(8,128)(2,1)} async-done(((bf16[32,32,512]{2,1,0:T(8,128)(2,1)}), bf16[32,32,512]{2,1,0:T(8,128)(2,1)}, u32[]{:S(2)}, u32[]{:S(2)}) %all-to-all-start.6) | async-done | bytes 1048608 | tf_op jit(solution)/shard_map/all_to_all | solution.py:33
  168.3 1.6 fusion.10
  169.9 2.3 %convolution_multiply_fusion = f32[256,512]{1,0:T(8,128)} fusion(bf16[1024,512]{1,0:T(8,128)(2,1)S(1)} %bitcast.52, bf16[1024,512]{1,0:T(8,128)(2,1)} %bitcast.17), kind=kOutput, calls=%fused_computation.5 | convolution fusion | flops 268566528 | bytes 2097152 | tf_op jit(solution)/shard_map/dot_general | solution.py:21
  172.2 1.3 fusion
  (24 shorter events, 0.8 us)
Async XLA Ops:
  0.6 22.5 %collective-permute-start = (bf16[512,256]{1,0:T(8,128)(2,1)}, bf16[512,256]{1,0:T(8,128)(2,1)S(1)}, u32[]{:S(2)}, u32[]{:S(2)}) collective-permute-start(bf16[512,256]{1,0:T(8,128)(2,1)} %param.6), channel_id=1, source_target_pairs={{0,16},{16,0},{1,17},{17,1},{2,18},{18,2},{3,19},{19,3},{4,20},{20... | collective-permute-start | bytes 786440 | tf_op jit(solution)/shard_map/ppermute | solution.py:53
  4.6 23.2 %collective-permute-start.2 = (bf16[256,512]{1,0:T(8,128)(2,1)}, bf16[256,512]{1,0:T(8,128)(2,1)S(1)}, u32[]{:S(2)}, u32[]{:S(2)}) collective-permute-start(bf16[256,512]{1,0:T(8,128)(2,1)} %param.7), channel_id=1, source_target_pairs={{0,16},{16,0},{1,17},{17,1},{2,18},{18,2},{3,19},{19,3},{4,20},{20... | collective-permute-start | bytes 786440 | tf_op jit(solution)/shard_map/ppermute | solution.py:53
  8.0 27.9 %all-to-all-start = ((bf16[16,16,512]{2,1,0:T(8,128)(2,1)}), bf16[16,16,512]{2,1,0:T(8,128)(2,1)S(1)}, u32[]{:S(2)}, u32[]{:S(2)}) async-start(bf16[16,16,512]{2,1,0:T(8,128)(2,1)} %broadcast_in_dim.10), calls=%async_computation | async-start | bytes 524288 | tf_op jit(solution)/shard_map/all_to_all | solution.py:33
  24.3 7.7 %collective-permute-start.1 = (bf16[512,512]{1,0:T(8,128)(2,1)S(1)}, bf16[512,512]{1,0:T(8,128)(2,1)S(1)}, u32[]{:S(2)}, u32[]{:S(2)}) collective-permute-start(bf16[512,512]{1,0:T(8,128)(2,1)S(1)} %maximum_select_fusion.4), channel_id=1, source_target_pairs={{0,8},{8,0},{1,9},{9,1},{2,10},{10,2},{3,11},{11,3},{4,12},{12,4},... | collective-permute-start | bytes 1572872 | tf_op jit(solution)/shard_map/ppermute | solution.py:53
  29.0 3.9 %collective-permute-start.3 = (bf16[512,512]{1,0:T(8,128)(2,1)S(1)}, bf16[512,512]{1,0:T(8,128)(2,1)}, u32[]{:S(2)}, u32[]{:S(2)}) collective-permute-start(bf16[512,512]{1,0:T(8,128)(2,1)S(1)} %maximum_select_fusion.5), channel_id=1, source_target_pairs={{0,8},{8,0},{1,9},{9,1},{2,10},{10,2},{3,11},{11,3},{4,12},{12,4},... | collective-permute-start | bytes 1572872 | tf_op jit(solution)/shard_map/ppermute | solution.py:53
  37.4 17.4 %all-to-all-start.1 = ((bf16[8,32,2048]{2,1,0:T(8,128)(2,1)}), bf16[8,32,2048]{2,1,0:T(8,128)(2,1)S(1)}, u32[]{:S(2)}, u32[]{:S(2)}) async-start(bf16[8,32,2048]{2,1,0:T(8,128)(2,1)} %pad_maximum_fusion), calls=%async_computation.1 | async-start | bytes 2097152 | tf_op jit(solution)/shard_map/all_to_all | solution.py:33
  68.6 30.9 %all-to-all-start.3 = ((bf16[16,16,512]{2,1,0:T(8,128)(2,1)}), bf16[16,16,512]{2,1,0:T(8,128)(2,1)S(1)}, u32[]{:S(2)}, u32[]{:S(2)}) async-start(bf16[16,16,512]{2,1,0:T(8,128)(2,1)} %bitcast.10), calls=%async_computation.3 | async-start | bytes 524288 | tf_op jit(solution)/shard_map/all_to_all | solution.py:33
  86.7 7.2 %collective-permute-start.4 = (bf16[256,512]{1,0:T(8,128)(2,1)S(1)}, bf16[256,512]{1,0:T(8,128)(2,1)S(1)}, u32[]{:S(2)}, u32[]{:S(2)}) collective-permute-start(bf16[256,512]{1,0:T(8,128)(2,1)S(1)} %bitcast.45), channel_id=1, source_target_pairs={{0,16},{16,0},{1,17},{17,1},{2,18},{18,2},{3,19},{19,3},{4,20},{20... | collective-permute-start | bytes 786440 | tf_op jit(solution)/shard_map/ppermute | solution.py:53
  89.0 6.1 %collective-permute-start.5 = (bf16[1,256,512]{2,1,0:T(8,128)(2,1)S(1)}, bf16[1,256,512]{2,1,0:T(8,128)(2,1)S(1)}, u32[]{:S(2)}, u32[]{:S(2)}) collective-permute-start(bf16[1,256,512]{2,1,0:T(8,128)(2,1)S(1)} %get-tuple-element.39), channel_id=1, source_target_pairs={{0,8},{8,0},{1,9},{9,1},{2,10},{10,2},{3,11},{11,3},{4,12},{12,4},... | collective-permute-start | bytes 786440 | tf_op jit(solution)/shard_map/ppermute | solution.py:66
  100.3 25.8 %all-to-all-start.4 = ((bf16[16,16,512]{2,1,0:T(8,128)(2,1)}), bf16[16,16,512]{2,1,0:T(8,128)(2,1)S(1)}, u32[]{:S(2)}, u32[]{:S(2)}) async-start(bf16[16,16,512]{2,1,0:T(8,128)(2,1)} %broadcast_in_dim.13), calls=%async_computation.4 | async-start | bytes 524288 | tf_op jit(solution)/shard_map/all_to_all | solution.py:33
  110.3 14.4 %collective-permute-start.6 = (bf16[512,512]{1,0:T(8,128)(2,1)S(1)}, bf16[512,512]{1,0:T(8,128)(2,1)S(1)}, u32[]{:S(2)}, u32[]{:S(2)}) collective-permute-start(bf16[512,512]{1,0:T(8,128)(2,1)S(1)} %maximum_select_fusion.6), channel_id=1, source_target_pairs={{0,8},{8,0},{1,9},{9,1},{2,10},{10,2},{3,11},{11,3},{4,12},{12,4},... | collective-permute-start | bytes 1572872 | tf_op jit(solution)/shard_map/ppermute | solution.py:53
  114.6 9.8 %collective-permute-start.7 = (bf16[2,256,256]{2,1,0:T(8,128)(2,1)S(1)}, bf16[2,256,256]{2,1,0:T(8,128)(2,1)S(1)}, u32[]{:S(2)}, u32[]{:S(2)}) collective-permute-start(bf16[2,256,256]{2,1,0:T(8,128)(2,1)S(1)} %get-tuple-element.37), channel_id=1, source_target_pairs={{0,16},{16,0},{1,17},{17,1},{2,18},{18,2},{3,19},{19,3},{4,20},{20... | collective-permute-start | bytes 786440 | tf_op jit(solution)/shard_map/ppermute | solution.py:66
  127.3 12.1 %all-to-all-start.5 = ((bf16[8,32,1024]{2,1,0:T(8,128)(2,1)}), bf16[8,32,1024]{2,1,0:T(8,128)(2,1)S(1)}, u32[]{:S(2)}, u32[]{:S(2)}) async-start(bf16[8,32,1024]{2,1,0:T(8,128)(2,1)} %bitcast.14), calls=%async_computation.5 | async-start | bytes 1048576 | tf_op jit(solution)/shard_map/all_to_all | solution.py:33
  130.8 20.9 %collective-permute-start.8 = (bf16[256,512]{1,0:T(8,128)(2,1)S(1)}, bf16[256,512]{1,0:T(8,128)(2,1)S(1)}, u32[]{:S(2)}, u32[]{:S(2)}) collective-permute-start(bf16[256,512]{1,0:T(8,128)(2,1)S(1)} %bitcast.48), channel_id=1, source_target_pairs={{0,16},{16,0},{1,17},{17,1},{2,18},{18,2},{3,19},{19,3},{4,20},{20... | collective-permute-start | bytes 786440 | tf_op jit(solution)/shard_map/ppermute | solution.py:53
  140.8 27.4 %all-to-all-start.6 = ((bf16[32,32,512]{2,1,0:T(8,128)(2,1)}), bf16[32,32,512]{2,1,0:T(8,128)(2,1)}, u32[]{:S(2)}, u32[]{:S(2)}) async-start(bf16[32,32,512]{2,1,0:T(8,128)(2,1)} %bitcast.16), calls=%async_computation.6 | async-start | bytes 2097152 | tf_op jit(solution)/shard_map/all_to_all | solution.py:33
  151.7 16.6 %copy-start = (bf16[1024,512]{1,0:T(8,128)(2,1)S(1)}, bf16[1024,512]{1,0:T(8,128)(2,1)}, u32[]{:S(2)}) copy-start(bf16[1024,512]{1,0:T(8,128)(2,1)} %maximum_select_fusion.2) | copy-start | bytes 3145732
  151.9 3.9 %collective-permute-start.9 = (bf16[512,512]{1,0:T(8,128)(2,1)S(1)}, bf16[512,512]{1,0:T(8,128)(2,1)S(1)}, u32[]{:S(2)}, u32[]{:S(2)}) collective-permute-start(bf16[512,512]{1,0:T(8,128)(2,1)S(1)} %maximum_select_fusion.9), channel_id=1, source_target_pairs={{0,8},{8,0},{1,9},{9,1},{2,10},{10,2},{3,11},{11,3},{4,12},{12,4},... | collective-permute-start | bytes 1572872 | tf_op jit(solution)/shard_map/ppermute | solution.py:53
  168.3 1.6 copy-start.1

commit v7 on v6

--- a/solution.py
+++ b/solution.py
@@ -1,6 +1,8 @@
 import jax
 import jax.numpy as jnp
 from jax import lax
+from jax.experimental import pallas as pl
+from jax.experimental.pallas import tpu as pltpu
 from jax.sharding import Mesh, PartitionSpec as P
 
 NEAR, COL = ("core", "xl"), ("xh", "y")
@@ -77,6 +79,28 @@
     return lax.optimization_barrier(arrays)
 
 
+def side_by_side(left, right, steps):
+    rows, cols = left.shape
+    part = rows // steps
+
+    def kernel(left, right, both):
+        both[:, :cols] = left[...]
+        both[:, cols:] = right[...]
+
+    half = pl.BlockSpec((part, cols), lambda i: (i, 0))
+    return pl.pallas_call(
+        kernel,
+        grid=(steps,),
+        out_shape=jax.ShapeDtypeStruct((rows, 2 * cols), BF),
+        in_specs=[half, half],
+        out_specs=pl.BlockSpec((part, 2 * cols), lambda i: (i, 0)),
+        compiler_params=pltpu.CompilerParams(vmem_limit_bytes=8 * 2**20),
+        cost_estimate=pl.CostEstimate(
+            flops=0, bytes_accessed=8 * rows * cols, transcendentals=0
+        ),
+    )(left, right)
+
+
 def on_device(tokens, probe_draw, w_in, w_out):
     total_rows = probe_draw.shape[0]
     own_rows, feats = tokens.shape
@@ -92,7 +116,14 @@
     signal_part = contract_cols(own_sign, w_out_all)
     own_tokens = gather(tokens, "z", nz)
     hidden_part = jnp.dot(own_tokens, w_in_all, preferred_element_type=F32)
-    blocks = split(jnp.concatenate([hidden_part, signal_part], axis=1), nc)
+    blocks = lax.cond(
+        lax.axis_index("core") == 0,
+        lambda *parts: side_by_side(*parts, 16),
+        lambda *parts: side_by_side(*parts, 1),
+        hidden_part.astype(BF),
+        signal_part.astype(BF),
+    )
+    blocks = split(blocks, nc)
     blocks, draw = tie(blocks, probe_draw)
     sign_all = (
         (2 * draw - 1)
@@ -106,17 +137,14 @@
     slopes, bending, gated_own = local_terms(both[:, :wide], both[:, wide:])
     gated = gather(gated_own, COL, nc)
     blocks = split(contract_cols(gated, w_in_all), nz)
-    blocks, late_tokens, late_gated = tie(blocks, own_tokens, gated)
+    blocks, late_tokens = tie(blocks, own_tokens)
     token_pair = pair_up(late_tokens, "xl", 0)
-    gated_pair = hand_over(late_gated[None], "core", 0)
-    jac_sum, token_pair, gated_pair = tie(
-        exchange(blocks, "z"), token_pair, gated_pair
-    )
+    jac_sum, token_pair, late_gated = tie(exchange(blocks, "z"), token_pair, gated)
     jac_own = add_up(jac_sum).astype(BF)
-    all_tokens = pair_up(token_pair, "core", 0)
-    gated_hid = hand_over(gated_pair, "xl", 1).reshape(total_rows, hid)
-    jac_rows, all_tokens, gated_hid = tie(
-        gather(jac_own, "z", nz), all_tokens, gated_hid
+    by_xl = late_gated.reshape(-1, 2, 2, hid).transpose(0, 2, 1, 3)
+    gated_pair = hand_over(by_xl.reshape(1, -1, wide), "xl", 0)
+    jac_rows, gated_pair, token_pair = tie(
+        gather(jac_own, "z", nz), gated_pair, token_pair
     )
     back_part = jnp.dot(jac_rows, w_in_all, preferred_element_type=F32)
     jac_pair = pair_up(jac_rows, "xl", 0)
@@ -126,9 +154,14 @@
     slope_own = (back_proj * slopes).astype(BF).reshape(rows, nn, hid)
     terms = jnp.concatenate([curv_own, slope_own], axis=2).transpose(1, 0, 2)
     terms = jnp.broadcast_to(terms[:, None], (nn, nc, rows, 2 * hid))
+    terms, jac_pair, gated_pair, token_pair = tie(
+        terms.reshape(nn * nc, rows, 2 * hid), jac_pair, gated_pair, token_pair
+    )
     jac_all = pair_up(jac_pair, "core", 0)
-    terms, jac_all = tie(
-        exchange(terms.reshape(nn * nc, rows, 2 * hid), NEAR + COL), jac_all
+    all_tokens = pair_up(token_pair, "core", 0)
+    gated_hid = hand_over(gated_pair[None], "core", 0).reshape(total_rows, hid)
+    terms, jac_all, all_tokens, gated_hid = tie(
+        exchange(terms, NEAR + COL), jac_all, all_tokens, gated_hid
     )
     terms = terms.reshape(total_rows, 2 * hid)
     curv_term, slope_term = terms[:, :hid], terms[:, hid:]

time: 175 us -> 172 us (0.983)
  starting transfers between devices: 94 us -> 85.2 us
  blocking collectives: 12.3 us -> 14.6 us
    ppermute x8, waiting for transfers between devices: 2.14 us -> 10 us  [pair_up(): far = lax.ppermute(array, name, [(0, 1), (1, 0)])]
    all_to_all x6, waiting for transfers between devices: 31.4 us -> 25.6 us  [exchange(): return lax.all_to_all(blocks, axes, 0, 0, tiled=True)]
    all_to_all x6, starting transfers between devices: 64.2 us -> 60.3 us  [exchange(): return lax.all_to_all(blocks, axes, 0, 0, tiled=True)]
    ppermute x2, waiting for transfers between devices: 8.5 us -> 4.8 us  [hand_over(): far = lax.ppermute(jnp.where(first, right, left), name, [(0, 1), (1, 0)])]
    ppermute x2, starting transfers between devices: 7.14 us -> 4.56 us  [hand_over(): far = lax.ppermute(jnp.where(first, right, left), name, [(0, 1), (1, 0)])]
    ppermute x8, starting transfers between devices: 22.6 us -> 20.4 us  [pair_up(): far = lax.ppermute(array, name, [(0, 1), (1, 0)])]
    all_to_all x1, blocking collectives: 12.3 us -> 14.6 us  [exchange(): return lax.all_to_all(blocks, axes, 0, 0, tiled=True)]
    select_n x7, other arithmetic: 4.96 us -> 7.21 us  [pair_up(): jnp.where(lax.axis_index(name) == 0, jnp.concatenate([array, far], axis=a...]
  transfers between devices with their start and end apart: 16 -> 16, of which waited for: 9 -> 10; matrix products, arithmetic and copies ran while one was open for 8% -> 9% of each run, Pallas kernels for 0% -> 0%
where the time goes in v7:
time: 172 us; the launch traced here: 169 us
  starting transfers between devices  85.2 us (50%)
  waiting for transfers between devices  40.5 us (24%)
  blocking collectives  14.6 us (8%)
  other arithmetic  10.9 us (6%)
  matrix products  10 us (6%)
  local copies, waits for them, and re-layouts  5.94 us (3%)
    all_to_all x6, starting transfers between devices, exchange(): return lax.all_to_all(blocks, axes, 0, 0, tiled=True)  60.3 us
    all_to_all x6, waiting for transfers between devices, exchange(): return lax.all_to_all(blocks, axes, 0, 0, tiled=True)  25.6 us
    ppermute x8, starting transfers between devices, pair_up(): far = lax.ppermute(array, name, [(0, 1), (1, 0)])  20.4 us
    all_to_all x1, blocking collectives, exchange(): return lax.all_to_all(blocks, axes, 0, 0, tiled=True)  14.6 us
    ppermute x8, waiting for transfers between devices, pair_up(): far = lax.ppermute(array, name, [(0, 1), (1, 0)])  10 us
    select_n x7, other arithmetic, pair_up(): jnp.where(lax.axis_index(name) == 0, jnp.concatenate([array, far], axis=a...  7.21 us
    dot_general x3, matrix products, contract_rows(): lax.dot_general(left, right, (((0,), (0,)), ((), ())), preferred_element_...  5.43 us
    ppermute x2, waiting for transfers between devices, hand_over(): far = lax.ppermute(jnp.where(first, right, left), name, [(0, 1), (1, 0)])  4.8 us
  transfers between devices with their start and end apart: 16, of which 10 were waited for; matrix products, arithmetic and copies ran while one was open for 9% of the time, Pallas kernels for 0%

profile of v7, /device:TPU:1, one launch (start us, length us, event | category | flops | bytes accessed | tf_op | source)
XLA Modules:
  0.0 169.2 jit_solution(5090247208892675155)
XLA Ops:
  0.6 4.0 %collective-permute-start = (bf16[512,256]{1,0:T(8,128)(2,1)}, bf16[512,256]{1,0:T(8,128)(2,1)S(1)}, u32[]{:S(2)}, u32[]{:S(2)}) collective-permute-start(bf16[512,256]{1,0:T(8,128)(2,1)} %param.8), channel_id=1, source_target_pairs={{0,16},{16,0},{1,17},{17,1},{2,18},{18,2},{3,19},{19,3},{4,20},{20... | collective-permute-start | bytes 786440 | tf_op jit(solution)/shard_map/ppermute | solution.py:55
  4.6 1.9 %collective-permute-start.2 = (bf16[256,512]{1,0:T(8,128)(2,1)}, bf16[256,512]{1,0:T(8,128)(2,1)S(1)}, u32[]{:S(2)}, u32[]{:S(2)}) collective-permute-start(bf16[256,512]{1,0:T(8,128)(2,1)} %param.9), channel_id=1, source_target_pairs={{0,16},{16,0},{1,17},{17,1},{2,18},{18,2},{3,19},{19,3},{4,20},{20... | collective-permute-start | bytes 786440 | tf_op jit(solution)/shard_map/ppermute | solution.py:55
  6.5 1.4 broadcast_in_dim.10
  8.0 15.2 %all-to-all-start = ((bf16[16,16,512]{2,1,0:T(8,128)(2,1)}), bf16[16,16,512]{2,1,0:T(8,128)(2,1)S(1)}, u32[]{:S(2)}, u32[]{:S(2)}) async-start(bf16[16,16,512]{2,1,0:T(8,128)(2,1)} %broadcast_in_dim.10), calls=%async_computation | async-start | bytes 524288 | tf_op jit(solution)/shard_map/all_to_all | solution.py:35
  23.1 1.2 maximum_select_fusion.5
  24.3 3.4 %collective-permute-start.1 = (bf16[512,512]{1,0:T(8,128)(2,1)S(1)}, bf16[512,512]{1,0:T(8,128)(2,1)S(1)}, u32[]{:S(2)}, u32[]{:S(2)}) collective-permute-start(bf16[512,512]{1,0:T(8,128)(2,1)S(1)} %maximum_select_fusion.5), channel_id=1, source_target_pairs={{0,8},{8,0},{1,9},{9,1},{2,10},{10,2},{3,11},{11,3},{4,12},{12,4},... | collective-permute-start | bytes 1572872 | tf_op jit(solution)/shard_map/ppermute | solution.py:55
  27.8 1.2 maximum_select_fusion.6
  29.0 1.9 %collective-permute-start.3 = (bf16[512,512]{1,0:T(8,128)(2,1)S(1)}, bf16[512,512]{1,0:T(8,128)(2,1)S(1)}, u32[]{:S(2)}, u32[]{:S(2)}) collective-permute-start(bf16[512,512]{1,0:T(8,128)(2,1)S(1)} %maximum_select_fusion.6), channel_id=1, source_target_pairs={{0,8},{8,0},{1,9},{9,1},{2,10},{10,2},{3,11},{11,3},{4,12},{12,4},... | collective-permute-start | bytes 1572872 | tf_op jit(solution)/shard_map/ppermute | solution.py:55
  30.9 1.1 add_convert_fusion.1
  32.0 0.3 maximum_select_fusion
  32.3 0.4 collective-permute-done.3
  32.8 0.8 copy-done.3
  33.6 1.7 convolution_convert_fusion.1
  35.2 0.7 all-to-all-done
  35.9 0.5 fusion.1
  36.4 1.3 conditional.1
  36.6 1.0 branch_0_fun.1
  37.7 6.6 %all-to-all-start.1 = ((bf16[8,32,2048]{2,1,0:T(8,128)(2,1)}), bf16[8,32,2048]{2,1,0:T(8,128)(2,1)S(1)}, u32[]{:S(2)}, u32[]{:S(2)}) async-start(bf16[8,32,2048]{2,1,0:T(8,128)(2,1)} %get-tuple-element.86), calls=%async_computation.1 | async-start | bytes 2097152 | tf_op jit(solution)/shard_map/all_to_all | solution.py:35
  44.3 1.9 %add_convert_fusion = bf16[1024,512]{1,0:T(8,128)(2,1)S(1)} fusion(s32[1024,512]{1,0:T(8,128)} %param.7), kind=kLoop, calls=%fused_computation.1 | loop fusion | flops 1572864 | bytes 3145728 | tf_op jit(solution)/shard_map/convert_element_type | solution.py:130
  46.2 1.1 copy.20
  47.3 7.8 %all-to-all-done.1 = bf16[8,32,2048]{2,1,0:T(8,128)(2,1)S(1)} async-done(((bf16[8,32,2048]{2,1,0:T(8,128)(2,1)}), bf16[8,32,2048]{2,1,0:T(8,128)(2,1)S(1)}, u32[]{:S(2)}, u32[]{:S(2)}) %all-to-all-start.1) | async-done | bytes 1048608 | tf_op jit(solution)/shard_map/all_to_all | solution.py:35
  55.3 14.6 %all_to_all.35 = bf16[8,32,1024]{2,1,0:T(8,128)(2,1)S(1)} all-to-all(bf16[8,32,1024]{2,1,0:T(8,128)(2,1)S(1)} %broadcast_in_dim.11), channel_id=1, replica_groups=mesh['z'=16,'xl'=2,'core'=2,'xh'=2,'y'=4] {'xh','y'}, dimensions={0} | all-to-all | bytes 1048576 | tf_op jit(solution)/shard_map/all_to_all | solution.py:35
  69.9 1.2 convolution_convert_fusion.3
  71.1 12.4 %all-to-all-start.3 = ((bf16[16,16,512]{2,1,0:T(8,128)(2,1)}), bf16[16,16,512]{2,1,0:T(8,128)(2,1)S(1)}, u32[]{:S(2)}, u32[]{:S(2)}) async-start(bf16[16,16,512]{2,1,0:T(8,128)(2,1)} %bitcast.10), calls=%async_computation.3 | async-start | bytes 524288 | tf_op jit(solution)/shard_map/all_to_all | solution.py:35
  83.5 2.3 %collective-permute-start.4 = (bf16[256,512]{1,0:T(8,128)(2,1)S(1)}, bf16[256,512]{1,0:T(8,128)(2,1)S(1)}, u32[]{:S(2)}, u32[]{:S(2)}) collective-permute-start(bf16[256,512]{1,0:T(8,128)(2,1)S(1)} %bitcast.41), channel_id=1, source_target_pairs={{0,16},{16,0},{1,17},{17,1},{2,18},{18,2},{3,19},{19,3},{4,20},{20... | collective-permute-start | bytes 786440 | tf_op jit(solution)/shard_map/ppermute | solution.py:55
  85.8 4.8 %collective-permute-done.4 = bf16[256,512]{1,0:T(8,128)(2,1)S(1)} collective-permute-done((bf16[256,512]{1,0:T(8,128)(2,1)S(1)}, bf16[256,512]{1,0:T(8,128)(2,1)S(1)}, u32[]{:S(2)}, u32[]{:S(2)}) %collective-permute-start.4) | collective-permute-done | bytes 262176 | tf_op jit(solution)/shard_map/ppermute | solution.py:55
  90.8 5.5 %all-to-all-done.3 = bf16[16,16,512]{2,1,0:T(8,128)(2,1)S(1)} async-done(((bf16[16,16,512]{2,1,0:T(8,128)(2,1)}), bf16[16,16,512]{2,1,0:T(8,128)(2,1)S(1)}, u32[]{:S(2)}, u32[]{:S(2)}) %all-to-all-start.3) | async-done | bytes 262176 | tf_op jit(solution)/shard_map/all_to_all | solution.py:35
  96.4 0.7 broadcast_in_dim.12
  97.1 6.2 %all-to-all-start.4 = ((bf16[16,16,512]{2,1,0:T(8,128)(2,1)}), bf16[16,16,512]{2,1,0:T(8,128)(2,1)S(1)}, u32[]{:S(2)}, u32[]{:S(2)}) async-start(bf16[16,16,512]{2,1,0:T(8,128)(2,1)} %broadcast_in_dim.12), calls=%async_computation.4 | async-start | bytes 524288 | tf_op jit(solution)/shard_map/all_to_all | solution.py:35
  103.7 2.3 %collective-permute-start.5 = (bf16[1,256,512]{1,2,0:T(8,128)(2,1)S(1)}, bf16[1,256,512]{1,2,0:T(8,128)(2,1)S(1)}, u32[]{:S(2)}, u32[]{:S(2)}) collective-permute-start(bf16[1,256,512]{1,2,0:T(8,128)(2,1)S(1)} %get-tuple-element.81), channel_id=1, source_target_pairs={{0,16},{16,0},{1,17},{17,1},{2,18},{18,2},{3,19},{19,3},{4,20},{20... | collective-permute-start | bytes 786440 | tf_op jit(solution)/shard_map/ppermute | solution.py:68
  106.0 4.8 %collective-permute-done.5 = bf16[1,256,512]{1,2,0:T(8,128)(2,1)S(1)} collective-permute-done((bf16[1,256,512]{1,2,0:T(8,128)(2,1)S(1)}, bf16[1,256,512]{1,2,0:T(8,128)(2,1)S(1)}, u32[]{:S(2)}, u32[]{:S(2)}) %collective-permute-start.5) | collective-permute-done | bytes 262176 | tf_op jit(solution)/shard_map/ppermute | solution.py:68
  110.9 5.3 %all-to-all-done.4 = bf16[16,16,512]{2,1,0:T(8,128)(2,1)S(1)} async-done(((bf16[16,16,512]{2,1,0:T(8,128)(2,1)}), bf16[16,16,512]{2,1,0:T(8,128)(2,1)S(1)}, u32[]{:S(2)}, u32[]{:S(2)}) %all-to-all-start.4) | async-done | bytes 262176 | tf_op jit(solution)/shard_map/all_to_all | solution.py:35
  116.1 1.2 convolution_convert_fusion
  117.4 3.5 %all-to-all-start.5 = ((bf16[8,32,1024]{2,1,0:T(8,128)(2,1)}), bf16[8,32,1024]{2,1,0:T(8,128)(2,1)S(1)}, u32[]{:S(2)}, u32[]{:S(2)}) async-start(bf16[8,32,1024]{2,1,0:T(8,128)(2,1)} %bitcast.15), calls=%async_computation.5 | async-start | bytes 1048576 | tf_op jit(solution)/shard_map/all_to_all | solution.py:35
  120.9 2.4 %collective-permute-start.6 = (bf16[256,512]{1,0:T(8,128)(2,1)S(1)}, bf16[256,512]{1,0:T(8,128)(2,1)S(1)}, u32[]{:S(2)}, u32[]{:S(2)}) collective-permute-start(bf16[256,512]{1,0:T(8,128)(2,1)S(1)} %bitcast.44), channel_id=1, source_target_pairs={{0,16},{16,0},{1,17},{17,1},{2,18},{18,2},{3,19},{19,3},{4,20},{20... | collective-permute-start | bytes 786440 | tf_op jit(solution)/shard_map/ppermute | solution.py:55
  123.3 4.8 %collective-permute-done.6 = bf16[256,512]{1,0:T(8,128)(2,1)S(1)} collective-permute-done((bf16[256,512]{1,0:T(8,128)(2,1)S(1)}, bf16[256,512]{1,0:T(8,128)(2,1)S(1)}, u32[]{:S(2)}, u32[]{:S(2)}) %collective-permute-start.6) | collective-permute-done | bytes 262176 | tf_op jit(solution)/shard_map/ppermute | solution.py:55
  128.3 1.1 all-to-all-done.5
  129.8 1.1 broadcast_in_dim.13
  130.9 16.4 %all-to-all-start.6 = ((bf16[32,32,512]{2,1,0:T(8,128)(2,1)}), bf16[32,32,512]{2,1,0:T(8,128)(2,1)}, u32[]{:S(2)}, u32[]{:S(2)}) async-start(bf16[32,32,512]{2,1,0:T(8,128)(2,1)} %bitcast.17), calls=%async_computation.6 | async-start | bytes 2097152 | tf_op jit(solution)/shard_map/all_to_all | solution.py:35
  147.3 2.2 %collective-permute-start.7 = (bf16[512,512]{1,0:T(8,128)(2,1)S(1)}, bf16[512,512]{1,0:T(8,128)(2,1)}, u32[]{:S(2)}, u32[]{:S(2)}) collective-permute-start(bf16[512,512]{1,0:T(8,128)(2,1)S(1)} %maximum_select_fusion.9), channel_id=1, source_target_pairs={{0,8},{8,0},{1,9},{9,1},{2,10},{10,2},{3,11},{11,3},{4,12},{12,4},... | collective-permute-start | bytes 1572872 | tf_op jit(solution)/shard_map/ppermute | solution.py:55
  149.6 2.2 %collective-permute-start.9 = (bf16[1,2,256,256]{2,3,1,0:T(8,128)(2,1)S(1)}, bf16[1,2,256,256]{2,3,1,0:T(8,128)(2,1)S(1)}, u32[]{:S(2)}, u32[]{:S(2)}) collective-permute-start(bf16[1,2,256,256]{2,3,1,0:T(8,128)(2,1)S(1)} %get-tuple-element.79), channel_id=1, source_target_pairs={{0,8},{8,0},{1,9},{9,1},{2,10},{10,2},{3,11},{11,3},{4,12},{12,4},... | collective-permute-start | bytes 786440 | tf_op jit(solution)/shard_map/ppermute | solution.py:68
  151.9 2.2 %collective-permute-start.8 = (bf16[512,512]{1,0:T(8,128)(2,1)S(1)}, bf16[512,512]{1,0:T(8,128)(2,1)}, u32[]{:S(2)}, u32[]{:S(2)}) collective-permute-start(bf16[512,512]{1,0:T(8,128)(2,1)S(1)} %maximum_select_fusion.7), channel_id=1, source_target_pairs={{0,8},{8,0},{1,9},{9,1},{2,10},{10,2},{3,11},{11,3},{4,12},{12,4},... | collective-permute-start | bytes 1572872 | tf_op jit(solution)/shard_map/ppermute | solution.py:55
  154.4 1.6 maximum_select_fusion.3
  156.0 2.5 %maximum_select_fusion.4 = bf16[1024,512]{1,0:T(8,128)(2,1)} fusion(bf16[512,512]{1,0:T(8,128)(2,1)} %collective-permute-done.8, bf16[512,512]{1,0:T(8,128)(2,1)S(1)} %maximum_select_fusion.7, pred[]{:T(512)S(6)} %eq.4), kind=kLoop, calls=%fused_computation.18 | loop fusion | flops 4718592 | bytes 2097153 | tf_op jit(solution)/shard_map/jit(_where)/select_n | solution.py:56
  158.6 5.2 %all-to-all-done.6 = bf16[32,32,512]{2,1,0:T(8,128)(2,1)} async-done(((bf16[32,32,512]{2,1,0:T(8,128)(2,1)}), bf16[32,32,512]{2,1,0:T(8,128)(2,1)}, u32[]{:S(2)}, u32[]{:S(2)}) %all-to-all-start.6) | async-done | bytes 1048608 | tf_op jit(solution)/shard_map/all_to_all | solution.py:35
  163.8 2.6 %convolution_multiply_fusion = f32[256,512]{1,0:T(8,128)} fusion(bf16[1024,512]{1,0:T(8,128)(2,1)} %bitcast.50, bf16[1024,512]{1,0:T(8,128)(2,1)} %bitcast.20), kind=kOutput, calls=%fused_computation.5 | convolution fusion | flops 268566528 | bytes 2097152 | tf_op jit(solution)/shard_map/dot_general | solution.py:23
  166.4 1.5 fusion.9
  168.0 1.3 fusion
  (33 shorter events, 1.9 us)
Async XLA Ops:
  0.6 22.5 %collective-permute-start = (bf16[512,256]{1,0:T(8,128)(2,1)}, bf16[512,256]{1,0:T(8,128)(2,1)S(1)}, u32[]{:S(2)}, u32[]{:S(2)}) collective-permute-start(bf16[512,256]{1,0:T(8,128)(2,1)} %param.8), channel_id=1, source_target_pairs={{0,16},{16,0},{1,17},{17,1},{2,18},{18,2},{3,19},{19,3},{4,20},{20... | collective-permute-start | bytes 786440 | tf_op jit(solution)/shard_map/ppermute | solution.py:55
  4.6 23.2 %collective-permute-start.2 = (bf16[256,512]{1,0:T(8,128)(2,1)}, bf16[256,512]{1,0:T(8,128)(2,1)S(1)}, u32[]{:S(2)}, u32[]{:S(2)}) collective-permute-start(bf16[256,512]{1,0:T(8,128)(2,1)} %param.9), channel_id=1, source_target_pairs={{0,16},{16,0},{1,17},{17,1},{2,18},{18,2},{3,19},{19,3},{4,20},{20... | collective-permute-start | bytes 786440 | tf_op jit(solution)/shard_map/ppermute | solution.py:55
  8.0 27.9 %all-to-all-start = ((bf16[16,16,512]{2,1,0:T(8,128)(2,1)}), bf16[16,16,512]{2,1,0:T(8,128)(2,1)S(1)}, u32[]{:S(2)}, u32[]{:S(2)}) async-start(bf16[16,16,512]{2,1,0:T(8,128)(2,1)} %broadcast_in_dim.10), calls=%async_computation | async-start | bytes 524288 | tf_op jit(solution)/shard_map/all_to_all | solution.py:35
  24.3 7.7 %collective-permute-start.1 = (bf16[512,512]{1,0:T(8,128)(2,1)S(1)}, bf16[512,512]{1,0:T(8,128)(2,1)S(1)}, u32[]{:S(2)}, u32[]{:S(2)}) collective-permute-start(bf16[512,512]{1,0:T(8,128)(2,1)S(1)} %maximum_select_fusion.5), channel_id=1, source_target_pairs={{0,8},{8,0},{1,9},{9,1},{2,10},{10,2},{3,11},{11,3},{4,12},{12,4},... | collective-permute-start | bytes 1572872 | tf_op jit(solution)/shard_map/ppermute | solution.py:55
  29.0 3.8 %collective-permute-start.3 = (bf16[512,512]{1,0:T(8,128)(2,1)S(1)}, bf16[512,512]{1,0:T(8,128)(2,1)S(1)}, u32[]{:S(2)}, u32[]{:S(2)}) collective-permute-start(bf16[512,512]{1,0:T(8,128)(2,1)S(1)} %maximum_select_fusion.6), channel_id=1, source_target_pairs={{0,8},{8,0},{1,9},{9,1},{2,10},{10,2},{3,11},{11,3},{4,12},{12,4},... | collective-permute-start | bytes 1572872 | tf_op jit(solution)/shard_map/ppermute | solution.py:55
  32.8 0.8 copy-start.3
  37.7 17.4 %all-to-all-start.1 = ((bf16[8,32,2048]{2,1,0:T(8,128)(2,1)}), bf16[8,32,2048]{2,1,0:T(8,128)(2,1)S(1)}, u32[]{:S(2)}, u32[]{:S(2)}) async-start(bf16[8,32,2048]{2,1,0:T(8,128)(2,1)} %get-tuple-element.86), calls=%async_computation.1 | async-start | bytes 2097152 | tf_op jit(solution)/shard_map/all_to_all | solution.py:35
  71.1 25.2 %all-to-all-start.3 = ((bf16[16,16,512]{2,1,0:T(8,128)(2,1)}), bf16[16,16,512]{2,1,0:T(8,128)(2,1)S(1)}, u32[]{:S(2)}, u32[]{:S(2)}) async-start(bf16[16,16,512]{2,1,0:T(8,128)(2,1)} %bitcast.10), calls=%async_computation.3 | async-start | bytes 524288 | tf_op jit(solution)/shard_map/all_to_all | solution.py:35
  83.5 7.1 %collective-permute-start.4 = (bf16[256,512]{1,0:T(8,128)(2,1)S(1)}, bf16[256,512]{1,0:T(8,128)(2,1)S(1)}, u32[]{:S(2)}, u32[]{:S(2)}) collective-permute-start(bf16[256,512]{1,0:T(8,128)(2,1)S(1)} %bitcast.41), channel_id=1, source_target_pairs={{0,16},{16,0},{1,17},{17,1},{2,18},{18,2},{3,19},{19,3},{4,20},{20... | collective-permute-start | bytes 786440 | tf_op jit(solution)/shard_map/ppermute | solution.py:55
  97.1 19.0 %all-to-all-start.4 = ((bf16[16,16,512]{2,1,0:T(8,128)(2,1)}), bf16[16,16,512]{2,1,0:T(8,128)(2,1)S(1)}, u32[]{:S(2)}, u32[]{:S(2)}) async-start(bf16[16,16,512]{2,1,0:T(8,128)(2,1)} %broadcast_in_dim.12), calls=%async_computation.4 | async-start | bytes 524288 | tf_op jit(solution)/shard_map/all_to_all | solution.py:35
  103.7 7.1 %collective-permute-start.5 = (bf16[1,256,512]{1,2,0:T(8,128)(2,1)S(1)}, bf16[1,256,512]{1,2,0:T(8,128)(2,1)S(1)}, u32[]{:S(2)}, u32[]{:S(2)}) collective-permute-start(bf16[1,256,512]{1,2,0:T(8,128)(2,1)S(1)} %get-tuple-element.81), channel_id=1, source_target_pairs={{0,16},{16,0},{1,17},{17,1},{2,18},{18,2},{3,19},{19,3},{4,20},{20... | collective-permute-start | bytes 786440 | tf_op jit(solution)/shard_map/ppermute | solution.py:68
  117.4 12.1 %all-to-all-start.5 = ((bf16[8,32,1024]{2,1,0:T(8,128)(2,1)}), bf16[8,32,1024]{2,1,0:T(8,128)(2,1)S(1)}, u32[]{:S(2)}, u32[]{:S(2)}) async-start(bf16[8,32,1024]{2,1,0:T(8,128)(2,1)} %bitcast.15), calls=%async_computation.5 | async-start | bytes 1048576 | tf_op jit(solution)/shard_map/all_to_all | solution.py:35
  120.9 7.2 %collective-permute-start.6 = (bf16[256,512]{1,0:T(8,128)(2,1)S(1)}, bf16[256,512]{1,0:T(8,128)(2,1)S(1)}, u32[]{:S(2)}, u32[]{:S(2)}) collective-permute-start(bf16[256,512]{1,0:T(8,128)(2,1)S(1)} %bitcast.44), channel_id=1, source_target_pairs={{0,16},{16,0},{1,17},{17,1},{2,18},{18,2},{3,19},{19,3},{4,20},{20... | collective-permute-start | bytes 786440 | tf_op jit(solution)/shard_map/ppermute | solution.py:55
  128.3 19.0 %copy-start = (bf16[512,512]{1,0:T(8,128)(2,1)}, bf16[512,512]{1,0:T(8,128)(2,1)S(1)}, u32[]{:S(2)}) copy-start(bf16[512,512]{1,0:T(8,128)(2,1)S(1)} %maximum_select_fusion.9) | copy-start | bytes 1572868
  130.9 32.9 %all-to-all-start.6 = ((bf16[32,32,512]{2,1,0:T(8,128)(2,1)}), bf16[32,32,512]{2,1,0:T(8,128)(2,1)}, u32[]{:S(2)}, u32[]{:S(2)}) async-start(bf16[32,32,512]{2,1,0:T(8,128)(2,1)} %bitcast.17), calls=%async_computation.6 | async-start | bytes 2097152 | tf_op jit(solution)/shard_map/all_to_all | solution.py:35
  147.3 7.1 %collective-permute-start.7 = (bf16[512,512]{1,0:T(8,128)(2,1)S(1)}, bf16[512,512]{1,0:T(8,128)(2,1)}, u32[]{:S(2)}, u32[]{:S(2)}) collective-permute-start(bf16[512,512]{1,0:T(8,128)(2,1)S(1)} %maximum_select_fusion.9), channel_id=1, source_target_pairs={{0,8},{8,0},{1,9},{9,1},{2,10},{10,2},{3,11},{11,3},{4,12},{12,4},... | collective-permute-start | bytes 1572872 | tf_op jit(solution)/shard_map/ppermute | solution.py:55
  149.6 4.9 %copy-start.1 = (bf16[512,512]{1,0:T(8,128)(2,1)S(1)}, bf16[512,512]{1,0:T(8,128)(2,1)}, u32[]{:S(2)}) copy-start(bf16[512,512]{1,0:T(8,128)(2,1)} %copy-done) | copy-start | bytes 1572868
  149.6 4.5 %collective-permute-start.9 = (bf16[1,2,256,256]{2,3,1,0:T(8,128)(2,1)S(1)}, bf16[1,2,256,256]{2,3,1,0:T(8,128)(2,1)S(1)}, u32[]{:S(2)}, u32[]{:S(2)}) collective-permute-start(bf16[1,2,256,256]{2,3,1,0:T(8,128)(2,1)S(1)} %get-tuple-element.79), channel_id=1, source_target_pairs={{0,8},{8,0},{1,9},{9,1},{2,10},{10,2},{3,11},{11,3},{4,12},{12,4},... | collective-permute-start | bytes 786440 | tf_op jit(solution)/shard_map/ppermute | solution.py:68
  151.9 4.1 %collective-permute-start.8 = (bf16[512,512]{1,0:T(8,128)(2,1)S(1)}, bf16[512,512]{1,0:T(8,128)(2,1)}, u32[]{:S(2)}, u32[]{:S(2)}) collective-permute-start(bf16[512,512]{1,0:T(8,128)(2,1)S(1)} %maximum_select_fusion.7), channel_id=1, source_target_pairs={{0,8},{8,0},{1,9},{9,1},{2,10},{10,2},{3,11},{11,3},{4,12},{12,4},... | collective-permute-start | bytes 1572872 | tf_op jit(solution)/shard_map/ppermute | solution.py:55
  158.6 7.9 %copy-start.2 = (bf16[1024,512]{1,0:T(8,128)(2,1)S(1)}, bf16[1024,512]{1,0:T(8,128)(2,1)}, u32[]{:S(2)}) copy-start(bf16[1024,512]{1,0:T(8,128)(2,1)} %maximum_select_fusion.4) | copy-start | bytes 3145732

commit v8 on v7

--- a/solution.py
+++ b/solution.py
@@ -99,6 +99,58 @@
             flops=0, bytes_accessed=8 * rows * cols, transcendentals=0
         ),
     )(left, right)
+
+
+def last_products(tokens, jac, terms, gated, signs, factor):
+    rows, hid = gated.shape
+    feats = tokens.shape[1]
+
+    def kernel(
+        tokens, jac, terms, gated, signs, grad_in, grad_out,
+        terms_here, gated_here, in_here, out_here, sem,
+    ):
+        get_gated = pltpu.make_async_copy(gated, gated_here, sem.at[0])
+        get_terms = pltpu.make_async_copy(terms, terms_here, sem.at[1])
+        get_gated.start()
+        get_terms.start()
+        get_gated.wait()
+        in_here[...] = contract_rows(jac[...], gated_here[...])
+        get_terms.wait()
+        in_here[...] = factor * (
+            in_here[...] + contract_rows(tokens[...], terms_here[:, :hid])
+        )
+        put_in = pltpu.make_async_copy(in_here, grad_in, sem.at[2])
+        put_in.start()
+        out_here[...] = factor * contract_rows(terms_here[:, hid:], signs[...])
+        put_out = pltpu.make_async_copy(out_here, grad_out, sem.at[3])
+        put_out.start()
+        put_in.wait()
+        put_out.wait()
+
+    whole = pl.BlockSpec(memory_space=pltpu.VMEM)
+    anywhere = pl.BlockSpec(memory_space=pl.ANY)
+    return pl.pallas_call(
+        kernel,
+        out_shape=(
+            jax.ShapeDtypeStruct((feats, hid), F32),
+            jax.ShapeDtypeStruct((hid, feats), F32),
+        ),
+        in_specs=[whole, whole, anywhere, anywhere, whole],
+        out_specs=(anywhere, anywhere),
+        scratch_shapes=[
+            pltpu.VMEM((rows, 2 * hid), BF),
+            pltpu.VMEM((rows, hid), BF),
+            pltpu.VMEM((feats, hid), F32),
+            pltpu.VMEM((hid, feats), F32),
+            pltpu.SemaphoreType.DMA((4,)),
+        ],
+        compiler_params=pltpu.CompilerParams(vmem_limit_bytes=16 * 2**20),
+        cost_estimate=pl.CostEstimate(
+            flops=6 * rows * hid * feats,
+            bytes_accessed=8 * rows * feats + 4 * rows * hid + 8 * hid * feats,
+            transcendentals=0,
+        ),
+    )(tokens, jac, terms, gated, signs)
 
 
 def on_device(tokens, probe_draw, w_in, w_out):
@@ -154,8 +206,8 @@
     slope_own = (back_proj * slopes).astype(BF).reshape(rows, nn, hid)
     terms = jnp.concatenate([curv_own, slope_own], axis=2).transpose(1, 0, 2)
     terms = jnp.broadcast_to(terms[:, None], (nn, nc, rows, 2 * hid))
-    terms, jac_pair, gated_pair, token_pair = tie(
-        terms.reshape(nn * nc, rows, 2 * hid), jac_pair, gated_pair, token_pair
+    terms, gated_pair, token_pair = tie(
+        terms.reshape(nn * nc, rows, 2 * hid), gated_pair, token_pair
     )
     jac_all = pair_up(jac_pair, "core", 0)
     all_tokens = pair_up(token_pair, "core", 0)
@@ -164,13 +216,9 @@
         exchange(terms, NEAR + COL), jac_all, all_tokens, gated_hid
     )
     terms = terms.reshape(total_rows, 2 * hid)
-    curv_term, slope_term = terms[:, :hid], terms[:, hid:]
-    factor = 1.0 / jnp.sqrt(jnp.float32(total_rows))
-    grad_in = factor * (
-        contract_rows(all_tokens, curv_term) + contract_rows(jac_all, gated_hid)
-    )
-    grad_out = factor * contract_rows(slope_term, sign_all)
-    return (grad_in, grad_out)
+    return last_products(
+        all_tokens, jac_all, terms, gated_hid, sign_all, total_rows**-0.5
+    )
 
 
 def solution(mesh):

time: 172 us -> 169 us (0.983)
  matrix products: 10 us -> 4.66 us
  Pallas kernels: 1.03 us -> 4.03 us
  local copies, waits for them, and re-layouts: 5.94 us -> 7.8 us
    dot_general x3 -> x0, matrix products: 5.43 us -> none  [contract_rows(): lax.dot_general(left, right, (((0,), (0,)), ((), ())), preferred_element_...]
    ppermute x8, waiting for transfers between devices: 10 us -> 5.36 us  [pair_up(): far = lax.ppermute(array, name, [(0, 1), (1, 0)])]
    all_to_all x6, waiting for transfers between devices: 25.6 us -> 29.9 us  [exchange(): return lax.all_to_all(blocks, axes, 0, 0, tiled=True)]
    pallas_call x0 -> x1, Pallas kernels: none -> 2.99 us  [last_products(): pl.pallas_call(kernel, out_shape=(jax.ShapeDtypeStruct((feats, hid), F32)...]
  transfers between devices with their start and end apart: 16 -> 16, of which waited for: 10 -> 9; matrix products, arithmetic and copies ran while one was open for 9% -> 11% of each run, Pallas kernels for 0% -> 0%
where the time goes in v8:
time: 169 us; the launch traced here: 167 us
  starting transfers between devices  83.8 us (50%)
  waiting for transfers between devices  40 us (24%)
  blocking collectives  14 us (8%)
  other arithmetic  12.2 us (7%)
  local copies, waits for them, and re-layouts  7.8 us (5%)
  matrix products  4.66 us (3%)
  Pallas kernels  4.03 us (2%)
    all_to_all x6, starting transfers between devices, exchange(): return lax.all_to_all(blocks, axes, 0, 0, tiled=True)  59 us
    all_to_all x6, waiting for transfers between devices, exchange(): return lax.all_to_all(blocks, axes, 0, 0, tiled=True)  29.9 us
    ppermute x8, starting transfers between devices, pair_up(): far = lax.ppermute(array, name, [(0, 1), (1, 0)])  20.3 us
    all_to_all x1, blocking collectives, exchange(): return lax.all_to_all(blocks, axes, 0, 0, tiled=True)  14 us
    select_n x7, other arithmetic, pair_up(): jnp.where(lax.axis_index(name) == 0, jnp.concatenate([array, far], axis=a...  7.26 us
    ppermute x8, waiting for transfers between devices, pair_up(): far = lax.ppermute(array, name, [(0, 1), (1, 0)])  5.36 us
    ppermute x2, waiting for transfers between devices, hand_over(): far = lax.ppermute(jnp.where(first, right, left), name, [(0, 1), (1, 0)])  4.79 us
    ppermute x2, starting transfers between devices, hand_over(): far = lax.ppermute(jnp.where(first, right, left), name, [(0, 1), (1, 0)])  4.42 us
  transfers between devices with their start and end apart: 16, of which 9 were waited for; matrix products, arithmetic and copies ran while one was open for 11% of the time, Pallas kernels for 0%

profile of v8, /device:TPU:1, one launch (start us, length us, event | category | flops | bytes accessed | tf_op | source)
XLA Modules:
  0.0 167.4 jit_solution(17950774765908735598)
XLA Ops:
  0.6 4.0 %collective-permute-start = (bf16[512,256]{1,0:T(8,128)(2,1)}, bf16[512,256]{1,0:T(8,128)(2,1)S(1)}, u32[]{:S(2)}, u32[]{:S(2)}) collective-permute-start(bf16[512,256]{1,0:T(8,128)(2,1)} %param.8), channel_id=1, source_target_pairs={{0,16},{16,0},{1,17},{17,1},{2,18},{18,2},{3,19},{19,3},{4,20},{20... | collective-permute-start | bytes 786440 | tf_op jit(solution)/shard_map/ppermute | solution.py:55
  4.6 1.9 %collective-permute-start.2 = (bf16[256,512]{1,0:T(8,128)(2,1)}, bf16[256,512]{1,0:T(8,128)(2,1)S(1)}, u32[]{:S(2)}, u32[]{:S(2)}) collective-permute-start(bf16[256,512]{1,0:T(8,128)(2,1)} %param.9), channel_id=1, source_target_pairs={{0,16},{16,0},{1,17},{17,1},{2,18},{18,2},{3,19},{19,3},{4,20},{20... | collective-permute-start | bytes 786440 | tf_op jit(solution)/shard_map/ppermute | solution.py:55
  6.5 1.4 broadcast_in_dim.10
  8.0 15.2 %all-to-all-start = ((bf16[16,16,512]{2,1,0:T(8,128)(2,1)}), bf16[16,16,512]{2,1,0:T(8,128)(2,1)S(1)}, u32[]{:S(2)}, u32[]{:S(2)}) async-start(bf16[16,16,512]{2,1,0:T(8,128)(2,1)} %broadcast_in_dim.10), calls=%async_computation | async-start | bytes 524288 | tf_op jit(solution)/shard_map/all_to_all | solution.py:35
  23.1 1.2 maximum_select_fusion.5
  24.3 3.4 %collective-permute-start.1 = (bf16[512,512]{1,0:T(8,128)(2,1)S(1)}, bf16[512,512]{1,0:T(8,128)(2,1)S(1)}, u32[]{:S(2)}, u32[]{:S(2)}) collective-permute-start(bf16[512,512]{1,0:T(8,128)(2,1)S(1)} %maximum_select_fusion.5), channel_id=1, source_target_pairs={{0,8},{8,0},{1,9},{9,1},{2,10},{10,2},{3,11},{11,3},{4,12},{12,4},... | collective-permute-start | bytes 1572872 | tf_op jit(solution)/shard_map/ppermute | solution.py:55
  27.7 1.2 maximum_select_fusion.6
  29.0 1.9 %collective-permute-start.3 = (bf16[512,512]{1,0:T(8,128)(2,1)S(1)}, bf16[512,512]{1,0:T(8,128)(2,1)}, u32[]{:S(2)}, u32[]{:S(2)}) collective-permute-start(bf16[512,512]{1,0:T(8,128)(2,1)S(1)} %maximum_select_fusion.6), channel_id=1, source_target_pairs={{0,8},{8,0},{1,9},{9,1},{2,10},{10,2},{3,11},{11,3},{4,12},{12,4},... | collective-permute-start | bytes 1572872 | tf_op jit(solution)/shard_map/ppermute | solution.py:55
  30.9 1.1 add_convert_fusion.1
  32.3 0.6 collective-permute-done.3
  32.9 1.8 %convolution_convert_fusion.1 = bf16[256,1024]{1,0:T(8,128)(2,1)S(1)} fusion(bf16[256,512]{1,0:T(8,128)(2,1)S(1)} %bitcast.47, bf16[512,512]{1,0:T(8,128)(2,1)} %collective-permute-done.3, bf16[512,512]{1,0:T(8,128)(2,1)S(1)} %maximum_select_fusion.6, pred[]{:T(512)S(6)} %eq.4), kind=kOutput, calls=%fused_computation.3 | convolution fusion | flops 273416192 | bytes 1835009 | tf_op jit(solution)/shard_map/dot_general | solution.py:29
  34.7 1.3 all-to-all-done
  35.9 0.5 fusion
  36.4 1.3 conditional.1
  36.6 1.0 branch_0_fun.1
  37.7 6.6 %all-to-all-start.1 = ((bf16[8,32,2048]{2,1,0:T(8,128)(2,1)}), bf16[8,32,2048]{2,1,0:T(8,128)(2,1)}, u32[]{:S(2)}, u32[]{:S(2)}) async-start(bf16[8,32,2048]{2,1,0:T(8,128)(2,1)} %get-tuple-element.80), calls=%async_computation.1 | async-start | bytes 2097152 | tf_op jit(solution)/shard_map/all_to_all | solution.py:35
  44.3 1.9 %add_convert_fusion = bf16[1024,512]{1,0:T(8,128)(2,1)S(1)} fusion(s32[1024,512]{1,0:T(8,128)} %param.7), kind=kLoop, calls=%fused_computation.1 | loop fusion | flops 1572864 | bytes 3145728 | tf_op jit(solution)/shard_map/convert_element_type | solution.py:182
  46.3 8.9 %all-to-all-done.1 = bf16[8,32,2048]{2,1,0:T(8,128)(2,1)} async-done(((bf16[8,32,2048]{2,1,0:T(8,128)(2,1)}), bf16[8,32,2048]{2,1,0:T(8,128)(2,1)}, u32[]{:S(2)}, u32[]{:S(2)}) %all-to-all-start.1) | async-done | bytes 1048608 | tf_op jit(solution)/shard_map/all_to_all | solution.py:35
  55.2 1.4 convert_reduce_fusion
  56.7 14.0 %all_to_all.35 = bf16[8,32,1024]{2,1,0:T(8,128)(2,1)S(1)} all-to-all(bf16[8,32,1024]{2,1,0:T(8,128)(2,1)S(1)} %broadcast_in_dim.11), channel_id=1, replica_groups=mesh['z'=16,'xl'=2,'core'=2,'xh'=2,'y'=4] {'xh','y'}, dimensions={0} | all-to-all | bytes 1048576 | tf_op jit(solution)/shard_map/all_to_all | solution.py:35
  70.7 1.2 convolution_convert_fusion.3
  71.9 13.0 %all-to-all-start.3 = ((bf16[16,16,512]{2,1,0:T(8,128)(2,1)}), bf16[16,16,512]{2,1,0:T(8,128)(2,1)S(1)}, u32[]{:S(2)}, u32[]{:S(2)}) async-start(bf16[16,16,512]{2,1,0:T(8,128)(2,1)} %bitcast.10), calls=%async_computation.3 | async-start | bytes 524288 | tf_op jit(solution)/shard_map/all_to_all | solution.py:35
  84.9 2.3 %collective-permute-start.4 = (bf16[256,512]{1,0:T(8,128)(2,1)S(1)}, bf16[256,512]{1,0:T(8,128)(2,1)S(1)}, u32[]{:S(2)}, u32[]{:S(2)}) collective-permute-start(bf16[256,512]{1,0:T(8,128)(2,1)S(1)} %bitcast.39), channel_id=1, source_target_pairs={{0,16},{16,0},{1,17},{17,1},{2,18},{18,2},{3,19},{19,3},{4,20},{20... | collective-permute-start | bytes 786440 | tf_op jit(solution)/shard_map/ppermute | solution.py:55
  87.2 4.8 %collective-permute-done.4 = bf16[256,512]{1,0:T(8,128)(2,1)S(1)} collective-permute-done((bf16[256,512]{1,0:T(8,128)(2,1)S(1)}, bf16[256,512]{1,0:T(8,128)(2,1)S(1)}, u32[]{:S(2)}, u32[]{:S(2)}) %collective-permute-start.4) | collective-permute-done | bytes 262176 | tf_op jit(solution)/shard_map/ppermute | solution.py:55
  92.0 1.0 maximum_select_fusion.7
  93.0 4.7 %all-to-all-done.3 = bf16[16,16,512]{2,1,0:T(8,128)(2,1)S(1)} async-done(((bf16[16,16,512]{2,1,0:T(8,128)(2,1)}), bf16[16,16,512]{2,1,0:T(8,128)(2,1)S(1)}, u32[]{:S(2)}, u32[]{:S(2)}) %all-to-all-start.3) | async-done | bytes 262176 | tf_op jit(solution)/shard_map/all_to_all | solution.py:35
  97.7 0.7 broadcast_in_dim.12
  98.5 7.0 %all-to-all-start.4 = ((bf16[16,16,512]{2,1,0:T(8,128)(2,1)}), bf16[16,16,512]{2,1,0:T(8,128)(2,1)S(1)}, u32[]{:S(2)}, u32[]{:S(2)}) async-start(bf16[16,16,512]{2,1,0:T(8,128)(2,1)} %broadcast_in_dim.12), calls=%async_computation.4 | async-start | bytes 524288 | tf_op jit(solution)/shard_map/all_to_all | solution.py:35
  105.5 1.0 copy.17
  106.5 1.1 copy.18
  107.6 2.3 %collective-permute-start.5 = (bf16[1,256,512]{1,2,0:T(8,128)(2,1)S(1)}, bf16[1,256,512]{1,2,0:T(8,128)(2,1)S(1)}, u32[]{:S(2)}, u32[]{:S(2)}) collective-permute-start(bf16[1,256,512]{1,2,0:T(8,128)(2,1)S(1)} %get-tuple-element.75), channel_id=1, source_target_pairs={{0,16},{16,0},{1,17},{17,1},{2,18},{18,2},{3,19},{19,3},{4,20},{20... | collective-permute-start | bytes 786440 | tf_op jit(solution)/shard_map/ppermute | solution.py:68
  110.0 4.8 %collective-permute-done.5 = bf16[1,256,512]{1,2,0:T(8,128)(2,1)S(1)} collective-permute-done((bf16[1,256,512]{1,2,0:T(8,128)(2,1)S(1)}, bf16[1,256,512]{1,2,0:T(8,128)(2,1)S(1)}, u32[]{:S(2)}, u32[]{:S(2)}) %collective-permute-start.5) | collective-permute-done | bytes 262176 | tf_op jit(solution)/shard_map/ppermute | solution.py:68
  114.8 3.5 %all-to-all-done.4 = bf16[16,16,512]{2,1,0:T(8,128)(2,1)S(1)} async-done(((bf16[16,16,512]{2,1,0:T(8,128)(2,1)}), bf16[16,16,512]{2,1,0:T(8,128)(2,1)S(1)}, u32[]{:S(2)}, u32[]{:S(2)}) %all-to-all-start.4) | async-done | bytes 262176 | tf_op jit(solution)/shard_map/all_to_all | solution.py:35
  118.4 1.2 convolution_convert_fusion
  119.6 3.5 %all-to-all-start.5 = ((bf16[8,32,1024]{2,1,0:T(8,128)(2,1)}), bf16[8,32,1024]{2,1,0:T(8,128)(2,1)S(1)}, u32[]{:S(2)}, u32[]{:S(2)}) async-start(bf16[8,32,1024]{2,1,0:T(8,128)(2,1)} %bitcast.15), calls=%async_computation.5 | async-start | bytes 1048576 | tf_op jit(solution)/shard_map/all_to_all | solution.py:35
  123.1 2.3 %collective-permute-start.6 = (bf16[256,512]{1,0:T(8,128)(2,1)S(1)}, bf16[256,512]{1,0:T(8,128)(2,1)S(1)}, u32[]{:S(2)}, u32[]{:S(2)}) collective-permute-start(bf16[256,512]{1,0:T(8,128)(2,1)S(1)} %bitcast.42), channel_id=1, source_target_pairs={{0,16},{16,0},{1,17},{17,1},{2,18},{18,2},{3,19},{19,3},{4,20},{20... | collective-permute-start | bytes 786440 | tf_op jit(solution)/shard_map/ppermute | solution.py:55
  125.4 6.2 %all-to-all-done.5 = bf16[8,32,1024]{2,1,0:T(8,128)(2,1)S(1)} async-done(((bf16[8,32,1024]{2,1,0:T(8,128)(2,1)}), bf16[8,32,1024]{2,1,0:T(8,128)(2,1)S(1)}, u32[]{:S(2)}, u32[]{:S(2)}) %all-to-all-start.5) | async-done | bytes 524320 | tf_op jit(solution)/shard_map/all_to_all | solution.py:35
  132.0 1.1 broadcast_in_dim.13
  133.1 13.7 %all-to-all-start.6 = ((bf16[32,32,512]{2,1,0:T(8,128)(2,1)}), bf16[32,32,512]{2,1,0:T(8,128)(2,1)}, u32[]{:S(2)}, u32[]{:S(2)}) async-start(bf16[32,32,512]{2,1,0:T(8,128)(2,1)} %bitcast.17), calls=%async_computation.6 | async-start | bytes 2097152 | tf_op jit(solution)/shard_map/all_to_all | solution.py:35
  147.1 2.2 %collective-permute-start.7 = (bf16[512,512]{1,0:T(8,128)(2,1)S(1)}, bf16[512,512]{1,0:T(8,128)(2,1)}, u32[]{:S(2)}, u32[]{:S(2)}) collective-permute-start(bf16[512,512]{1,0:T(8,128)(2,1)S(1)} %maximum_select_fusion.9), channel_id=1, source_target_pairs={{0,8},{8,0},{1,9},{9,1},{2,10},{10,2},{3,11},{11,3},{4,12},{12,4},... | collective-permute-start | bytes 1572872 | tf_op jit(solution)/shard_map/ppermute | solution.py:55
  149.3 2.1 %collective-permute-start.9 = (bf16[1,2,256,256]{2,3,1,0:T(8,128)(2,1)S(1)}, bf16[1,2,256,256]{2,3,1,0:T(8,128)(2,1)S(1)}, u32[]{:S(2)}, u32[]{:S(2)}) collective-permute-start(bf16[1,2,256,256]{2,3,1,0:T(8,128)(2,1)S(1)} %get-tuple-element.73), channel_id=1, source_target_pairs={{0,8},{8,0},{1,9},{9,1},{2,10},{10,2},{3,11},{11,3},{4,12},{12,4},... | collective-permute-start | bytes 786440 | tf_op jit(solution)/shard_map/ppermute | solution.py:68
  151.5 2.2 %collective-permute-start.8 = (bf16[512,512]{1,0:T(8,128)(2,1)S(1)}, bf16[512,512]{1,0:T(8,128)(2,1)}, u32[]{:S(2)}, u32[]{:S(2)}) collective-permute-start(bf16[512,512]{1,0:T(8,128)(2,1)S(1)} %copy-done.1), channel_id=1, source_target_pairs={{0,8},{8,0},{1,9},{9,1},{2,10},{10,2},{3,11},{11,3},{4,12},{12,4},... | collective-permute-start | bytes 1572872 | tf_op jit(solution)/shard_map/ppermute | solution.py:55
  153.8 1.0 copy.20
  154.8 1.6 maximum_select_fusion.3.jac
  156.4 1.8 %maximum_select_fusion.4.tokens = bf16[1024,512]{1,0:T(8,128)(2,1)S(1)} fusion(bf16[512,512]{1,0:T(8,128)(2,1)} %collective-permute-done.8, bf16[512,512]{1,0:T(8,128)(2,1)} %maximum_select_fusion.7, pred[]{:T(512)S(6)} %eq.4), kind=kLoop, calls=%fused_computation.15 | loop fusion | flops 4718592 | bytes 2097153 | tf_op jit(solution)/shard_map/jit(_where)/select_n | solution.py:56
  158.2 5.2 %all-to-all-done.6 = bf16[32,32,512]{2,1,0:T(8,128)(2,1)} async-done(((bf16[32,32,512]{2,1,0:T(8,128)(2,1)}), bf16[32,32,512]{2,1,0:T(8,128)(2,1)}, u32[]{:S(2)}, u32[]{:S(2)}) %all-to-all-start.6) | async-done | bytes 1048608 | tf_op jit(solution)/shard_map/all_to_all | solution.py:35
  163.4 1.0 copy-done
  164.5 3.0 %shard_map.59 = (f32[512,256]{1,0:T(8,128)}, f32[256,512]{1,0:T(8,128)}) custom-call(bf16[1024,512]{1,0:T(8,128)(2,1)S(1)} %maximum_select_fusion.4.tokens, bf16[1024,512]{1,0:T(8,128)(2,1)S(1)} %maximum_select_fusion.3.jac, bf16[1024,512]{1,0:T(8,128)(2,1)} %bitcast.20.terms, bf16[1024,256]{1,0:T(8,128)(2,1)S(1)} %bitcast.33, bf16[1024,512]{1,0:T(8,128)(2,1)S(1)} %bitcast.32), custom_call_target="tpu_custom_call" | custom-call | flops 805306368 | bytes 6291456 | tf_op jit(solution)/shard_map/pallas_call | solution.py:132
  (27 shorter events, 1.5 us)
Async XLA Ops:
  0.6 22.5 %collective-permute-start = (bf16[512,256]{1,0:T(8,128)(2,1)}, bf16[512,256]{1,0:T(8,128)(2,1)S(1)}, u32[]{:S(2)}, u32[]{:S(2)}) collective-permute-start(bf16[512,256]{1,0:T(8,128)(2,1)} %param.8), channel_id=1, source_target_pairs={{0,16},{16,0},{1,17},{17,1},{2,18},{18,2},{3,19},{19,3},{4,20},{20... | collective-permute-start | bytes 786440 | tf_op jit(solution)/shard_map/ppermute | solution.py:55
  4.6 23.2 %collective-permute-start.2 = (bf16[256,512]{1,0:T(8,128)(2,1)}, bf16[256,512]{1,0:T(8,128)(2,1)S(1)}, u32[]{:S(2)}, u32[]{:S(2)}) collective-permute-start(bf16[256,512]{1,0:T(8,128)(2,1)} %param.9), channel_id=1, source_target_pairs={{0,16},{16,0},{1,17},{17,1},{2,18},{18,2},{3,19},{19,3},{4,20},{20... | collective-permute-start | bytes 786440 | tf_op jit(solution)/shard_map/ppermute | solution.py:55
  8.0 27.9 %all-to-all-start = ((bf16[16,16,512]{2,1,0:T(8,128)(2,1)}), bf16[16,16,512]{2,1,0:T(8,128)(2,1)S(1)}, u32[]{:S(2)}, u32[]{:S(2)}) async-start(bf16[16,16,512]{2,1,0:T(8,128)(2,1)} %broadcast_in_dim.10), calls=%async_computation | async-start | bytes 524288 | tf_op jit(solution)/shard_map/all_to_all | solution.py:35
  24.3 7.7 %collective-permute-start.1 = (bf16[512,512]{1,0:T(8,128)(2,1)S(1)}, bf16[512,512]{1,0:T(8,128)(2,1)S(1)}, u32[]{:S(2)}, u32[]{:S(2)}) collective-permute-start(bf16[512,512]{1,0:T(8,128)(2,1)S(1)} %maximum_select_fusion.5), channel_id=1, source_target_pairs={{0,8},{8,0},{1,9},{9,1},{2,10},{10,2},{3,11},{11,3},{4,12},{12,4},... | collective-permute-start | bytes 1572872 | tf_op jit(solution)/shard_map/ppermute | solution.py:55
  29.0 3.9 %collective-permute-start.3 = (bf16[512,512]{1,0:T(8,128)(2,1)S(1)}, bf16[512,512]{1,0:T(8,128)(2,1)}, u32[]{:S(2)}, u32[]{:S(2)}) collective-permute-start(bf16[512,512]{1,0:T(8,128)(2,1)S(1)} %maximum_select_fusion.6), channel_id=1, source_target_pairs={{0,8},{8,0},{1,9},{9,1},{2,10},{10,2},{3,11},{11,3},{4,12},{12,4},... | collective-permute-start | bytes 1572872 | tf_op jit(solution)/shard_map/ppermute | solution.py:55
  37.7 17.5 %all-to-all-start.1 = ((bf16[8,32,2048]{2,1,0:T(8,128)(2,1)}), bf16[8,32,2048]{2,1,0:T(8,128)(2,1)}, u32[]{:S(2)}, u32[]{:S(2)}) async-start(bf16[8,32,2048]{2,1,0:T(8,128)(2,1)} %get-tuple-element.80), calls=%async_computation.1 | async-start | bytes 2097152 | tf_op jit(solution)/shard_map/all_to_all | solution.py:35
  71.9 25.8 %all-to-all-start.3 = ((bf16[16,16,512]{2,1,0:T(8,128)(2,1)}), bf16[16,16,512]{2,1,0:T(8,128)(2,1)S(1)}, u32[]{:S(2)}, u32[]{:S(2)}) async-start(bf16[16,16,512]{2,1,0:T(8,128)(2,1)} %bitcast.10), calls=%async_computation.3 | async-start | bytes 524288 | tf_op jit(solution)/shard_map/all_to_all | solution.py:35
  84.9 7.1 %collective-permute-start.4 = (bf16[256,512]{1,0:T(8,128)(2,1)S(1)}, bf16[256,512]{1,0:T(8,128)(2,1)S(1)}, u32[]{:S(2)}, u32[]{:S(2)}) collective-permute-start(bf16[256,512]{1,0:T(8,128)(2,1)S(1)} %bitcast.39), channel_id=1, source_target_pairs={{0,16},{16,0},{1,17},{17,1},{2,18},{18,2},{3,19},{19,3},{4,20},{20... | collective-permute-start | bytes 786440 | tf_op jit(solution)/shard_map/ppermute | solution.py:55
  98.5 19.9 %all-to-all-start.4 = ((bf16[16,16,512]{2,1,0:T(8,128)(2,1)}), bf16[16,16,512]{2,1,0:T(8,128)(2,1)S(1)}, u32[]{:S(2)}, u32[]{:S(2)}) async-start(bf16[16,16,512]{2,1,0:T(8,128)(2,1)} %broadcast_in_dim.12), calls=%async_computation.4 | async-start | bytes 524288 | tf_op jit(solution)/shard_map/all_to_all | solution.py:35
  107.6 7.1 %collective-permute-start.5 = (bf16[1,256,512]{1,2,0:T(8,128)(2,1)S(1)}, bf16[1,256,512]{1,2,0:T(8,128)(2,1)S(1)}, u32[]{:S(2)}, u32[]{:S(2)}) collective-permute-start(bf16[1,256,512]{1,2,0:T(8,128)(2,1)S(1)} %get-tuple-element.75), channel_id=1, source_target_pairs={{0,16},{16,0},{1,17},{17,1},{2,18},{18,2},{3,19},{19,3},{4,20},{20... | collective-permute-start | bytes 786440 | tf_op jit(solution)/shard_map/ppermute | solution.py:68
  119.6 12.1 %all-to-all-start.5 = ((bf16[8,32,1024]{2,1,0:T(8,128)(2,1)}), bf16[8,32,1024]{2,1,0:T(8,128)(2,1)S(1)}, u32[]{:S(2)}, u32[]{:S(2)}) async-start(bf16[8,32,1024]{2,1,0:T(8,128)(2,1)} %bitcast.15), calls=%async_computation.5 | async-start | bytes 1048576 | tf_op jit(solution)/shard_map/all_to_all | solution.py:35
  123.1 23.7 %collective-permute-start.6 = (bf16[256,512]{1,0:T(8,128)(2,1)S(1)}, bf16[256,512]{1,0:T(8,128)(2,1)S(1)}, u32[]{:S(2)}, u32[]{:S(2)}) collective-permute-start(bf16[256,512]{1,0:T(8,128)(2,1)S(1)} %bitcast.42), channel_id=1, source_target_pairs={{0,16},{16,0},{1,17},{17,1},{2,18},{18,2},{3,19},{19,3},{4,20},{20... | collective-permute-start | bytes 786440 | tf_op jit(solution)/shard_map/ppermute | solution.py:55
  133.1 18.3 %copy-start.1 = (bf16[512,512]{1,0:T(8,128)(2,1)S(1)}, bf16[512,512]{1,0:T(8,128)(2,1)}, u32[]{:S(2)}) copy-start(bf16[512,512]{1,0:T(8,128)(2,1)} %maximum_select_fusion.7) | copy-start | bytes 1572868
  133.1 30.3 %all-to-all-start.6 = ((bf16[32,32,512]{2,1,0:T(8,128)(2,1)}), bf16[32,32,512]{2,1,0:T(8,128)(2,1)}, u32[]{:S(2)}, u32[]{:S(2)}) async-start(bf16[32,32,512]{2,1,0:T(8,128)(2,1)} %bitcast.17), calls=%async_computation.6 | async-start | bytes 2097152 | tf_op jit(solution)/shard_map/all_to_all | solution.py:35
  147.1 7.7 %collective-permute-start.7 = (bf16[512,512]{1,0:T(8,128)(2,1)S(1)}, bf16[512,512]{1,0:T(8,128)(2,1)}, u32[]{:S(2)}, u32[]{:S(2)}) collective-permute-start(bf16[512,512]{1,0:T(8,128)(2,1)S(1)} %maximum_select_fusion.9), channel_id=1, source_target_pairs={{0,8},{8,0},{1,9},{9,1},{2,10},{10,2},{3,11},{11,3},{4,12},{12,4},... | collective-permute-start | bytes 1572872 | tf_op jit(solution)/shard_map/ppermute | solution.py:55
  149.3 4.4 %collective-permute-start.9 = (bf16[1,2,256,256]{2,3,1,0:T(8,128)(2,1)S(1)}, bf16[1,2,256,256]{2,3,1,0:T(8,128)(2,1)S(1)}, u32[]{:S(2)}, u32[]{:S(2)}) collective-permute-start(bf16[1,2,256,256]{2,3,1,0:T(8,128)(2,1)S(1)} %get-tuple-element.73), channel_id=1, source_target_pairs={{0,8},{8,0},{1,9},{9,1},{2,10},{10,2},{3,11},{11,3},{4,12},{12,4},... | collective-permute-start | bytes 786440 | tf_op jit(solution)/shard_map/ppermute | solution.py:68
  151.5 4.9 %collective-permute-start.8 = (bf16[512,512]{1,0:T(8,128)(2,1)S(1)}, bf16[512,512]{1,0:T(8,128)(2,1)}, u32[]{:S(2)}, u32[]{:S(2)}) collective-permute-start(bf16[512,512]{1,0:T(8,128)(2,1)S(1)} %copy-done.1), channel_id=1, source_target_pairs={{0,8},{8,0},{1,9},{9,1},{2,10},{10,2},{3,11},{11,3},{4,12},{12,4},... | collective-permute-start | bytes 1572872 | tf_op jit(solution)/shard_map/ppermute | solution.py:55
  163.4 1.0 copy-start

commit v9 on v8

--- a/solution.py
+++ b/solution.py
@@ -79,21 +79,28 @@
     return lax.optimization_barrier(arrays)
 
 
-def side_by_side(left, right, steps):
+def side_by_side(left, right, part):
     rows, cols = left.shape
-    part = rows // steps
-
-    def kernel(left, right, both):
-        both[:, :cols] = left[...]
-        both[:, cols:] = right[...]
-
-    half = pl.BlockSpec((part, cols), lambda i: (i, 0))
+
+    def kernel(left, right, both, made, sem):
+        for at in range(0, rows, part):
+            now = pl.ds(at, min(part, rows - at))
+            made[now, :cols] = left[now, :]
+            made[now, cols:] = right[now, :]
+            put = pltpu.make_async_copy(made.at[now], both.at[now], sem)
+            put.start()
+            put.wait()
+
+    whole = pl.BlockSpec(memory_space=pltpu.VMEM)
     return pl.pallas_call(
         kernel,
-        grid=(steps,),
         out_shape=jax.ShapeDtypeStruct((rows, 2 * cols), BF),
-        in_specs=[half, half],
-        out_specs=pl.BlockSpec((part, 2 * cols), lambda i: (i, 0)),
+        in_specs=[whole, whole],
+        out_specs=pl.BlockSpec(memory_space=pl.ANY),
+        scratch_shapes=[
+            pltpu.VMEM((rows, 2 * cols), BF),
+            pltpu.SemaphoreType.DMA,
+        ],
         compiler_params=pltpu.CompilerParams(vmem_limit_bytes=8 * 2**20),
         cost_estimate=pl.CostEstimate(
             flops=0, bytes_accessed=8 * rows * cols, transcendentals=0
@@ -153,6 +160,27 @@
     )(tokens, jac, terms, gated, signs)
 
 
+def copies(block, count, steps):
+    rows, cols = block.shape
+    per = count // steps
+
+    def kernel(block, out):
+        for k in range(per):
+            out[k] = block[...]
+
+    return pl.pallas_call(
+        kernel,
+        grid=(steps,),
+        out_shape=jax.ShapeDtypeStruct((count, rows, cols), BF),
+        in_specs=[pl.BlockSpec((rows, cols), lambda i: (0, 0))],
+        out_specs=pl.BlockSpec((per, rows, cols), lambda i: (i, 0, 0)),
+        compiler_params=pltpu.CompilerParams(vmem_limit_bytes=4 * 2**20),
+        cost_estimate=pl.CostEstimate(
+            flops=0, bytes_accessed=2 * (count + 1) * rows * cols, transcendentals=0
+        ),
+    )(block)
+
+
 def on_device(tokens, probe_draw, w_in, w_out):
     total_rows = probe_draw.shape[0]
     own_rows, feats = tokens.shape
@@ -166,12 +194,18 @@
     own_draw = lax.dynamic_index_in_dim(draw, mine, axis=1, keepdims=False)
     own_sign = (2 * own_draw - 1).astype(BF).reshape(nz * own_rows, feats)
     signal_part = contract_cols(own_sign, w_out_all)
-    own_tokens = gather(tokens, "z", nz)
+    spread = lax.cond(
+        lax.axis_index("core") == 0,
+        lambda block: copies(block, nz, 8),
+        lambda block: copies(block, nz, 1),
+        tokens,
+    )
+    own_tokens = exchange(spread, "z").reshape(nz * own_rows, feats)
     hidden_part = jnp.dot(own_tokens, w_in_all, preferred_element_type=F32)
     blocks = lax.cond(
         lax.axis_index("core") == 0,
-        lambda *parts: side_by_side(*parts, 16),
-        lambda *parts: side_by_side(*parts, 1),
+        lambda *parts: side_by_side(*parts, 48),
+        lambda *parts: side_by_side(*parts, 256),
         hidden_part.astype(BF),
         signal_part.astype(BF),
     )

time: 169 us -> 168 us (level)
  starting transfers between devices: 83.8 us -> 86.2 us
    ppermute x8, starting transfers between devices: 20.3 us -> 22.2 us  [pair_up(): far = lax.ppermute(array, name, [(0, 1), (1, 0)])]
  transfers between devices with their start and end apart: 16 -> 16, of which waited for: 9 -> 9; matrix products, arithmetic and copies ran while one was open for 11% -> 9% of each run, Pallas kernels for 0% -> 1%
where the time goes in v9:
time: 168 us; the launch traced here: 166 us
  starting transfers between devices  86.2 us (51%)
  waiting for transfers between devices  40.4 us (24%)
  blocking collectives  12.5 us (7%)
  other arithmetic  11.2 us (7%)
  local copies, waits for them, and re-layouts  6.15 us (4%)
  Pallas kernels  5.47 us (3%)
  matrix products  3.33 us (2%)
    all_to_all x6, starting transfers between devices, exchange(): return lax.all_to_all(blocks, axes, 0, 0, tiled=True)  59.6 us
    all_to_all x6, waiting for transfers between devices, exchange(): return lax.all_to_all(blocks, axes, 0, 0, tiled=True)  30.3 us
    ppermute x8, starting transfers between devices, pair_up(): far = lax.ppermute(array, name, [(0, 1), (1, 0)])  22.2 us
    all_to_all x1, blocking collectives, exchange(): return lax.all_to_all(blocks, axes, 0, 0, tiled=True)  12.5 us
    select_n x7, other arithmetic, pair_up(): jnp.where(lax.axis_index(name) == 0, jnp.concatenate([array, far], axis=a...  6.29 us
    ppermute x8, waiting for transfers between devices, pair_up(): far = lax.ppermute(array, name, [(0, 1), (1, 0)])  5.25 us
    ppermute x2, waiting for transfers between devices, hand_over(): far = lax.ppermute(jnp.where(first, right, left), name, [(0, 1), (1, 0)])  4.81 us
    ppermute x2, starting transfers between devices, hand_over(): far = lax.ppermute(jnp.where(first, right, left), name, [(0, 1), (1, 0)])  4.4 us
  transfers between devices with their start and end apart: 16, of which 9 were waited for; matrix products, arithmetic and copies ran while one was open for 9% of the time, Pallas kernels for 1%

profile of v9, /device:TPU:1, one launch (start us, length us, event | category | flops | bytes accessed | tf_op | source)
XLA Modules:
  0.0 166.2 jit_solution(11406160784270080291)
XLA Ops:
  0.6 4.1 %collective-permute-start = (bf16[512,256]{1,0:T(8,128)(2,1)}, bf16[512,256]{1,0:T(8,128)(2,1)S(1)}, u32[]{:S(2)}, u32[]{:S(2)}) collective-permute-start(bf16[512,256]{1,0:T(8,128)(2,1)} %param.10), channel_id=1, source_target_pairs={{0,16},{16,0},{1,17},{17,1},{2,18},{18,2},{3,19},{19,3},{4,20},{20... | collective-permute-start | bytes 786440 | tf_op jit(solution)/shard_map/ppermute | solution.py:55
  4.7 1.9 %collective-permute-start.2 = (bf16[256,512]{1,0:T(8,128)(2,1)}, bf16[256,512]{1,0:T(8,128)(2,1)S(1)}, u32[]{:S(2)}, u32[]{:S(2)}) collective-permute-start(bf16[256,512]{1,0:T(8,128)(2,1)} %param.11), channel_id=1, source_target_pairs={{0,16},{16,0},{1,17},{17,1},{2,18},{18,2},{3,19},{19,3},{4,20},{20... | collective-permute-start | bytes 786440 | tf_op jit(solution)/shard_map/ppermute | solution.py:55
  6.7 1.5 conditional.2
  6.7 1.4 branch_0_fun.2
  8.1 15.2 %all-to-all-start = ((bf16[16,16,512]{2,1,0:T(8,128)(2,1)}), bf16[16,16,512]{2,1,0:T(8,128)(2,1)S(1)}, u32[]{:S(2)}, u32[]{:S(2)}) async-start(bf16[16,16,512]{2,1,0:T(8,128)(2,1)} %get-tuple-element.73), calls=%async_computation | async-start | bytes 524288 | tf_op jit(solution)/shard_map/all_to_all | solution.py:35
  23.3 1.2 maximum_select_fusion.5
  24.5 5.2 %collective-permute-start.1 = (bf16[512,512]{1,0:T(8,128)(2,1)S(1)}, bf16[512,512]{1,0:T(8,128)(2,1)S(1)}, u32[]{:S(2)}, u32[]{:S(2)}) collective-permute-start(bf16[512,512]{1,0:T(8,128)(2,1)S(1)} %maximum_select_fusion.5), channel_id=1, source_target_pairs={{0,8},{8,0},{1,9},{9,1},{2,10},{10,2},{3,11},{11,3},{4,12},{12,4},... | collective-permute-start | bytes 1572872 | tf_op jit(solution)/shard_map/ppermute | solution.py:55
  29.9 1.9 %collective-permute-start.3 = (bf16[512,512]{1,0:T(8,128)(2,1)S(1)}, bf16[512,512]{1,0:T(8,128)(2,1)S(1)}, u32[]{:S(2)}, u32[]{:S(2)}) collective-permute-start(bf16[512,512]{1,0:T(8,128)(2,1)S(1)} %maximum_select_fusion.6), channel_id=1, source_target_pairs={{0,8},{8,0},{1,9},{9,1},{2,10},{10,2},{3,11},{11,3},{4,12},{12,4},... | collective-permute-start | bytes 1572872 | tf_op jit(solution)/shard_map/ppermute | solution.py:55
  31.8 1.1 add_convert_fusion.1
  33.3 0.4 collective-permute-done.3
  33.7 0.5 convolution_convert_fusion.1
  34.2 1.9 %all-to-all-done = bf16[16,16,512]{2,1,0:T(8,128)(2,1)S(1)} async-done(((bf16[16,16,512]{2,1,0:T(8,128)(2,1)}), bf16[16,16,512]{2,1,0:T(8,128)(2,1)S(1)}, u32[]{:S(2)}, u32[]{:S(2)}) %all-to-all-start) | async-done | bytes 262176 | tf_op jit(solution)/shard_map/all_to_all | solution.py:35
  36.1 0.4 convolution_convert_fusion.2
  36.5 1.1 conditional.3
  36.5 1.0 branch_0_fun.3
  37.6 6.7 %all-to-all-start.1 = ((bf16[8,32,2048]{2,1,0:T(8,128)(2,1)}), bf16[8,32,2048]{2,1,0:T(8,128)(2,1)}, u32[]{:S(2)}, u32[]{:S(2)}) async-start(bf16[8,32,2048]{2,1,0:T(8,128)(2,1)} %get-tuple-element.74), calls=%async_computation.1 | async-start | bytes 2097152 | tf_op jit(solution)/shard_map/all_to_all | solution.py:35
  44.2 1.9 %add_convert_fusion = bf16[1024,512]{1,0:T(8,128)(2,1)S(1)} fusion(s32[1024,512]{1,0:T(8,128)} %param.9), kind=kLoop, calls=%fused_computation.1 | loop fusion | flops 1572864 | bytes 3145728 | tf_op jit(solution)/shard_map/convert_element_type | solution.py:216
  46.2 8.9 %all-to-all-done.1 = bf16[8,32,2048]{2,1,0:T(8,128)(2,1)} async-done(((bf16[8,32,2048]{2,1,0:T(8,128)(2,1)}), bf16[8,32,2048]{2,1,0:T(8,128)(2,1)}, u32[]{:S(2)}, u32[]{:S(2)}) %all-to-all-start.1) | async-done | bytes 1048608 | tf_op jit(solution)/shard_map/all_to_all | solution.py:35
  55.1 1.4 convert_reduce_fusion
  56.6 12.5 %all_to_all.35 = bf16[8,32,1024]{2,1,0:T(8,128)(2,1)S(1)} all-to-all(bf16[8,32,1024]{2,1,0:T(8,128)(2,1)S(1)} %broadcast_in_dim.8), channel_id=1, replica_groups=mesh['z'=16,'xl'=2,'core'=2,'xh'=2,'y'=4] {'xh','y'}, dimensions={0} | all-to-all | bytes 1048576 | tf_op jit(solution)/shard_map/all_to_all | solution.py:35
  69.1 1.2 convolution_convert_fusion.3
  70.3 11.0 %all-to-all-start.3 = ((bf16[16,16,512]{2,1,0:T(8,128)(2,1)}), bf16[16,16,512]{2,1,0:T(8,128)(2,1)S(1)}, u32[]{:S(2)}, u32[]{:S(2)}) async-start(bf16[16,16,512]{2,1,0:T(8,128)(2,1)} %bitcast.9), calls=%async_computation.3 | async-start | bytes 524288 | tf_op jit(solution)/shard_map/all_to_all | solution.py:35
  81.3 2.3 %collective-permute-start.4 = (bf16[256,512]{1,0:T(8,128)(2,1)S(1)}, bf16[256,512]{1,0:T(8,128)(2,1)S(1)}, u32[]{:S(2)}, u32[]{:S(2)}) collective-permute-start(bf16[256,512]{1,0:T(8,128)(2,1)S(1)} %bitcast.37), channel_id=1, source_target_pairs={{0,16},{16,0},{1,17},{17,1},{2,18},{18,2},{3,19},{19,3},{4,20},{20... | collective-permute-start | bytes 786440 | tf_op jit(solution)/shard_map/ppermute | solution.py:55
  83.6 4.8 %collective-permute-done.4 = bf16[256,512]{1,0:T(8,128)(2,1)S(1)} collective-permute-done((bf16[256,512]{1,0:T(8,128)(2,1)S(1)}, bf16[256,512]{1,0:T(8,128)(2,1)S(1)}, u32[]{:S(2)}, u32[]{:S(2)}) %collective-permute-start.4) | collective-permute-done | bytes 262176 | tf_op jit(solution)/shard_map/ppermute | solution.py:55
  88.4 1.0 maximum_select_fusion.7
  89.4 4.6 %all-to-all-done.3 = bf16[16,16,512]{2,1,0:T(8,128)(2,1)S(1)} async-done(((bf16[16,16,512]{2,1,0:T(8,128)(2,1)}), bf16[16,16,512]{2,1,0:T(8,128)(2,1)S(1)}, u32[]{:S(2)}, u32[]{:S(2)}) %all-to-all-start.3) | async-done | bytes 262176 | tf_op jit(solution)/shard_map/all_to_all | solution.py:35
  94.1 0.7 broadcast_in_dim.9
  94.8 7.1 %all-to-all-start.4 = ((bf16[16,16,512]{2,1,0:T(8,128)(2,1)}), bf16[16,16,512]{2,1,0:T(8,128)(2,1)S(1)}, u32[]{:S(2)}, u32[]{:S(2)}) async-start(bf16[16,16,512]{2,1,0:T(8,128)(2,1)} %broadcast_in_dim.9), calls=%async_computation.4 | async-start | bytes 524288 | tf_op jit(solution)/shard_map/all_to_all | solution.py:35
  101.9 1.0 copy.11
  102.9 1.1 copy.12
  104.0 2.3 %collective-permute-start.5 = (bf16[1,256,512]{1,2,0:T(8,128)(2,1)S(1)}, bf16[1,256,512]{1,2,0:T(8,128)(2,1)S(1)}, u32[]{:S(2)}, u32[]{:S(2)}) collective-permute-start(bf16[1,256,512]{1,2,0:T(8,128)(2,1)S(1)} %get-tuple-element.68), channel_id=1, source_target_pairs={{0,16},{16,0},{1,17},{17,1},{2,18},{18,2},{3,19},{19,3},{4,20},{20... | collective-permute-start | bytes 786440 | tf_op jit(solution)/shard_map/ppermute | solution.py:68
  106.4 4.8 %collective-permute-done.5 = bf16[1,256,512]{1,2,0:T(8,128)(2,1)S(1)} collective-permute-done((bf16[1,256,512]{1,2,0:T(8,128)(2,1)S(1)}, bf16[1,256,512]{1,2,0:T(8,128)(2,1)S(1)}, u32[]{:S(2)}, u32[]{:S(2)}) %collective-permute-start.5) | collective-permute-done | bytes 262176 | tf_op jit(solution)/shard_map/ppermute | solution.py:68
  111.2 3.4 %all-to-all-done.4 = bf16[16,16,512]{2,1,0:T(8,128)(2,1)S(1)} async-done(((bf16[16,16,512]{2,1,0:T(8,128)(2,1)}), bf16[16,16,512]{2,1,0:T(8,128)(2,1)S(1)}, u32[]{:S(2)}, u32[]{:S(2)}) %all-to-all-start.4) | async-done | bytes 262176 | tf_op jit(solution)/shard_map/all_to_all | solution.py:35
  114.7 1.2 convolution_convert_fusion
  115.9 3.5 %all-to-all-start.5 = ((bf16[8,32,1024]{2,1,0:T(8,128)(2,1)}), bf16[8,32,1024]{2,1,0:T(8,128)(2,1)S(1)}, u32[]{:S(2)}, u32[]{:S(2)}) async-start(bf16[8,32,1024]{2,1,0:T(8,128)(2,1)} %bitcast.14), calls=%async_computation.5 | async-start | bytes 1048576 | tf_op jit(solution)/shard_map/all_to_all | solution.py:35
  119.4 2.3 %collective-permute-start.6 = (bf16[256,512]{1,0:T(8,128)(2,1)S(1)}, bf16[256,512]{1,0:T(8,128)(2,1)S(1)}, u32[]{:S(2)}, u32[]{:S(2)}) collective-permute-start(bf16[256,512]{1,0:T(8,128)(2,1)S(1)} %bitcast.40), channel_id=1, source_target_pairs={{0,16},{16,0},{1,17},{17,1},{2,18},{18,2},{3,19},{19,3},{4,20},{20... | collective-permute-start | bytes 786440 | tf_op jit(solution)/shard_map/ppermute | solution.py:55
  121.7 6.3 %all-to-all-done.5 = bf16[8,32,1024]{2,1,0:T(8,128)(2,1)S(1)} async-done(((bf16[8,32,1024]{2,1,0:T(8,128)(2,1)}), bf16[8,32,1024]{2,1,0:T(8,128)(2,1)S(1)}, u32[]{:S(2)}, u32[]{:S(2)}) %all-to-all-start.5) | async-done | bytes 524320 | tf_op jit(solution)/shard_map/all_to_all | solution.py:35
  128.3 1.1 broadcast_in_dim.10
  129.4 16.2 %all-to-all-start.6 = ((bf16[32,32,512]{2,1,0:T(8,128)(2,1)}), bf16[32,32,512]{2,1,0:T(8,128)(2,1)}, u32[]{:S(2)}, u32[]{:S(2)}) async-start(bf16[32,32,512]{2,1,0:T(8,128)(2,1)} %bitcast.16), calls=%async_computation.6 | async-start | bytes 2097152 | tf_op jit(solution)/shard_map/all_to_all | solution.py:35
  145.8 2.2 %collective-permute-start.7 = (bf16[512,512]{1,0:T(8,128)(2,1)S(1)}, bf16[512,512]{1,0:T(8,128)(2,1)}, u32[]{:S(2)}, u32[]{:S(2)}) collective-permute-start(bf16[512,512]{1,0:T(8,128)(2,1)S(1)} %maximum_select_fusion.9), channel_id=1, source_target_pairs={{0,8},{8,0},{1,9},{9,1},{2,10},{10,2},{3,11},{11,3},{4,12},{12,4},... | collective-permute-start | bytes 1572872 | tf_op jit(solution)/shard_map/ppermute | solution.py:55
  148.1 2.1 %collective-permute-start.9 = (bf16[1,2,256,256]{2,3,1,0:T(8,128)(2,1)S(1)}, bf16[1,2,256,256]{2,3,1,0:T(8,128)(2,1)S(1)}, u32[]{:S(2)}, u32[]{:S(2)}) collective-permute-start(bf16[1,2,256,256]{2,3,1,0:T(8,128)(2,1)S(1)} %get-tuple-element.66), channel_id=1, source_target_pairs={{0,8},{8,0},{1,9},{9,1},{2,10},{10,2},{3,11},{11,3},{4,12},{12,4},... | collective-permute-start | bytes 786440 | tf_op jit(solution)/shard_map/ppermute | solution.py:68
  150.2 2.2 %collective-permute-start.8 = (bf16[512,512]{1,0:T(8,128)(2,1)S(1)}, bf16[512,512]{1,0:T(8,128)(2,1)}, u32[]{:S(2)}, u32[]{:S(2)}) collective-permute-start(bf16[512,512]{1,0:T(8,128)(2,1)S(1)} %copy-done.1), channel_id=1, source_target_pairs={{0,8},{8,0},{1,9},{9,1},{2,10},{10,2},{3,11},{11,3},{4,12},{12,4},... | collective-permute-start | bytes 1572872 | tf_op jit(solution)/shard_map/ppermute | solution.py:55
  152.6 1.0 copy.14
  153.6 1.6 maximum_select_fusion.3.jac
  155.2 1.8 %maximum_select_fusion.4.tokens = bf16[1024,512]{1,0:T(8,128)(2,1)S(1)} fusion(bf16[512,512]{1,0:T(8,128)(2,1)} %collective-permute-done.8, bf16[512,512]{1,0:T(8,128)(2,1)} %maximum_select_fusion.7, pred[]{:T(512)S(6)} %eq.4), kind=kLoop, calls=%fused_computation.14 | loop fusion | flops 4718592 | bytes 2097153 | tf_op jit(solution)/shard_map/jit(_where)/select_n | solution.py:56
  157.0 5.2 %all-to-all-done.6 = bf16[32,32,512]{2,1,0:T(8,128)(2,1)} async-done(((bf16[32,32,512]{2,1,0:T(8,128)(2,1)}), bf16[32,32,512]{2,1,0:T(8,128)(2,1)}, u32[]{:S(2)}, u32[]{:S(2)}) %all-to-all-start.6) | async-done | bytes 1048608 | tf_op jit(solution)/shard_map/all_to_all | solution.py:35
  162.2 1.0 copy-done
  163.2 3.0 %shard_map.65 = (f32[512,256]{1,0:T(8,128)}, f32[256,512]{1,0:T(8,128)}) custom-call(bf16[1024,512]{1,0:T(8,128)(2,1)S(1)} %maximum_select_fusion.4.tokens, bf16[1024,512]{1,0:T(8,128)(2,1)S(1)} %maximum_select_fusion.3.jac, bf16[1024,512]{1,0:T(8,128)(2,1)} %bitcast.19.terms, bf16[1024,256]{1,0:T(8,128)(2,1)S(1)} %bitcast.31, bf16[1024,512]{1,0:T(8,128)(2,1)S(1)} %bitcast.30), custom_call_target="tpu_custom_call" | custom-call | flops 805306368 | bytes 6291456 | tf_op jit(solution)/shard_map/pallas_call | solution.py:139
  (29 shorter events, 1.5 us)
Async XLA Ops:
  0.6 29.1 %copy-start.2 = (bf16[256,512]{1,0:T(8,128)(2,1)S(1)}, bf16[256,512]{1,0:T(8,128)(2,1)}, u32[]{:S(2)}) copy-start(bf16[256,512]{1,0:T(8,128)(2,1)} %param.11) | copy-start | bytes 786436
  0.6 22.7 %collective-permute-start = (bf16[512,256]{1,0:T(8,128)(2,1)}, bf16[512,256]{1,0:T(8,128)(2,1)S(1)}, u32[]{:S(2)}, u32[]{:S(2)}) collective-permute-start(bf16[512,256]{1,0:T(8,128)(2,1)} %param.10), channel_id=1, source_target_pairs={{0,16},{16,0},{1,17},{17,1},{2,18},{18,2},{3,19},{19,3},{4,20},{20... | collective-permute-start | bytes 786440 | tf_op jit(solution)/shard_map/ppermute | solution.py:55
  4.7 25.0 %collective-permute-start.2 = (bf16[256,512]{1,0:T(8,128)(2,1)}, bf16[256,512]{1,0:T(8,128)(2,1)S(1)}, u32[]{:S(2)}, u32[]{:S(2)}) collective-permute-start(bf16[256,512]{1,0:T(8,128)(2,1)} %param.11), channel_id=1, source_target_pairs={{0,16},{16,0},{1,17},{17,1},{2,18},{18,2},{3,19},{19,3},{4,20},{20... | collective-permute-start | bytes 786440 | tf_op jit(solution)/shard_map/ppermute | solution.py:55
  8.1 27.9 %all-to-all-start = ((bf16[16,16,512]{2,1,0:T(8,128)(2,1)}), bf16[16,16,512]{2,1,0:T(8,128)(2,1)S(1)}, u32[]{:S(2)}, u32[]{:S(2)}) async-start(bf16[16,16,512]{2,1,0:T(8,128)(2,1)} %get-tuple-element.73), calls=%async_computation | async-start | bytes 524288 | tf_op jit(solution)/shard_map/all_to_all | solution.py:35
  24.5 8.5 %collective-permute-start.1 = (bf16[512,512]{1,0:T(8,128)(2,1)S(1)}, bf16[512,512]{1,0:T(8,128)(2,1)S(1)}, u32[]{:S(2)}, u32[]{:S(2)}) collective-permute-start(bf16[512,512]{1,0:T(8,128)(2,1)S(1)} %maximum_select_fusion.5), channel_id=1, source_target_pairs={{0,8},{8,0},{1,9},{9,1},{2,10},{10,2},{3,11},{11,3},{4,12},{12,4},... | collective-permute-start | bytes 1572872 | tf_op jit(solution)/shard_map/ppermute | solution.py:55
  29.9 3.8 %collective-permute-start.3 = (bf16[512,512]{1,0:T(8,128)(2,1)S(1)}, bf16[512,512]{1,0:T(8,128)(2,1)S(1)}, u32[]{:S(2)}, u32[]{:S(2)}) collective-permute-start(bf16[512,512]{1,0:T(8,128)(2,1)S(1)} %maximum_select_fusion.6), channel_id=1, source_target_pairs={{0,8},{8,0},{1,9},{9,1},{2,10},{10,2},{3,11},{11,3},{4,12},{12,4},... | collective-permute-start | bytes 1572872 | tf_op jit(solution)/shard_map/ppermute | solution.py:55
  37.6 17.5 %all-to-all-start.1 = ((bf16[8,32,2048]{2,1,0:T(8,128)(2,1)}), bf16[8,32,2048]{2,1,0:T(8,128)(2,1)}, u32[]{:S(2)}, u32[]{:S(2)}) async-start(bf16[8,32,2048]{2,1,0:T(8,128)(2,1)} %get-tuple-element.74), calls=%async_computation.1 | async-start | bytes 2097152 | tf_op jit(solution)/shard_map/all_to_all | solution.py:35
  70.3 23.8 %all-to-all-start.3 = ((bf16[16,16,512]{2,1,0:T(8,128)(2,1)}), bf16[16,16,512]{2,1,0:T(8,128)(2,1)S(1)}, u32[]{:S(2)}, u32[]{:S(2)}) async-start(bf16[16,16,512]{2,1,0:T(8,128)(2,1)} %bitcast.9), calls=%async_computation.3 | async-start | bytes 524288 | tf_op jit(solution)/shard_map/all_to_all | solution.py:35
  81.3 7.1 %collective-permute-start.4 = (bf16[256,512]{1,0:T(8,128)(2,1)S(1)}, bf16[256,512]{1,0:T(8,128)(2,1)S(1)}, u32[]{:S(2)}, u32[]{:S(2)}) collective-permute-start(bf16[256,512]{1,0:T(8,128)(2,1)S(1)} %bitcast.37), channel_id=1, source_target_pairs={{0,16},{16,0},{1,17},{17,1},{2,18},{18,2},{3,19},{19,3},{4,20},{20... | collective-permute-start | bytes 786440 | tf_op jit(solution)/shard_map/ppermute | solution.py:55
  94.8 19.9 %all-to-all-start.4 = ((bf16[16,16,512]{2,1,0:T(8,128)(2,1)}), bf16[16,16,512]{2,1,0:T(8,128)(2,1)S(1)}, u32[]{:S(2)}, u32[]{:S(2)}) async-start(bf16[16,16,512]{2,1,0:T(8,128)(2,1)} %broadcast_in_dim.9), calls=%async_computation.4 | async-start | bytes 524288 | tf_op jit(solution)/shard_map/all_to_all | solution.py:35
  104.0 7.1 %collective-permute-start.5 = (bf16[1,256,512]{1,2,0:T(8,128)(2,1)S(1)}, bf16[1,256,512]{1,2,0:T(8,128)(2,1)S(1)}, u32[]{:S(2)}, u32[]{:S(2)}) collective-permute-start(bf16[1,256,512]{1,2,0:T(8,128)(2,1)S(1)} %get-tuple-element.68), channel_id=1, source_target_pairs={{0,16},{16,0},{1,17},{17,1},{2,18},{18,2},{3,19},{19,3},{4,20},{20... | collective-permute-start | bytes 786440 | tf_op jit(solution)/shard_map/ppermute | solution.py:68
  115.9 12.1 %all-to-all-start.5 = ((bf16[8,32,1024]{2,1,0:T(8,128)(2,1)}), bf16[8,32,1024]{2,1,0:T(8,128)(2,1)S(1)}, u32[]{:S(2)}, u32[]{:S(2)}) async-start(bf16[8,32,1024]{2,1,0:T(8,128)(2,1)} %bitcast.14), calls=%async_computation.5 | async-start | bytes 1048576 | tf_op jit(solution)/shard_map/all_to_all | solution.py:35
  119.4 26.2 %collective-permute-start.6 = (bf16[256,512]{1,0:T(8,128)(2,1)S(1)}, bf16[256,512]{1,0:T(8,128)(2,1)S(1)}, u32[]{:S(2)}, u32[]{:S(2)}) collective-permute-start(bf16[256,512]{1,0:T(8,128)(2,1)S(1)} %bitcast.40), channel_id=1, source_target_pairs={{0,16},{16,0},{1,17},{17,1},{2,18},{18,2},{3,19},{19,3},{4,20},{20... | collective-permute-start | bytes 786440 | tf_op jit(solution)/shard_map/ppermute | solution.py:55
  129.4 20.8 %copy-start.1 = (bf16[512,512]{1,0:T(8,128)(2,1)S(1)}, bf16[512,512]{1,0:T(8,128)(2,1)}, u32[]{:S(2)}) copy-start(bf16[512,512]{1,0:T(8,128)(2,1)} %maximum_select_fusion.7) | copy-start | bytes 1572868
  129.4 32.8 %all-to-all-start.6 = ((bf16[32,32,512]{2,1,0:T(8,128)(2,1)}), bf16[32,32,512]{2,1,0:T(8,128)(2,1)}, u32[]{:S(2)}, u32[]{:S(2)}) async-start(bf16[32,32,512]{2,1,0:T(8,128)(2,1)} %bitcast.16), calls=%async_computation.6 | async-start | bytes 2097152 | tf_op jit(solution)/shard_map/all_to_all | solution.py:35
  145.8 7.7 %collective-permute-start.7 = (bf16[512,512]{1,0:T(8,128)(2,1)S(1)}, bf16[512,512]{1,0:T(8,128)(2,1)}, u32[]{:S(2)}, u32[]{:S(2)}) collective-permute-start(bf16[512,512]{1,0:T(8,128)(2,1)S(1)} %maximum_select_fusion.9), channel_id=1, source_target_pairs={{0,8},{8,0},{1,9},{9,1},{2,10},{10,2},{3,11},{11,3},{4,12},{12,4},... | collective-permute-start | bytes 1572872 | tf_op jit(solution)/shard_map/ppermute | solution.py:55
  148.1 4.4 %collective-permute-start.9 = (bf16[1,2,256,256]{2,3,1,0:T(8,128)(2,1)S(1)}, bf16[1,2,256,256]{2,3,1,0:T(8,128)(2,1)S(1)}, u32[]{:S(2)}, u32[]{:S(2)}) collective-permute-start(bf16[1,2,256,256]{2,3,1,0:T(8,128)(2,1)S(1)} %get-tuple-element.66), channel_id=1, source_target_pairs={{0,8},{8,0},{1,9},{9,1},{2,10},{10,2},{3,11},{11,3},{4,12},{12,4},... | collective-permute-start | bytes 786440 | tf_op jit(solution)/shard_map/ppermute | solution.py:68
  150.2 4.9 %collective-permute-start.8 = (bf16[512,512]{1,0:T(8,128)(2,1)S(1)}, bf16[512,512]{1,0:T(8,128)(2,1)}, u32[]{:S(2)}, u32[]{:S(2)}) collective-permute-start(bf16[512,512]{1,0:T(8,128)(2,1)S(1)} %copy-done.1), channel_id=1, source_target_pairs={{0,8},{8,0},{1,9},{9,1},{2,10},{10,2},{3,11},{11,3},{4,12},{12,4},... | collective-permute-start | bytes 1572872 | tf_op jit(solution)/shard_map/ppermute | solution.py:55
  162.2 1.0 copy-start

commit v10 on v9

--- a/solution.py
+++ b/solution.py
@@ -196,7 +196,7 @@
     signal_part = contract_cols(own_sign, w_out_all)
     spread = lax.cond(
         lax.axis_index("core") == 0,
-        lambda block: copies(block, nz, 8),
+        lambda block: copies(block, nz, 16),
         lambda block: copies(block, nz, 1),
         tokens,
     )
@@ -204,7 +204,7 @@
     hidden_part = jnp.dot(own_tokens, w_in_all, preferred_element_type=F32)
     blocks = lax.cond(
         lax.axis_index("core") == 0,
-        lambda *parts: side_by_side(*parts, 48),
+        lambda *parts: side_by_side(*parts, 64),
         lambda *parts: side_by_side(*parts, 256),
         hidden_part.astype(BF),
         signal_part.astype(BF),

time: 168 us -> 175 us (1.042)
  starting transfers between devices: 86.2 us -> 95 us
    all_to_all x6, starting transfers between devices: 59.6 us -> 66.2 us  [exchange(): return lax.all_to_all(blocks, axes, 0, 0, tiled=True)]
    ppermute x8, starting transfers between devices: 22.2 us -> 24.5 us  [pair_up(): far = lax.ppermute(array, name, [(0, 1), (1, 0)])]
    all_to_all x6, waiting for transfers between devices: 30.3 us -> 28.2 us  [exchange(): return lax.all_to_all(blocks, axes, 0, 0, tiled=True)]
  transfers between devices with their start and end apart: 16 -> 16, of which waited for: 9 -> 8; matrix products, arithmetic and copies ran while one was open for 9% -> 8% of each run, Pallas kernels for 1% -> 1%
where the time goes in v10:
time: 175 us; the launch traced here: 173 us
  starting transfers between devices  95 us (54%)
  waiting for transfers between devices  38.7 us (22%)
  blocking collectives  12.3 us (7%)
  other arithmetic  11.2 us (6%)
  local copies, waits for them, and re-layouts  6.15 us (4%)
  Pallas kernels  5.47 us (3%)
  matrix products  3.34 us (2%)
    all_to_all x6, starting transfers between devices, exchange(): return lax.all_to_all(blocks, axes, 0, 0, tiled=True)  66.2 us
    all_to_all x6, waiting for transfers between devices, exchange(): return lax.all_to_all(blocks, axes, 0, 0, tiled=True)  28.2 us
    ppermute x8, starting transfers between devices, pair_up(): far = lax.ppermute(array, name, [(0, 1), (1, 0)])  24.5 us
    all_to_all x1, blocking collectives, exchange(): return lax.all_to_all(blocks, axes, 0, 0, tiled=True)  12.3 us
    select_n x7, other arithmetic, pair_up(): jnp.where(lax.axis_index(name) == 0, jnp.concatenate([array, far], axis=a...  6.29 us
    ppermute x8, waiting for transfers between devices, pair_up(): far = lax.ppermute(array, name, [(0, 1), (1, 0)])  5.3 us
    ppermute x2, waiting for transfers between devices, hand_over(): far = lax.ppermute(jnp.where(first, right, left), name, [(0, 1), (1, 0)])  5.15 us
    ppermute x2, starting transfers between devices, hand_over(): far = lax.ppermute(jnp.where(first, right, left), name, [(0, 1), (1, 0)])  4.35 us
  transfers between devices with their start and end apart: 16, of which 8 were waited for; matrix products, arithmetic and copies ran while one was open for 8% of the time, Pallas kernels for 1%

profile of v10, /device:TPU:1, one launch (start us, length us, event | category | flops | bytes accessed | tf_op | source)
XLA Modules:
  0.0 173.3 jit_solution(10282596028144724954)
XLA Ops:
  0.6 4.1 %collective-permute-start = (bf16[512,256]{1,0:T(8,128)(2,1)}, bf16[512,256]{1,0:T(8,128)(2,1)S(1)}, u32[]{:S(2)}, u32[]{:S(2)}) collective-permute-start(bf16[512,256]{1,0:T(8,128)(2,1)} %param.10), channel_id=1, source_target_pairs={{0,16},{16,0},{1,17},{17,1},{2,18},{18,2},{3,19},{19,3},{4,20},{20... | collective-permute-start | bytes 786440 | tf_op jit(solution)/shard_map/ppermute | solution.py:55
  4.7 1.9 %collective-permute-start.2 = (bf16[256,512]{1,0:T(8,128)(2,1)}, bf16[256,512]{1,0:T(8,128)(2,1)S(1)}, u32[]{:S(2)}, u32[]{:S(2)}) collective-permute-start(bf16[256,512]{1,0:T(8,128)(2,1)} %param.11), channel_id=1, source_target_pairs={{0,16},{16,0},{1,17},{17,1},{2,18},{18,2},{3,19},{19,3},{4,20},{20... | collective-permute-start | bytes 786440 | tf_op jit(solution)/shard_map/ppermute | solution.py:55
  6.7 1.5 conditional.2
  6.7 1.4 branch_0_fun.2
  8.1 15.2 %all-to-all-start = ((bf16[16,16,512]{2,1,0:T(8,128)(2,1)}), bf16[16,16,512]{2,1,0:T(8,128)(2,1)S(1)}, u32[]{:S(2)}, u32[]{:S(2)}) async-start(bf16[16,16,512]{2,1,0:T(8,128)(2,1)} %get-tuple-element.73), calls=%async_computation | async-start | bytes 524288 | tf_op jit(solution)/shard_map/all_to_all | solution.py:35
  23.3 1.2 maximum_select_fusion.5
  24.5 7.6 %collective-permute-start.1 = (bf16[512,512]{1,0:T(8,128)(2,1)S(1)}, bf16[512,512]{1,0:T(8,128)(2,1)S(1)}, u32[]{:S(2)}, u32[]{:S(2)}) collective-permute-start(bf16[512,512]{1,0:T(8,128)(2,1)S(1)} %maximum_select_fusion.5), channel_id=1, source_target_pairs={{0,8},{8,0},{1,9},{9,1},{2,10},{10,2},{3,11},{11,3},{4,12},{12,4},... | collective-permute-start | bytes 1572872 | tf_op jit(solution)/shard_map/ppermute | solution.py:55
  32.3 1.9 %collective-permute-start.3 = (bf16[512,512]{1,0:T(8,128)(2,1)S(1)}, bf16[512,512]{1,0:T(8,128)(2,1)S(1)}, u32[]{:S(2)}, u32[]{:S(2)}) collective-permute-start(bf16[512,512]{1,0:T(8,128)(2,1)S(1)} %maximum_select_fusion.6), channel_id=1, source_target_pairs={{0,8},{8,0},{1,9},{9,1},{2,10},{10,2},{3,11},{11,3},{4,12},{12,4},... | collective-permute-start | bytes 1572872 | tf_op jit(solution)/shard_map/ppermute | solution.py:55
  34.2 1.1 add_convert_fusion.1
  35.4 0.3 maximum_select_fusion
  35.7 0.4 collective-permute-done.3
  36.1 0.5 convolution_convert_fusion.1
  36.6 0.4 convolution_convert_fusion.2
  37.0 1.1 conditional.3
  37.0 1.0 branch_0_fun.3
  38.1 6.7 %all-to-all-start.1 = ((bf16[8,32,2048]{2,1,0:T(8,128)(2,1)}), bf16[8,32,2048]{2,1,0:T(8,128)(2,1)}, u32[]{:S(2)}, u32[]{:S(2)}) async-start(bf16[8,32,2048]{2,1,0:T(8,128)(2,1)} %get-tuple-element.74), calls=%async_computation.1 | async-start | bytes 2097152 | tf_op jit(solution)/shard_map/all_to_all | solution.py:35
  44.8 1.9 %add_convert_fusion = bf16[1024,512]{1,0:T(8,128)(2,1)S(1)} fusion(s32[1024,512]{1,0:T(8,128)} %param.9), kind=kLoop, calls=%fused_computation.1 | loop fusion | flops 1572864 | bytes 3145728 | tf_op jit(solution)/shard_map/convert_element_type | solution.py:216
  46.7 8.9 %all-to-all-done.1 = bf16[8,32,2048]{2,1,0:T(8,128)(2,1)} async-done(((bf16[8,32,2048]{2,1,0:T(8,128)(2,1)}), bf16[8,32,2048]{2,1,0:T(8,128)(2,1)}, u32[]{:S(2)}, u32[]{:S(2)}) %all-to-all-start.1) | async-done | bytes 1048608 | tf_op jit(solution)/shard_map/all_to_all | solution.py:35
  55.6 1.4 convert_reduce_fusion
  57.1 12.3 %all_to_all.35 = bf16[8,32,1024]{2,1,0:T(8,128)(2,1)S(1)} all-to-all(bf16[8,32,1024]{2,1,0:T(8,128)(2,1)S(1)} %broadcast_in_dim.8), channel_id=1, replica_groups=mesh['z'=16,'xl'=2,'core'=2,'xh'=2,'y'=4] {'xh','y'}, dimensions={0} | all-to-all | bytes 1048576 | tf_op jit(solution)/shard_map/all_to_all | solution.py:35
  69.5 1.2 convolution_convert_fusion.3
  70.7 18.4 %all-to-all-start.3 = ((bf16[16,16,512]{2,1,0:T(8,128)(2,1)}), bf16[16,16,512]{2,1,0:T(8,128)(2,1)S(1)}, u32[]{:S(2)}, u32[]{:S(2)}) async-start(bf16[16,16,512]{2,1,0:T(8,128)(2,1)} %bitcast.9), calls=%async_computation.3 | async-start | bytes 524288 | tf_op jit(solution)/shard_map/all_to_all | solution.py:35
  89.1 2.3 %collective-permute-start.4 = (bf16[256,512]{1,0:T(8,128)(2,1)S(1)}, bf16[256,512]{1,0:T(8,128)(2,1)S(1)}, u32[]{:S(2)}, u32[]{:S(2)}) collective-permute-start(bf16[256,512]{1,0:T(8,128)(2,1)S(1)} %bitcast.37), channel_id=1, source_target_pairs={{0,16},{16,0},{1,17},{17,1},{2,18},{18,2},{3,19},{19,3},{4,20},{20... | collective-permute-start | bytes 786440 | tf_op jit(solution)/shard_map/ppermute | solution.py:55
  91.4 4.9 %collective-permute-done.4 = bf16[256,512]{1,0:T(8,128)(2,1)S(1)} collective-permute-done((bf16[256,512]{1,0:T(8,128)(2,1)S(1)}, bf16[256,512]{1,0:T(8,128)(2,1)S(1)}, u32[]{:S(2)}, u32[]{:S(2)}) %collective-permute-start.4) | collective-permute-done | bytes 262176 | tf_op jit(solution)/shard_map/ppermute | solution.py:55
  96.2 1.0 maximum_select_fusion.7
  97.2 4.7 %all-to-all-done.3 = bf16[16,16,512]{2,1,0:T(8,128)(2,1)S(1)} async-done(((bf16[16,16,512]{2,1,0:T(8,128)(2,1)}), bf16[16,16,512]{2,1,0:T(8,128)(2,1)S(1)}, u32[]{:S(2)}, u32[]{:S(2)}) %all-to-all-start.3) | async-done | bytes 262176 | tf_op jit(solution)/shard_map/all_to_all | solution.py:35
  101.9 0.7 broadcast_in_dim.9
  102.6 10.0 %all-to-all-start.4 = ((bf16[16,16,512]{2,1,0:T(8,128)(2,1)}), bf16[16,16,512]{2,1,0:T(8,128)(2,1)S(1)}, u32[]{:S(2)}, u32[]{:S(2)}) async-start(bf16[16,16,512]{2,1,0:T(8,128)(2,1)} %broadcast_in_dim.9), calls=%async_computation.4 | async-start | bytes 524288 | tf_op jit(solution)/shard_map/all_to_all | solution.py:35
  112.6 1.0 copy.11
  113.6 1.1 copy.12
  114.7 2.3 %collective-permute-start.5 = (bf16[1,256,512]{1,2,0:T(8,128)(2,1)S(1)}, bf16[1,256,512]{1,2,0:T(8,128)(2,1)S(1)}, u32[]{:S(2)}, u32[]{:S(2)}) collective-permute-start(bf16[1,256,512]{1,2,0:T(8,128)(2,1)S(1)} %get-tuple-element.68), channel_id=1, source_target_pairs={{0,16},{16,0},{1,17},{17,1},{2,18},{18,2},{3,19},{19,3},{4,20},{20... | collective-permute-start | bytes 786440 | tf_op jit(solution)/shard_map/ppermute | solution.py:68
  117.0 5.2 %collective-permute-done.5 = bf16[1,256,512]{1,2,0:T(8,128)(2,1)S(1)} collective-permute-done((bf16[1,256,512]{1,2,0:T(8,128)(2,1)S(1)}, bf16[1,256,512]{1,2,0:T(8,128)(2,1)S(1)}, u32[]{:S(2)}, u32[]{:S(2)}) %collective-permute-start.5) | collective-permute-done | bytes 262176 | tf_op jit(solution)/shard_map/ppermute | solution.py:68
  122.2 3.2 %all-to-all-done.4 = bf16[16,16,512]{2,1,0:T(8,128)(2,1)S(1)} async-done(((bf16[16,16,512]{2,1,0:T(8,128)(2,1)}), bf16[16,16,512]{2,1,0:T(8,128)(2,1)S(1)}, u32[]{:S(2)}, u32[]{:S(2)}) %all-to-all-start.4) | async-done | bytes 262176 | tf_op jit(solution)/shard_map/all_to_all | solution.py:35
  125.4 1.2 convolution_convert_fusion
  126.6 3.5 %all-to-all-start.5 = ((bf16[8,32,1024]{2,1,0:T(8,128)(2,1)}), bf16[8,32,1024]{2,1,0:T(8,128)(2,1)S(1)}, u32[]{:S(2)}, u32[]{:S(2)}) async-start(bf16[8,32,1024]{2,1,0:T(8,128)(2,1)} %bitcast.14), calls=%async_computation.5 | async-start | bytes 1048576 | tf_op jit(solution)/shard_map/all_to_all | solution.py:35
  130.1 2.3 %collective-permute-start.6 = (bf16[256,512]{1,0:T(8,128)(2,1)S(1)}, bf16[256,512]{1,0:T(8,128)(2,1)S(1)}, u32[]{:S(2)}, u32[]{:S(2)}) collective-permute-start(bf16[256,512]{1,0:T(8,128)(2,1)S(1)} %bitcast.40), channel_id=1, source_target_pairs={{0,16},{16,0},{1,17},{17,1},{2,18},{18,2},{3,19},{19,3},{4,20},{20... | collective-permute-start | bytes 786440 | tf_op jit(solution)/shard_map/ppermute | solution.py:55
  132.4 6.3 %all-to-all-done.5 = bf16[8,32,1024]{2,1,0:T(8,128)(2,1)S(1)} async-done(((bf16[8,32,1024]{2,1,0:T(8,128)(2,1)}), bf16[8,32,1024]{2,1,0:T(8,128)(2,1)S(1)}, u32[]{:S(2)}, u32[]{:S(2)}) %all-to-all-start.5) | async-done | bytes 524320 | tf_op jit(solution)/shard_map/all_to_all | solution.py:35
  139.0 1.1 broadcast_in_dim.10
  140.1 12.5 %all-to-all-start.6 = ((bf16[32,32,512]{2,1,0:T(8,128)(2,1)}), bf16[32,32,512]{2,1,0:T(8,128)(2,1)}, u32[]{:S(2)}, u32[]{:S(2)}) async-start(bf16[32,32,512]{2,1,0:T(8,128)(2,1)} %bitcast.16), calls=%async_computation.6 | async-start | bytes 2097152 | tf_op jit(solution)/shard_map/all_to_all | solution.py:35
  152.9 2.2 %collective-permute-start.7 = (bf16[512,512]{1,0:T(8,128)(2,1)S(1)}, bf16[512,512]{1,0:T(8,128)(2,1)}, u32[]{:S(2)}, u32[]{:S(2)}) collective-permute-start(bf16[512,512]{1,0:T(8,128)(2,1)S(1)} %maximum_select_fusion.9), channel_id=1, source_target_pairs={{0,8},{8,0},{1,9},{9,1},{2,10},{10,2},{3,11},{11,3},{4,12},{12,4},... | collective-permute-start | bytes 1572872 | tf_op jit(solution)/shard_map/ppermute | solution.py:55
  155.2 2.1 %collective-permute-start.9 = (bf16[1,2,256,256]{2,3,1,0:T(8,128)(2,1)S(1)}, bf16[1,2,256,256]{2,3,1,0:T(8,128)(2,1)S(1)}, u32[]{:S(2)}, u32[]{:S(2)}) collective-permute-start(bf16[1,2,256,256]{2,3,1,0:T(8,128)(2,1)S(1)} %get-tuple-element.66), channel_id=1, source_target_pairs={{0,8},{8,0},{1,9},{9,1},{2,10},{10,2},{3,11},{11,3},{4,12},{12,4},... | collective-permute-start | bytes 786440 | tf_op jit(solution)/shard_map/ppermute | solution.py:68
  157.3 2.2 %collective-permute-start.8 = (bf16[512,512]{1,0:T(8,128)(2,1)S(1)}, bf16[512,512]{1,0:T(8,128)(2,1)}, u32[]{:S(2)}, u32[]{:S(2)}) collective-permute-start(bf16[512,512]{1,0:T(8,128)(2,1)S(1)} %copy-done.1), channel_id=1, source_target_pairs={{0,8},{8,0},{1,9},{9,1},{2,10},{10,2},{3,11},{11,3},{4,12},{12,4},... | collective-permute-start | bytes 1572872 | tf_op jit(solution)/shard_map/ppermute | solution.py:55
  159.6 1.0 copy.14
  160.6 1.6 maximum_select_fusion.3.jac
  162.2 1.8 %maximum_select_fusion.4.tokens = bf16[1024,512]{1,0:T(8,128)(2,1)S(1)} fusion(bf16[512,512]{1,0:T(8,128)(2,1)} %collective-permute-done.8, bf16[512,512]{1,0:T(8,128)(2,1)} %maximum_select_fusion.7, pred[]{:T(512)S(6)} %eq.4), kind=kLoop, calls=%fused_computation.14 | loop fusion | flops 4718592 | bytes 2097153 | tf_op jit(solution)/shard_map/jit(_where)/select_n | solution.py:56
  164.0 5.2 %all-to-all-done.6 = bf16[32,32,512]{2,1,0:T(8,128)(2,1)} async-done(((bf16[32,32,512]{2,1,0:T(8,128)(2,1)}), bf16[32,32,512]{2,1,0:T(8,128)(2,1)}, u32[]{:S(2)}, u32[]{:S(2)}) %all-to-all-start.6) | async-done | bytes 1048608 | tf_op jit(solution)/shard_map/all_to_all | solution.py:35
  169.2 1.0 copy-done
  170.3 3.0 %shard_map.65 = (f32[512,256]{1,0:T(8,128)}, f32[256,512]{1,0:T(8,128)}) custom-call(bf16[1024,512]{1,0:T(8,128)(2,1)S(1)} %maximum_select_fusion.4.tokens, bf16[1024,512]{1,0:T(8,128)(2,1)S(1)} %maximum_select_fusion.3.jac, bf16[1024,512]{1,0:T(8,128)(2,1)} %bitcast.19.terms, bf16[1024,256]{1,0:T(8,128)(2,1)S(1)} %bitcast.31, bf16[1024,512]{1,0:T(8,128)(2,1)S(1)} %bitcast.30), custom_call_target="tpu_custom_call" | custom-call | flops 805306368 | bytes 6291456 | tf_op jit(solution)/shard_map/pallas_call | solution.py:139
  (29 shorter events, 1.2 us)
Async XLA Ops:
  0.6 31.4 %copy-start.2 = (bf16[256,512]{1,0:T(8,128)(2,1)S(1)}, bf16[256,512]{1,0:T(8,128)(2,1)}, u32[]{:S(2)}) copy-start(bf16[256,512]{1,0:T(8,128)(2,1)} %param.11) | copy-start | bytes 786436
  0.6 22.7 %collective-permute-start = (bf16[512,256]{1,0:T(8,128)(2,1)}, bf16[512,256]{1,0:T(8,128)(2,1)S(1)}, u32[]{:S(2)}, u32[]{:S(2)}) collective-permute-start(bf16[512,256]{1,0:T(8,128)(2,1)} %param.10), channel_id=1, source_target_pairs={{0,16},{16,0},{1,17},{17,1},{2,18},{18,2},{3,19},{19,3},{4,20},{20... | collective-permute-start | bytes 786440 | tf_op jit(solution)/shard_map/ppermute | solution.py:55
  4.7 27.3 %collective-permute-start.2 = (bf16[256,512]{1,0:T(8,128)(2,1)}, bf16[256,512]{1,0:T(8,128)(2,1)S(1)}, u32[]{:S(2)}, u32[]{:S(2)}) collective-permute-start(bf16[256,512]{1,0:T(8,128)(2,1)} %param.11), channel_id=1, source_target_pairs={{0,16},{16,0},{1,17},{17,1},{2,18},{18,2},{3,19},{19,3},{4,20},{20... | collective-permute-start | bytes 786440 | tf_op jit(solution)/shard_map/ppermute | solution.py:55
  8.1 28.5 %all-to-all-start = ((bf16[16,16,512]{2,1,0:T(8,128)(2,1)}), bf16[16,16,512]{2,1,0:T(8,128)(2,1)S(1)}, u32[]{:S(2)}, u32[]{:S(2)}) async-start(bf16[16,16,512]{2,1,0:T(8,128)(2,1)} %get-tuple-element.73), calls=%async_computation | async-start | bytes 524288 | tf_op jit(solution)/shard_map/all_to_all | solution.py:35
  24.5 10.9 %collective-permute-start.1 = (bf16[512,512]{1,0:T(8,128)(2,1)S(1)}, bf16[512,512]{1,0:T(8,128)(2,1)S(1)}, u32[]{:S(2)}, u32[]{:S(2)}) collective-permute-start(bf16[512,512]{1,0:T(8,128)(2,1)S(1)} %maximum_select_fusion.5), channel_id=1, source_target_pairs={{0,8},{8,0},{1,9},{9,1},{2,10},{10,2},{3,11},{11,3},{4,12},{12,4},... | collective-permute-start | bytes 1572872 | tf_op jit(solution)/shard_map/ppermute | solution.py:55
  32.3 3.8 %collective-permute-start.3 = (bf16[512,512]{1,0:T(8,128)(2,1)S(1)}, bf16[512,512]{1,0:T(8,128)(2,1)S(1)}, u32[]{:S(2)}, u32[]{:S(2)}) collective-permute-start(bf16[512,512]{1,0:T(8,128)(2,1)S(1)} %maximum_select_fusion.6), channel_id=1, source_target_pairs={{0,8},{8,0},{1,9},{9,1},{2,10},{10,2},{3,11},{11,3},{4,12},{12,4},... | collective-permute-start | bytes 1572872 | tf_op jit(solution)/shard_map/ppermute | solution.py:55
  38.1 17.5 %all-to-all-start.1 = ((bf16[8,32,2048]{2,1,0:T(8,128)(2,1)}), bf16[8,32,2048]{2,1,0:T(8,128)(2,1)}, u32[]{:S(2)}, u32[]{:S(2)}) async-start(bf16[8,32,2048]{2,1,0:T(8,128)(2,1)} %get-tuple-element.74), calls=%async_computation.1 | async-start | bytes 2097152 | tf_op jit(solution)/shard_map/all_to_all | solution.py:35
  70.7 31.2 %all-to-all-start.3 = ((bf16[16,16,512]{2,1,0:T(8,128)(2,1)}), bf16[16,16,512]{2,1,0:T(8,128)(2,1)S(1)}, u32[]{:S(2)}, u32[]{:S(2)}) async-start(bf16[16,16,512]{2,1,0:T(8,128)(2,1)} %bitcast.9), calls=%async_computation.3 | async-start | bytes 524288 | tf_op jit(solution)/shard_map/all_to_all | solution.py:35
  89.1 7.1 %collective-permute-start.4 = (bf16[256,512]{1,0:T(8,128)(2,1)S(1)}, bf16[256,512]{1,0:T(8,128)(2,1)S(1)}, u32[]{:S(2)}, u32[]{:S(2)}) collective-permute-start(bf16[256,512]{1,0:T(8,128)(2,1)S(1)} %bitcast.37), channel_id=1, source_target_pairs={{0,16},{16,0},{1,17},{17,1},{2,18},{18,2},{3,19},{19,3},{4,20},{20... | collective-permute-start | bytes 786440 | tf_op jit(solution)/shard_map/ppermute | solution.py:55
  102.6 22.8 %all-to-all-start.4 = ((bf16[16,16,512]{2,1,0:T(8,128)(2,1)}), bf16[16,16,512]{2,1,0:T(8,128)(2,1)S(1)}, u32[]{:S(2)}, u32[]{:S(2)}) async-start(bf16[16,16,512]{2,1,0:T(8,128)(2,1)} %broadcast_in_dim.9), calls=%async_computation.4 | async-start | bytes 524288 | tf_op jit(solution)/shard_map/all_to_all | solution.py:35
  114.7 7.4 %collective-permute-start.5 = (bf16[1,256,512]{1,2,0:T(8,128)(2,1)S(1)}, bf16[1,256,512]{1,2,0:T(8,128)(2,1)S(1)}, u32[]{:S(2)}, u32[]{:S(2)}) collective-permute-start(bf16[1,256,512]{1,2,0:T(8,128)(2,1)S(1)} %get-tuple-element.68), channel_id=1, source_target_pairs={{0,16},{16,0},{1,17},{17,1},{2,18},{18,2},{3,19},{19,3},{4,20},{20... | collective-permute-start | bytes 786440 | tf_op jit(solution)/shard_map/ppermute | solution.py:68
  126.6 12.1 %all-to-all-start.5 = ((bf16[8,32,1024]{2,1,0:T(8,128)(2,1)}), bf16[8,32,1024]{2,1,0:T(8,128)(2,1)S(1)}, u32[]{:S(2)}, u32[]{:S(2)}) async-start(bf16[8,32,1024]{2,1,0:T(8,128)(2,1)} %bitcast.14), calls=%async_computation.5 | async-start | bytes 1048576 | tf_op jit(solution)/shard_map/all_to_all | solution.py:35
  130.1 22.5 %collective-permute-start.6 = (bf16[256,512]{1,0:T(8,128)(2,1)S(1)}, bf16[256,512]{1,0:T(8,128)(2,1)S(1)}, u32[]{:S(2)}, u32[]{:S(2)}) collective-permute-start(bf16[256,512]{1,0:T(8,128)(2,1)S(1)} %bitcast.40), channel_id=1, source_target_pairs={{0,16},{16,0},{1,17},{17,1},{2,18},{18,2},{3,19},{19,3},{4,20},{20... | collective-permute-start | bytes 786440 | tf_op jit(solution)/shard_map/ppermute | solution.py:55
  140.1 17.2 %copy-start.1 = (bf16[512,512]{1,0:T(8,128)(2,1)S(1)}, bf16[512,512]{1,0:T(8,128)(2,1)}, u32[]{:S(2)}) copy-start(bf16[512,512]{1,0:T(8,128)(2,1)} %maximum_select_fusion.7) | copy-start | bytes 1572868
  140.1 29.1 %all-to-all-start.6 = ((bf16[32,32,512]{2,1,0:T(8,128)(2,1)}), bf16[32,32,512]{2,1,0:T(8,128)(2,1)}, u32[]{:S(2)}, u32[]{:S(2)}) async-start(bf16[32,32,512]{2,1,0:T(8,128)(2,1)} %bitcast.16), calls=%async_computation.6 | async-start | bytes 2097152 | tf_op jit(solution)/shard_map/all_to_all | solution.py:35
  152.9 7.7 %collective-permute-start.7 = (bf16[512,512]{1,0:T(8,128)(2,1)S(1)}, bf16[512,512]{1,0:T(8,128)(2,1)}, u32[]{:S(2)}, u32[]{:S(2)}) collective-permute-start(bf16[512,512]{1,0:T(8,128)(2,1)S(1)} %maximum_select_fusion.9), channel_id=1, source_target_pairs={{0,8},{8,0},{1,9},{9,1},{2,10},{10,2},{3,11},{11,3},{4,12},{12,4},... | collective-permute-start | bytes 1572872 | tf_op jit(solution)/shard_map/ppermute | solution.py:55
  155.2 4.4 %collective-permute-start.9 = (bf16[1,2,256,256]{2,3,1,0:T(8,128)(2,1)S(1)}, bf16[1,2,256,256]{2,3,1,0:T(8,128)(2,1)S(1)}, u32[]{:S(2)}, u32[]{:S(2)}) collective-permute-start(bf16[1,2,256,256]{2,3,1,0:T(8,128)(2,1)S(1)} %get-tuple-element.66), channel_id=1, source_target_pairs={{0,8},{8,0},{1,9},{9,1},{2,10},{10,2},{3,11},{11,3},{4,12},{12,4},... | collective-permute-start | bytes 786440 | tf_op jit(solution)/shard_map/ppermute | solution.py:68
  157.3 4.9 %collective-permute-start.8 = (bf16[512,512]{1,0:T(8,128)(2,1)S(1)}, bf16[512,512]{1,0:T(8,128)(2,1)}, u32[]{:S(2)}, u32[]{:S(2)}) collective-permute-start(bf16[512,512]{1,0:T(8,128)(2,1)S(1)} %copy-done.1), channel_id=1, source_target_pairs={{0,8},{8,0},{1,9},{9,1},{2,10},{10,2},{3,11},{11,3},{4,12},{12,4},... | collective-permute-start | bytes 1572872 | tf_op jit(solution)/shard_map/ppermute | solution.py:55
  169.2 1.0 copy-start
